TPU v7x, 32 devices: a whole 2x2x4 slice. The times are simulated.
32 devices in a mesh: wide: 8 (over z, x), narrow: 4 (over y, core).
Axes of the slice: x: 2, y: 2, z: 4, core: 2. Of those that a mesh axis runs over, the one named last changes fastest.
Arguments:
- embed_table: bfloat16 [131072, 640], P('wide', 'narrow'), may hold values from -6 to 6
- requests: int32 [8, 8, 768, 40], P('wide', None, None, 'narrow'), may hold values from -1 to 16383, as said below
- slot_index: int32 [49152, 40], P('wide', 'narrow'), may hold values from 0 to 6143, as said below
- event_mask: int32 [49152], P(('wide', 'narrow')), may hold values from 0 to 1, as said below
- labels: int32 [49152], P(('wide', 'narrow')), may hold values from 0 to 1
- dense_feats: float32 [49152, 128], P(('wide', 'narrow')), may hold values from -40 to 40
- proj_weight: bfloat16 [640, 512], P('narrow'), may hold values from -0.25 to 0.25
- dense_weight: bfloat16 [128, 512], replicated, may hold values from -0.5 to 0.5
- proj_bias: bfloat16 [512], replicated, may hold values from -4 to 4
- up_weight: bfloat16 [14, 512, 1024], P(None, None, 'narrow'), may hold values from -0.25 to 0.25
- down_weight: bfloat16 [14, 1024, 512], P(None, 'narrow'), may hold values from -0.1875 to 0.1875
- norm_gain: bfloat16 [14, 512], replicated, may hold values from 0.5 to 1.5
- norm_shift: bfloat16 [14, 512], replicated, may hold values from -4 to 4
- gate_weight: bfloat16 [6, 512, 6], replicated, may hold values from -0.125 to 0.125
- tower_in: bfloat16 [6, 512, 128], replicated, may hold values from -0.25 to 0.25
- tower_bias: bfloat16 [6, 128], replicated, may hold values from -4 to 4
- tower_out: bfloat16 [6, 128], replicated, may hold values from -0.5 to 0.5
- tower_out_bias: bfloat16 [6], replicated, may hold values from -6 to 6
Outputs:
- logits: float32 [49152], P(('wide', 'narrow'))
- row_grads: float32 [8, 8, 768, 640], P('wide', None, None, 'narrow')
- proj_weight_grad: float32 [640, 512], P('narrow')
- dense_weight_grad: float32 [128, 512], replicated
- proj_bias_grad: float32 [512], replicated
- up_weight_grad: float32 [14, 512, 1024], P(None, None, 'narrow')
- down_weight_grad: float32 [14, 1024, 512], P(None, 'narrow')
- norm_gain_grad: float32 [14, 512], replicated
- norm_shift_grad: float32 [14, 512], replicated
- gate_weight_grad: float32 [6, 512, 6], replicated
- tower_in_grad: float32 [6, 512, 128], replicated
- tower_bias_grad: float32 [6, 128], replicated
- tower_out_grad: float32 [6, 128], replicated
- tower_out_bias_grad: float32 [6], replicated
Inputs may be any that keep to these rules, and one draw needn't show every extreme that they name: requests[w, o, s, f] is the row, counted within owner o's 16384 rows, looked up by field f of the event of device w whose slot in field f is o * 768 + s; -1 where that event is padding. `slot_index`: for each device of wide and each field, the 6144 events of that device hold distinct slots. `event_mask`: A device's events form 6 blocks of 1024, block d holding domain d; live events come first in a block, a quarter or more of each block is live, and every device has a full block.
All inputs are finite; a program needn't handle non-finite values.
Results may differ from a plain program's by a relative error of at most 0.01.
Values may be sent and summed in bfloat16 or wider, within the bound.
A program may use at most 320 MiB of HBM per device.

v0:
```python
import jax
import jax.numpy as jnp
from jax import lax
from jax.sharding import PartitionSpec as P

D = 512
EMB = 16
DOMAINS = 6
SHARED = 2
DOM_EXP = 2
DSLOT = 1024


highest = lax.Precision.HIGHEST


def layer_norm(values, gains, shifts):
    center = jnp.mean(values, axis=-1, keepdims=True)
    centered = values - center
    variance = jnp.mean(centered * centered, axis=-1, keepdims=True)
    return centered * lax.rsqrt(variance + 1e-05) * gains + shifts


def combine(outputs, logits_gate, gains, shifts):
    normed = layer_norm(outputs, gains, shifts)
    shared_gates = jax.nn.softmax(logits_gate[:, :SHARED], axis=-1)
    domain_gates = jax.nn.softmax(logits_gate[:, SHARED : SHARED + DOM_EXP], axis=-1)
    top_gates = jax.nn.softmax(logits_gate[:, SHARED + DOM_EXP :], axis=-1)
    mixture = top_gates[:, 0:1] * jnp.einsum(
        "rk,krm->rm", shared_gates, normed[:SHARED], precision=highest
    )
    return mixture + top_gates[:, 1:2] * jnp.einsum(
        "rj,jrm->rm", domain_gates, normed[SHARED:], precision=highest
    )


def shards(
    embed_table,
    requests,
    slot_index,
    event_mask,
    labels,
    dense_feats,
    proj_weight,
    dense_weight,
    proj_bias,
    up_weight,
    down_weight,
    norm_gain,
    norm_shift,
    gate_weight,
    tower_in,
    tower_bias,
    tower_out,
    tower_out_bias,
):
    narrow_count = lax.axis_size("narrow")
    ev_rows = slot_index.shape[0]
    quarter = ev_rows // narrow_count
    fields_here = slot_index.shape[1]
    hid_here = up_weight.shape[2]
    table_rows = embed_table.reshape(embed_table.shape[0] * fields_here, EMB)
    asked = lax.all_to_all(requests[0], "wide", split_axis=0, concat_axis=0, tiled=True)
    field_ids = jnp.arange(fields_here, dtype=jnp.int32)
    flat_index = jnp.maximum(asked, 0) * fields_here + field_ids
    found = jnp.take(table_rows, flat_index, axis=0)
    found = jnp.where((asked >= 0)[..., None], found, jnp.zeros_like(found))
    found = found.reshape(asked.shape[0], asked.shape[1], fields_here * EMB)
    received = lax.all_to_all(found, "wide", split_axis=0, concat_axis=0, tiled=True)
    rows_three = received.reshape(ev_rows, fields_here, EMB)
    embedded = jnp.take_along_axis(rows_three, slot_index[:, :, None], axis=0).reshape(
        ev_rows, fields_here * EMB
    )
    local_rows = lax.axis_index("narrow") * quarter + jnp.arange(quarter, dtype=jnp.int32)
    domain_of = local_rows // DSLOT
    onehot = (domain_of[:, None] == jnp.arange(DOMAINS, dtype=jnp.int32)[None, :]).astype(
        jnp.float32
    )
    live_rows = event_mask.astype(jnp.float32)
    weighted = onehot * live_rows[:, None]
    part_counts = jnp.sum(weighted, axis=0)
    part_sums = jnp.dot(weighted.T, dense_feats, precision=highest)
    totals, counts = lax.psum((part_sums, part_counts), ("wide", "narrow"))
    domain_means = totals / counts[:, None]
    deviation = dense_feats - jnp.dot(onehot, domain_means, precision=highest)
    part_spread = jnp.dot(weighted.T, deviation * deviation, precision=highest)
    spread = lax.psum(part_spread, ("wide", "narrow")) / counts[:, None]
    centered = dense_feats - jnp.dot(onehot, domain_means, precision=highest)
    dense_low = (centered * jnp.dot(onehot, lax.rsqrt(spread + 1e-05), precision=highest)).astype(
        jnp.bfloat16
    )
    projected = lax.psum_scatter(
        jnp.dot(embedded, proj_weight, preferred_element_type=jnp.float32),
        "narrow",
        scatter_dimension=0,
        tiled=True,
    )
    projected = projected + jnp.dot(dense_low, dense_weight, preferred_element_type=jnp.float32)
    projected = projected + proj_bias.astype(jnp.float32)
    inputs_low = projected.astype(jnp.bfloat16)
    inputs_full = lax.all_gather(inputs_low, "narrow", axis=0, tiled=True)
    up_shared = up_weight[:SHARED]
    down_shared = down_weight[:SHARED]
    up_domain = up_weight[SHARED:].reshape(DOMAINS, DOM_EXP, D, hid_here)
    down_domain = down_weight[SHARED:].reshape(DOMAINS, DOM_EXP, hid_here, D)
    blocks = inputs_full.reshape(DOMAINS, DSLOT, D)
    pre_shared = jnp.einsum(
        "rm,kmh->krh", inputs_full, up_shared, preferred_element_type=jnp.float32
    )
    pre_domain = jnp.einsum("dsm,djmh->djsh", blocks, up_domain, preferred_element_type=jnp.float32)
    gelu_shared, shared_back = jax.vjp(jax.nn.gelu, pre_shared)
    gelu_domain, domain_back = jax.vjp(jax.nn.gelu, pre_domain)
    act_shared = gelu_shared.astype(jnp.bfloat16)
    act_domain = gelu_domain.astype(jnp.bfloat16)
    out_shared = jnp.einsum(
        "krh,khm->krm", act_shared, down_shared, preferred_element_type=jnp.float32
    )
    out_domain = jnp.einsum(
        "djsh,djhm->jdsm", act_domain, down_domain, preferred_element_type=jnp.float32
    )
    partial_out = jnp.concatenate([out_shared, out_domain.reshape(DOM_EXP, ev_rows, D)], axis=0)
    expert_out = lax.psum_scatter(partial_out, "narrow", scatter_dimension=1, tiled=True)
    gain_float = norm_gain.astype(jnp.float32)
    shift_float = norm_shift.astype(jnp.float32)
    gain_rows = jnp.concatenate(
        [
            jnp.broadcast_to(gain_float[:SHARED, None, :], (SHARED, quarter, D)),
            jnp.einsum(
                "re,ejm->jrm",
                onehot,
                gain_float[SHARED:].reshape(DOMAINS, DOM_EXP, D),
                precision=highest,
            ),
        ],
        axis=0,
    )
    shift_rows = jnp.concatenate(
        [
            jnp.broadcast_to(shift_float[:SHARED, None, :], (SHARED, quarter, D)),
            jnp.einsum(
                "re,ejm->jrm",
                onehot,
                shift_float[SHARED:].reshape(DOMAINS, DOM_EXP, D),
                precision=highest,
            ),
        ],
        axis=0,
    )
    gate_all = jnp.einsum(
        "rm,emg->reg", inputs_low, gate_weight, preferred_element_type=jnp.float32
    )
    gate_logits = jnp.einsum("reg,re->rg", gate_all, onehot, precision=highest)
    mixture, combine_back = jax.vjp(combine, expert_out, gate_logits, gain_rows, shift_rows)
    hidden_low = mixture.astype(jnp.bfloat16)
    tower_all = jnp.einsum("rm,emk->rek", hidden_low, tower_in, preferred_element_type=jnp.float32)
    tower_pre = jnp.einsum("rek,re->rk", tower_all, onehot, precision=highest)
    tower_pre = tower_pre + jnp.dot(onehot, tower_bias.astype(jnp.float32), precision=highest)
    tower_act, tower_back = jax.vjp(jax.nn.gelu, tower_pre)
    out_rows = jnp.dot(onehot, tower_out.astype(jnp.float32), precision=highest)
    logits = jnp.sum(tower_act * out_rows, axis=1)
    logits = logits + jnp.dot(onehot, tower_out_bias.astype(jnp.float32), precision=highest)
    logit_grad = (jax.nn.sigmoid(logits) - labels.astype(jnp.float32)) * live_rows
    out_bias_grad = jnp.dot(onehot.T, logit_grad, precision=highest)
    out_vector_grad = jnp.dot(onehot.T, logit_grad[:, None] * tower_act, precision=highest)
    pre_low = tower_back(logit_grad[:, None] * out_rows)[0].astype(jnp.bfloat16)
    bias_tower_grad = jnp.dot(onehot.T, pre_low.astype(jnp.float32), precision=highest)
    pre_domains = pre_low[:, None, :] * onehot.astype(jnp.bfloat16)[:, :, None]
    tower_weight_grad = jnp.einsum(
        "rm,rek->emk", hidden_low, pre_domains, preferred_element_type=jnp.float32
    )
    hidden_grad = jnp.einsum(
        "rek,emk->rm", pre_domains, tower_in, preferred_element_type=jnp.float32
    )
    out_grad, gate_logit_grad, gain_rows_grad, shift_rows_grad = combine_back(hidden_grad)
    gain_grad = jnp.concatenate(
        [
            jnp.sum(gain_rows_grad[:SHARED], axis=1),
            jnp.einsum("re,jrm->ejm", onehot, gain_rows_grad[SHARED:], precision=highest).reshape(
                DOMAINS * DOM_EXP, D
            ),
        ],
        axis=0,
    )
    shift_grad = jnp.concatenate(
        [
            jnp.sum(shift_rows_grad[:SHARED], axis=1),
            jnp.einsum("re,jrm->ejm", onehot, shift_rows_grad[SHARED:], precision=highest).reshape(
                DOMAINS * DOM_EXP, D
            ),
        ],
        axis=0,
    )
    gate_domains = gate_logit_grad[:, None, :] * onehot[:, :, None]
    gate_grad = jnp.einsum(
        "rm,reg->emg", inputs_low.astype(jnp.float32), gate_domains, precision=highest
    )
    inputs_gate_grad = jnp.einsum(
        "reg,emg->rm", gate_domains, gate_weight.astype(jnp.float32), precision=highest
    )
    out_full = lax.all_gather(out_grad.astype(jnp.bfloat16), "narrow", axis=1, tiled=True)
    grad_shared = out_full[:SHARED]
    grad_domain = out_full[SHARED:].reshape(DOM_EXP, DOMAINS, DSLOT, D)
    act_shared_grad = jnp.einsum(
        "krm,khm->krh", grad_shared, down_shared, preferred_element_type=jnp.float32
    )
    act_domain_grad = jnp.einsum(
        "jdsm,djhm->djsh", grad_domain, down_domain, preferred_element_type=jnp.float32
    )
    down_shared_grad = jnp.einsum(
        "krh,krm->khm", act_shared, grad_shared, preferred_element_type=jnp.float32
    )
    down_domain_grad = jnp.einsum(
        "djsh,jdsm->djhm", act_domain, grad_domain, preferred_element_type=jnp.float32
    )
    shared_low = shared_back(act_shared_grad)[0].astype(jnp.bfloat16)
    domain_low = domain_back(act_domain_grad)[0].astype(jnp.bfloat16)
    up_shared_grad = jnp.einsum(
        "rm,krh->kmh", inputs_full, shared_low, preferred_element_type=jnp.float32
    )
    up_domain_grad = jnp.einsum(
        "dsm,djsh->djmh", blocks, domain_low, preferred_element_type=jnp.float32
    )
    input_partial = jnp.einsum(
        "krh,kmh->rm", shared_low, up_shared, preferred_element_type=jnp.float32
    )
    input_partial = input_partial + jnp.einsum(
        "djsh,djmh->dsm", domain_low, up_domain, preferred_element_type=jnp.float32
    ).reshape(ev_rows, D)
    up_grad = jnp.concatenate(
        [up_shared_grad, up_domain_grad.reshape(DOMAINS * DOM_EXP, D, hid_here)], axis=0
    )
    down_grad = jnp.concatenate(
        [down_shared_grad, down_domain_grad.reshape(DOMAINS * DOM_EXP, hid_here, D)], axis=0
    )
    input_sum = (
        lax.psum_scatter(input_partial, "narrow", scatter_dimension=0, tiled=True)
        + inputs_gate_grad
    )
    input_low = input_sum.astype(jnp.bfloat16)
    input_full_grad = lax.all_gather(input_low, "narrow", axis=0, tiled=True)
    proj_grad = jnp.einsum(
        "rc,rm->cm", embedded, input_full_grad, preferred_element_type=jnp.float32
    )
    dense_grad = jnp.einsum("rc,rm->cm", dense_low, input_low, preferred_element_type=jnp.float32)
    bias_grad = jnp.sum(input_low.astype(jnp.float32), axis=0)
    embed_grad = jnp.einsum(
        "rm,cm->rc", input_full_grad, proj_weight, preferred_element_type=jnp.float32
    )
    embed_grad = embed_grad.reshape(ev_rows, fields_here, EMB)
    field_cols = jnp.arange(fields_here, dtype=jnp.int32)[None, :]
    returned = jnp.zeros_like(embed_grad).at[slot_index, field_cols].set(embed_grad)
    returned = returned.reshape(requests.shape[1], requests.shape[2], fields_here * EMB)
    row_grads = lax.all_to_all(
        returned.astype(jnp.bfloat16), "wide", split_axis=0, concat_axis=0, tiled=True
    ).astype(returned.dtype)[None]
    up_grad, down_grad, proj_grad = lax.psum((up_grad, down_grad, proj_grad), "wide")
    common = lax.psum(
        (
            dense_grad,
            bias_grad,
            gain_grad,
            shift_grad,
            gate_grad,
            tower_weight_grad,
            bias_tower_grad,
            out_vector_grad,
            out_bias_grad,
        ),
        ("wide", "narrow"),
    )
    return (
        logits,
        row_grads,
        proj_grad,
        common[0],
        common[1],
        up_grad,
        down_grad,
        common[2],
        common[3],
        common[4],
        common[5],
        common[6],
        common[7],
        common[8],
    )


def solution(mesh):
    placed = (
        P("wide", "narrow"),
        P("wide", None, None, "narrow"),
        P("wide", "narrow"),
        P(("wide", "narrow")),
        P(("wide", "narrow")),
        P(("wide", "narrow"), None),
        P("narrow", None),
        P(),
        P(),
        P(None, None, "narrow"),
        P(None, "narrow", None),
        P(),
        P(),
        P(),
        P(),
        P(),
        P(),
        P(),
    )
    return jax.shard_map(
        shards,
        mesh=mesh,
        in_specs=placed,
        out_specs=(
            P(("wide", "narrow")),
            P("wide", None, None, "narrow"),
            P("narrow", None),
            P(),
            P(),
            P(None, None, "narrow"),
            P(None, "narrow", None),
            P(),
            P(),
            P(),
            P(),
            P(),
            P(),
            P(),
        ),
        check_vma=False,
    )
```

profile of v0, /device:TPU:0, one launch (start us, length us, event | category | flops | bytes accessed | tf_op | source)
XLA Modules:
  0.0 4210.6 jit_solution(12185265747700113801)
XLA Ops:
  26.0 46.2 %reshape.238 = bf16[163840,16]{1,0:T(8,128)(2,1)} reshape(bf16[16384,160]{1,0:T(8,128)(2,1)} %copy.90) | data formatting | bytes 10485760 | tf_op jit(solution)/shard_map/reshape | solution.py:62
  82.1 938.9 %gather_fusion = bf16[61440,16]{1,0:T(8,128)(2,1)} fusion(bf16[163840,16]{1,0:T(8,128)(2,1)} %reshape.238, s32[61440]{0:T(1024)S(1)} %broadcast_clamp_fusion), kind=kCustom, calls=%fused_computation | custom fusion | bytes 4177920 | tf_op jit(solution)/shard_map/jit(_take)/gather | solution.py:66
  1032.1 67.6 %reshape.263 = bf16[8,768,10,16]{2,1,0,3:T(8,128)(2,1)} reshape(bf16[61440,16]{0,1:T(8,128)(2,1)S(1)} %copy.92) | data formatting | bytes 3932160 | tf_op jit(solution)/shard_map/jit(_take)/gather | solution.py:66
  1099.7 22.5 select_select_fusion
  1122.2 22.0 copy.93
  1159.3 36.0 all-to-all-done.1
  1210.1 1000.0 %gather_fusion.1 = bf16[61440,16]{1,0:T(8,128)(2,1)} fusion(bf16[6144,10,16]{2,0,1:T(8,128)(2,1)} %copy.96, s32[61440]{0:T(1024)S(1)} %reshape.270), kind=kCustom, calls=%fused_computation.1 | custom fusion | bytes 4423680 | tf_op jit(solution)/shard_map/jit(take_along_axis)/gather | solution.py:71
  2221.2 67.6 %reshape.273 = bf16[6144,10,16]{1,0,2:T(8,128)(2,1)} reshape(bf16[61440,16]{0,1:T(8,128)(2,1)S(1)} %copy.97) | data formatting | bytes 3932160 | tf_op jit(solution)/shard_map/jit(take_along_axis)/gather | solution.py:71
  2288.8 20.9 broadcast_select_fusion
  2309.7 19.2 copy.98
  2337.3 38.0 all-reduce.8
  2376.6 42.2 %psum.107 = f32[6,128]{1,0:T(8,128)S(1)} all-reduce(f32[6,128]{1,0:T(8,128)S(1)} %fusion.84), channel_id=1, replica_groups=mesh['wide'=8,'narrow'=4] {'wide','narrow'}, use_global_device_ids=true, to_apply=%region_4.5 | all-reduce | flops 768 | bytes 6144 | tf_op jit(solution)/shard_map/psum | solution.py:87
  2419.7 16.4 reduce-scatter.4.cloned.1.call-done
  2447.3 38.9 all-gather.4.cloned.1.call-done
  2516.1 13.0 fusion.42
  2529.1 33.3 pad_maximum_fusion
  2571.8 333.9 %reduce-scatter.6.cloned.1.call-done = f32[4,1536,512]{2,1,0:T(8,128)} async-done(((f32[4,6144,512]{2,1,0:T(8,128)}), f32[4,1536,512]{2,1,0:T(8,128)}) %reduce-scatter.6.cloned.1.call-update) | async-done | bytes 12582928 | tf_op jit(solution)/shard_map/reduce_scatter | solution.py:122
  2924.6 16.0 fusion.20
  2979.5 13.2 multiply_reduce_fusion.3
  2992.7 13.3 multiply_reduce_fusion
  3016.0 16.7 multiply_multiply_fusion.4
  3032.8 153.9 %all-gather.6.cloned.1.call-done = bf16[4,6144,512]{2,1,0:T(8,128)(2,1)} async-done(((bf16[4,1536,512]{2,1,0:T(8,128)(2,1)}), bf16[4,6144,512]{2,1,0:T(8,128)(2,1)}) %all-gather.6.cloned.1.call-update) | async-done | bytes 25165840 | tf_op jit(solution)/shard_map/all_gather | solution.py:200
  3197.2 16.7 fusion.15
  3225.6 17.7 fusion.8
  3243.3 14.5 bitcast_add_fusion
  3274.2 82.8 %reduce-scatter.8.cloned.1.call-done = f32[1536,512]{1,0:T(8,128)} async-done(((f32[6144,512]{1,0:T(8,128)}), f32[1536,512]{1,0:T(8,128)}) %reduce-scatter.8.cloned.1.call-update) | async-done | bytes 3145744 | tf_op jit(solution)/shard_map/reduce_scatter | solution.py:236
  3459.0 19.8 reshape.278
  3478.8 162.5 %scatter_custom_fusion = f32[61440,16]{1,0:T(8,128)} fusion(s32[61440]{0:T(1024)S(1)} %reshape.276, f32[61440,16]{1,0:T(8,128)} %reshape.278, f32[]{:T(128)} %constant.48.clone.1), kind=kCustom, calls=%fused_computation.16 | custom fusion | bytes 3932672
  3641.3 16.3 convert_element_type.92
  3657.7 18.8 convert_element_type.90
  3689.4 85.8 %all-to-all-done.2 = bf16[8,768,160]{1,2,0:T(8,128)(2,1)S(1)} async-done(((bf16[8,768,160]{1,2,0:T(8,128)(2,1)}), bf16[8,768,160]{1,2,0:T(8,128)(2,1)S(1)}, u32[]{:S(2)}, u32[]{:S(2)}) %all-to-all-start.2) | async-done | bytes 1966112 | tf_op jit(solution)/shard_map/all_to_all | solution.py:253
  3777.5 408.0 %all-reduce.19.cloned.1.call-done = (f32[160,512]{1,0:T(8,128)}, f32[14,512,256]{2,1,0:T(8,128)}, f32[14,256,512]{2,1,0:T(8,128)}) async-done(((f32[160,512]{1,0:T(8,128)}, f32[14,512,256]{2,1,0:T(8,128)}, f32[14,256,512]{2,1,0:T(8,128)}), (f32[160,512]{1,0:T(8,128)}, f32[14,512,256]{2,1,0:T(8,128)}, f32[14,256,512]{2,1,0:T(8,128)})) %all-reduce.19.cloned.1.call-update) | async-done | bytes 15007760 | tf_op jit(solution)/shard_map/psum | solution.py:256
  (296 shorter events, 382.8 us)
Async XLA Ops:
  7.2 2953.8 %copy-start = (bf16[6,512,128]{2,1,0:T(8,128)(2,1)S(1)}, bf16[6,512,128]{2,1,0:T(8,128)(2,1)}, u32[]{:S(2)}) copy-start(bf16[6,512,128]{2,1,0:T(8,128)(2,1)} %param.32) | copy-start | bytes 2359300
  9.0 63.1 %all-to-all-start = ((s32[8,768,10]{1,2,0:T(8,128)}), s32[8,768,10]{1,2,0:T(8,128)S(1)}, u32[]{:S(2)}, u32[]{:S(2)}) async-start(s32[8,768,10]{1,2,0:T(8,128)} %bitcast.167), calls=%async_computation | async-start | bytes 786432 | tf_op jit(solution)/shard_map/all_to_all | solution.py:63
  1122.2 27.0 copy-start.11
  1144.2 51.1 %all-to-all-start.1 = ((bf16[8,768,160]{1,2,0:T(8,128)(2,1)}), bf16[8,768,160]{1,2,0:T(8,128)(2,1)S(1)}, u32[]{:S(2)}, u32[]{:S(2)}) async-start(bf16[8,768,160]{1,2,0:T(8,128)(2,1)} %bitcast.187), calls=%async_computation.1 | async-start | bytes 3932160 | tf_op jit(solution)/shard_map/all_to_all | solution.py:69
  1149.2 1286.9 %reduce-scatter.4.cloned.1.call-start = ((), (), s32[]{:S(2)}) async-start(), calls=%async_computation.6 | async-start | bytes 15728640 | tf_op jit(solution)/shard_map/reduce_scatter | solution.py:92
  2221.1 67.6 %copy-start.17 = (pred[6144,10]{1,0:T(8,128)(4,1)S(1)}, pred[6144,10]{1,0:T(8,128)(4,1)}, u32[]{:S(2)}) copy-start(pred[6144,10]{1,0:T(8,128)(4,1)} %copy.86) | copy-start | bytes 184324
  2336.6 149.7 %all-gather.4.cloned.1.call-start = ((), (), s32[]{:S(2)}) async-start(), calls=%async_computation.7 | async-start | bytes 7864320 | tf_op jit(solution)/shard_map/all_gather | solution.py:101
  2419.7 27.7 copy-start.13
  2439.7 466.0 %reduce-scatter.6.cloned.1.call-start = ((), (), s32[]{:S(2)}) async-start(), calls=%async_computation.8 | async-start | bytes 62914560 | tf_op jit(solution)/shard_map/reduce_scatter | solution.py:122
  2562.4 624.2 %all-gather.6.cloned.1.call-start = ((), (), s32[]{:S(2)}) async-start(), calls=%async_computation.9 | async-start | bytes 31457280 | tf_op jit(solution)/shard_map/all_gather | solution.py:200
  2570.9 388.9 %copy-start.28 = (f32[1536,6]{0,1:T(8,128)}, f32[1536,6]{0,1:T(8,128)S(1)}, u32[]{:S(2)}) copy-start(f32[1536,6]{0,1:T(8,128)S(1)} %get-tuple-element.104) | copy-start | bytes 110596
  2570.9 395.1 %copy-start.36 = (bf16[1536,6]{0,1:T(8,128)(2,1)}, bf16[1536,6]{0,1:T(8,128)(2,1)S(1)}, u32[]{:S(2)}) copy-start(bf16[1536,6]{0,1:T(8,128)(2,1)S(1)} %get-tuple-element.103) | copy-start | bytes 55300
  2571.5 346.1 %copy-start.19 = (f32[1536,6]{0,1:T(8,128)}, f32[1536,6]{0,1:T(8,128)S(1)}, u32[]{:S(2)}) copy-start(f32[1536,6]{0,1:T(8,128)S(1)} %fusion.69) | copy-start | bytes 110596
  2571.6 339.7 %copy-start.22 = (f32[1536]{0:T(1024)}, f32[1536]{0:T(1024)S(1)}, u32[]{:S(2)}) copy-start(f32[1536]{0:T(1024)S(1)} %get-tuple-element.68) | copy-start | bytes 18436
  2571.6 339.7 %copy-start.24 = (f32[1536]{0:T(1024)}, f32[1536]{0:T(1024)S(1)}, u32[]{:S(2)}) copy-start(f32[1536]{0:T(1024)S(1)} %get-tuple-element.69) | copy-start | bytes 18436
  2571.6 339.7 %copy-start.26 = (f32[1536]{0:T(1024)}, f32[1536]{0:T(1024)S(1)}, u32[]{:S(2)}) copy-start(f32[1536]{0:T(1024)S(1)} %get-tuple-element.70) | copy-start | bytes 18436
  2571.7 339.5 %copy-start.30 = (f32[1536]{0:T(1024)}, f32[1536]{0:T(1024)S(1)}, u32[]{:S(2)}) copy-start(f32[1536]{0:T(1024)S(1)} %get-tuple-element.65) | copy-start | bytes 18436
  2571.7 339.5 %copy-start.32 = (f32[1536]{0:T(1024)}, f32[1536]{0:T(1024)S(1)}, u32[]{:S(2)}) copy-start(f32[1536]{0:T(1024)S(1)} %get-tuple-element.66) | copy-start | bytes 18436
  2571.7 339.5 %copy-start.34 = (f32[1536]{0:T(1024)}, f32[1536]{0:T(1024)S(1)}, u32[]{:S(2)}) copy-start(f32[1536]{0:T(1024)S(1)} %get-tuple-element.67) | copy-start | bytes 18436
  2979.5 26.5 slice-start
  2979.5 26.5 slice-start.1
  3032.7 324.3 %reduce-scatter.8.cloned.1.call-start = ((), (), s32[]{:S(2)}) async-start(), calls=%async_computation.10 | async-start | bytes 15728640 | tf_op jit(solution)/shard_map/reduce_scatter | solution.py:236
  3257.8 181.9 %all-gather.8.cloned.1.call-start = ((), (), s32[]{:S(2)}) async-start(), calls=%async_computation.11 | async-start | bytes 7864320 | tf_op jit(solution)/shard_map/all_gather | solution.py:240
  3263.1 94.0 %copy-start.29 = (f32[1536,6]{0,1:T(8,128)S(1)}, f32[1536,6]{0,1:T(8,128)}, u32[]{:S(2)}) copy-start(f32[1536,6]{0,1:T(8,128)} %copy-done.28) | copy-start | bytes 110596
  3263.1 94.0 %copy-start.52 = (bf16[6,512,6]{1,2,0:T(8,128)(2,1)S(1)}, bf16[6,512,6]{1,2,0:T(8,128)(2,1)}, u32[]{:S(2)}) copy-start(bf16[6,512,6]{1,2,0:T(8,128)(2,1)} %param.31) | copy-start | bytes 110596
  3268.6 98.3 %copy-start.10 = (bf16[1536,128]{0,1:T(8,128)(2,1)S(1)}, bf16[1536,128]{0,1:T(8,128)(2,1)}, u32[]{:S(2)}) copy-start(bf16[1536,128]{0,1:T(8,128)(2,1)} %copy-done.9) | copy-start | bytes 1179652
  3273.5 100.0 %copy-start.37 = (bf16[1536,6]{0,1:T(8,128)(2,1)S(1)}, bf16[1536,6]{0,1:T(8,128)(2,1)}, u32[]{:S(2)}) copy-start(bf16[1536,6]{0,1:T(8,128)(2,1)} %copy-done.36) | copy-start | bytes 55300
  3362.1 15.4 slice-start.5
  3362.2 324.2 %all-reduce.17.cloned.1.call-start = ((), (), s32[]{:S(2)}) async-start(), calls=%async_computation.13 | async-start | bytes 3866624 | tf_op jit(solution)/shard_map/psum | solution.py:257
  3412.1 365.4 %all-reduce.15.cloned.1.call-start = ((), (), s32[]{:S(2)}) async-start(), calls=%async_computation.12 | async-start | bytes 152576 | tf_op jit(solution)/shard_map/psum | solution.py:257
  3439.2 746.2 %all-reduce.19.cloned.1.call-start = ((), (), s32[]{:S(2)}) async-start(), calls=%async_computation.14 | async-start | bytes 30015488 | tf_op jit(solution)/shard_map/psum | solution.py:256
  3680.9 94.4 %all-to-all-start.2 = ((bf16[8,768,160]{1,2,0:T(8,128)(2,1)}), bf16[8,768,160]{1,2,0:T(8,128)(2,1)S(1)}, u32[]{:S(2)}, u32[]{:S(2)}) async-start(bf16[8,768,160]{1,2,0:T(8,128)(2,1)} %copy.111), calls=%async_computation.5 | async-start | bytes 3932160 | tf_op jit(solution)/shard_map/all_to_all | solution.py:253
  (47 other events, 338.0 us)
Sparse Core Ops, SparseCore 0:
  2336.7 99.2 reduce-scatter.3
  2439.9 46.3 all-gather.3
  2562.5 343.1 reduce-scatter.5
  3032.9 153.7 all-gather.5
  3257.9 99.0 reduce-scatter.7
  3362.3 46.3 all-gather.7
  3416.6 134.2 all-reduce.16
  3559.5 120.8 all-reduce.14
  3686.6 498.8 all-reduce.18
where the time goes:
time: 4230 us; the launch traced here: 4210 us
  local copies, waits for them, and re-layouts  2510 us (59%)
  waiting for transfers between devices  1160 us (27%)
  matrix products  215 us (5%)
  other arithmetic  213 us (5%)
  blocking collectives  80.2 us (2%)
    gather x5, local copies, waits for them, and re-layouts, shards(): jnp.take_along_axis(rows_three, slot_index[:, :, None], axis=0)  1090 us
    gather x3, local copies, waits for them, and re-layouts, shards(): found = jnp.take(table_rows, flat_index, axis=0)  1020 us
    psum x1, waiting for transfers between devices, shards(): lax.psum((up_grad, down_grad, proj_grad), 'wide')  408 us
    reduce_scatter x1, waiting for transfers between devices, shards(): lax.psum_scatter(partial_out, 'narrow', scatter_dimension=1, tiled=True)  334 us
    unnamed x151, local copies, waits for them, and re-layouts  206 us
    all_gather x1, waiting for transfers between devices, shards(): lax.all_gather(out_grad.astype(jnp.bfloat16), 'narrow', axis=1, tiled=True)  154 us
    all_to_all x1, waiting for transfers between devices, shards(): lax.all_to_all(returned.astype(jnp.bfloat16), 'wide', split_axis=0, conca...  85.8 us
  transfers between devices with their start and end apart: 12, of which 8 were waited for; matrix products, arithmetic and copies ran while one was open for 10% of the time, Pallas kernels for 0%

commit v1 on v0

v1 whole, which is shorter than its diff:
```python
import functools

import jax
import jax.numpy as jnp
from jax import lax
from jax.experimental import pallas as pl
from jax.experimental.pallas import tpu as pltpu
from jax.sharding import PartitionSpec as P

D = 512
HID = 1024
EMB = 16
DENSE = 128
DOMAINS = 6
SHARED = 2
DOM_EXP = 2
DSLOT = 1024
HALF = DSLOT // 2
VMEM = 56 * 2**20
BF = jnp.bfloat16
F32 = jnp.float32


def dot(a, b, ca, cb):
    return lax.dot_general(a, b, (((ca,), (cb,)), ((), ())), preferred_element_type=F32)


def lookup_kernel(lo_n, hi_n, fields, idx_ref, tab_ref, out_ref):
    length = idx_ref.shape[-1]
    shift = hi_n.bit_length() - 1
    for f in range(fields):
        idx = idx_ref[0, f : f + 1, :]
        hi = jnp.where(idx >= 0, idx & (hi_n - 1), -1)
        lo = lax.shift_right_logical(jnp.maximum(idx, 0), shift)
        hot = (lax.broadcasted_iota(jnp.int32, (hi_n, length), 0) == hi).astype(BF)
        lhs = tab_ref[:, f * EMB : (f + 1) * EMB, :].reshape(lo_n * EMB, hi_n)
        res = jnp.dot(lhs, hot, preferred_element_type=F32)
        acc = res[0:EMB]
        for step in range(1, lo_n):
            acc = jnp.where(lo == step, res[step * EMB : (step + 1) * EMB], acc)
        out_ref[0, f * EMB : (f + 1) * EMB, :] = acc.astype(BF)


def lookup(idx, tab, name, order=lambda i: i):
    groups, fields, length = idx.shape
    lo_n, cols, hi_n = tab.shape
    return pl.pallas_call(
        functools.partial(lookup_kernel, lo_n, hi_n, fields),
        grid=(groups,),
        in_specs=[
            pl.BlockSpec((1, fields, length), lambda i: (order(i), 0, 0)),
            pl.BlockSpec((lo_n, cols, hi_n), lambda i: (0, 0, 0)),
        ],
        out_specs=pl.BlockSpec((1, cols, length), lambda i: (i, 0, 0)),
        out_shape=jax.ShapeDtypeStruct((groups, cols, length), BF),
        compiler_params=pltpu.CompilerParams(vmem_limit_bytes=VMEM),
        cost_estimate=pl.CostEstimate(
            flops=2 * groups * length * cols * lo_n * hi_n, bytes_accessed=8 * 2**20, transcendentals=0
        ),
        name=name,
    )(idx, tab)


def place_kernel(lo_n, hi_n, steps, idx_ref, grad_ref, out_ref):
    length = idx_ref.shape[-1] // steps
    shift = hi_n.bit_length() - 1
    total = None
    for s in range(steps):
        cols = slice(s * length, (s + 1) * length)
        idx = idx_ref[0, :, cols]
        hi = idx & (hi_n - 1)
        lo = lax.shift_right_logical(idx, shift)
        grad = grad_ref[0, :, cols]
        hot = (lax.broadcasted_iota(jnp.int32, (hi_n, length), 0) == hi).astype(BF)
        lhs = jnp.concatenate(
            [jnp.where(lo == step, grad, jnp.zeros_like(grad)) for step in range(lo_n)], axis=0
        )
        part = dot(lhs, hot, 1, 1)
        total = part if total is None else total + part
    out_ref[...] = total.reshape(lo_n, EMB, hi_n).astype(BF)


def place(idx, grad, lo_n, hi_n):
    fields, _, length = idx.shape
    return pl.pallas_call(
        functools.partial(place_kernel, lo_n, hi_n, 4),
        grid=(fields,),
        in_specs=[
            pl.BlockSpec((1, 1, length), lambda i: (i, 0, 0)),
            pl.BlockSpec((1, EMB, length), lambda i: (i, 0, 0)),
        ],
        out_specs=pl.BlockSpec((lo_n, EMB, hi_n), lambda i: (0, i, 0)),
        out_shape=jax.ShapeDtypeStruct((lo_n, fields * EMB, hi_n), BF),
        compiler_params=pltpu.CompilerParams(vmem_limit_bytes=VMEM),
        cost_estimate=pl.CostEstimate(
            flops=2 * fields * EMB * length * lo_n * hi_n, bytes_accessed=6 * 2**20, transcendentals=0
        ),
        name="place_rows",
    )(idx, grad)


def layer_norm(values, gains, shifts):
    center = jnp.mean(values, axis=-1, keepdims=True)
    centered = values - center
    variance = jnp.mean(centered * centered, axis=-1, keepdims=True)
    return centered * lax.rsqrt(variance + 1e-05) * gains + shifts


def combine(outputs, logits_gate, gains, shifts):
    normed = layer_norm(outputs, gains, shifts)
    shared_gates = jax.nn.softmax(logits_gate[:, :SHARED], axis=-1)
    domain_gates = jax.nn.softmax(logits_gate[:, SHARED : SHARED + DOM_EXP], axis=-1)
    top_gates = jax.nn.softmax(logits_gate[:, SHARED + DOM_EXP :], axis=-1)
    shared = sum(shared_gates[:, k : k + 1] * normed[k] for k in range(SHARED))
    own = sum(domain_gates[:, k : k + 1] * normed[SHARED + k] for k in range(DOM_EXP))
    return top_gates[:, 0:1] * shared + top_gates[:, 1:2] * own


def split_dot(rows, weights, spec):
    return jnp.concatenate(
        [
            jnp.einsum(spec, rows[:DSLOT], weights[0], preferred_element_type=F32),
            jnp.einsum(spec, rows[DSLOT:], weights[1], preferred_element_type=F32),
        ],
        axis=0,
    )


def split_sum(rows):
    return jnp.stack([jnp.sum(rows[:DSLOT], axis=0), jnp.sum(rows[DSLOT:], axis=0)])


def spread_rows(pair, rows):
    full = jnp.broadcast_to(pair[0], (DSLOT,) + pair[0].shape)
    half = jnp.broadcast_to(pair[1], (rows - DSLOT,) + pair[1].shape)
    return jnp.concatenate([full, half], axis=0)


def own_stats(rows, weight):
    count = jnp.sum(weight)
    mean = jnp.sum(rows * weight[:, None], axis=0) / jnp.maximum(count, 1.0)
    off = rows - mean
    return [mean, jnp.sum(off * off * weight[:, None], axis=0), jnp.broadcast_to(count, mean.shape)]


def pool(means, squares, counts):
    total = jnp.sum(counts, axis=0)
    mean = jnp.sum(counts * means, axis=0) / total
    off = means - mean
    return mean, (jnp.sum(squares, axis=0) + jnp.sum(counts * off * off, axis=0)) / total


def shards(
    embed_table,
    requests,
    slot_index,
    event_mask,
    labels,
    dense_feats,
    proj_weight,
    dense_weight,
    proj_bias,
    up_weight,
    down_weight,
    norm_gain,
    norm_shift,
    gate_weight,
    tower_in,
    tower_bias,
    tower_out,
    tower_out_bias,
):
    narrow = lax.axis_size("narrow")
    me = lax.axis_index("narrow")
    chip, core = me // 2, me % 2
    ev_rows, fields = slot_index.shape
    rows = ev_rows // narrow
    owners, cap = requests.shape[1], requests.shape[2]
    hid_here = up_weight.shape[2]
    other_chip = [(i, i ^ 2) for i in range(narrow)]
    other_core = [(i, i ^ 1) for i in range(narrow)]
    full = 3 * chip + 2 * core
    half = 3 * chip + 1

    def swap(x, pairs):
        return lax.ppermute(x, "narrow", pairs)

    asked = lax.all_to_all(requests[0].transpose(0, 2, 1), "wide", 0, 0, tiled=True)

    def chip_experts(w, which):
        return jnp.concatenate(
            [w[:SHARED], lax.dynamic_slice_in_dim(w, SHARED + 6 * which, 6, axis=0)], axis=0
        )

    def core_experts(w, which, axis):
        at = lambda start, size: lax.dynamic_slice_in_dim(w, start, size, axis=axis)
        return jnp.concatenate([at(0, 2), at(2 + 4 * which, 2), at(4, 2)], axis=axis)

    def bring(w):
        near = chip_experts(w, chip)
        far = swap(chip_experts(w, 1 - chip), other_chip)
        both = jnp.stack([near, far])
        mine = core_experts(both, core, 1)
        theirs = swap(core_experts(both, 1 - core, 1), other_core)
        return jnp.concatenate([mine, theirs], axis=0)

    up = bring(up_weight)
    down = bring(down_weight)
    up = up.transpose(1, 2, 0, 3).reshape(6, D, HID)
    down = down.transpose(1, 0, 2, 3).reshape(6, HID, D)
    proj_full = lax.all_gather(proj_weight, "narrow", axis=0, tiled=True)

    def turned(x):
        return jnp.where(core == 1, jnp.roll(x, -HALF, axis=0), x)

    live = turned(event_mask).astype(F32)
    label_rows = turned(labels).astype(F32)
    feats = turned(dense_feats)
    blank = jnp.zeros((2, DENSE), F32)
    stats = jnp.stack(own_stats(feats[:DSLOT], live[:DSLOT]) + own_stats(feats[DSLOT:], live[DSLOT:]))
    stats = jnp.concatenate([stats, blank], axis=0)
    stats = jnp.concatenate([stats, swap(stats, other_core)], axis=0)
    every = lax.all_to_all(
        jnp.broadcast_to(stats, (owners,) + stats.shape), "wide", 0, 0, tiled=True
    )
    full_mean, full_spread = pool(every[:, 0], every[:, 1], every[:, 2])
    both = jnp.concatenate([every[:, 3:6], every[:, 11:14]], axis=0)
    half_mean, half_spread = pool(both[:, 0], both[:, 1], both[:, 2])
    centered = feats - spread_rows(jnp.stack([full_mean, half_mean]), rows)
    scale = lax.rsqrt(jnp.stack([full_spread, half_spread]) + 1e-05)
    dense_low = (centered * spread_rows(scale, rows)).astype(BF)

    table_rows = embed_table.shape[0]
    tab = embed_table.reshape(32, table_rows // 32, fields * EMB).transpose(0, 2, 1)
    if cap % 128 == 0:
        found = lookup(asked, tab, "lookup_rows")
    else:
        flat = asked.transpose(1, 0, 2).reshape(fields, DOMAINS, DSLOT).transpose(1, 0, 2)
        found = lookup(flat, tab, "lookup_rows")
        found = found.transpose(1, 0, 2).reshape(fields * EMB, owners, cap).transpose(1, 0, 2)
    received = lax.all_to_all(found, "wide", 0, 0, tiled=True)

    hi_n = 256
    lo_n = ev_rows // hi_n
    received = received.transpose(1, 0, 2).reshape(fields * EMB, lo_n, hi_n).transpose(1, 0, 2)
    blocks = ev_rows // HALF
    order = [q * 3 + (s + q % 2) % 3 for q in range(narrow) for s in range(3)]
    slots = slot_index.reshape(blocks, HALF, fields)
    slots = jnp.stack([slots[b] for b in order]).transpose(0, 2, 1)
    embedded = lookup(slots, received, "order_rows")
    embedded = embedded.reshape(narrow, 3, fields * EMB, HALF).transpose(0, 2, 1, 3)
    embedded = embedded.reshape(narrow, fields * EMB, rows)
    embedded = lax.all_to_all(embedded, "narrow", 0, 0, tiled=True)
    embedded = embedded.reshape(narrow * fields * EMB, rows)

    projected = dot(embedded, proj_full, 0, 0) + jnp.dot(dense_low, dense_weight, preferred_element_type=F32)
    projected = projected + proj_bias.astype(F32)
    inputs = projected.astype(BF)

    parts = ((slice(0, 2), slice(0, rows)), (slice(2, 4), slice(0, DSLOT)), (slice(4, 6), slice(DSLOT, rows)))
    pres = [jnp.einsum("rm,kmh->krh", inputs[r], up[k], preferred_element_type=F32) for k, r in parts]
    gelus = [jax.vjp(jax.nn.gelu, pre) for pre in pres]
    acts = [g[0].astype(BF) for g in gelus]
    outs = [
        jnp.einsum("krh,khm->krm", a, down[k], preferred_element_type=F32) for a, (k, r) in zip(acts, parts)
    ]
    expert_out = jnp.concatenate([outs[0], jnp.concatenate(outs[1:], axis=1)], axis=0)

    def pick(w):
        return jnp.stack(
            [
                lax.dynamic_index_in_dim(w, full, keepdims=False),
                lax.dynamic_index_in_dim(w, half, keepdims=False),
            ]
        )

    def expert_rows(w):
        w = w.astype(F32)
        own = pick(w[SHARED:].reshape(DOMAINS, DOM_EXP, D))
        return jnp.concatenate(
            [
                jnp.broadcast_to(w[:SHARED, None, :], (SHARED, rows, D)),
                spread_rows(own, rows).transpose(1, 0, 2),
            ],
            axis=0,
        )

    gate_two = pick(gate_weight)
    gate_logits = split_dot(inputs, gate_two, "rm,mg->rg")
    mixture, combine_back = jax.vjp(
        combine, expert_out, gate_logits, expert_rows(norm_gain), expert_rows(norm_shift)
    )
    hidden = mixture.astype(BF)
    tower_two = pick(tower_in)
    tower_pre = split_dot(hidden, tower_two, "rm,mk->rk")
    tower_pre = tower_pre + spread_rows(pick(tower_bias).astype(F32), rows)
    tower_act, tower_back = jax.vjp(jax.nn.gelu, tower_pre)
    out_rows = spread_rows(pick(tower_out).astype(F32), rows)
    logits = jnp.sum(tower_act * out_rows, axis=1)
    logits = logits + spread_rows(pick(tower_out_bias).astype(F32), rows)
    logit_grad = (jax.nn.sigmoid(logits) - label_rows) * live
    out_bias_grad = split_sum(logit_grad)
    out_vector_grad = split_sum(logit_grad[:, None] * tower_act)
    pre_low = tower_back(logit_grad[:, None] * out_rows)[0].astype(BF)
    bias_tower_grad = split_sum(pre_low.astype(F32))

    def split_outer(a, b):
        return jnp.stack(
            [dot(a[:DSLOT], b[:DSLOT], 0, 0), dot(a[DSLOT:], b[DSLOT:], 0, 0)]
        )

    tower_weight_grad = split_outer(hidden, pre_low)
    hidden_grad = split_dot(pre_low, tower_two, "rk,mk->rm")
    out_grad, gate_logit_grad, gain_rows_grad, shift_rows_grad = combine_back(hidden_grad)

    def expert_sums(g):
        own = jnp.stack([jnp.sum(g[SHARED:, :DSLOT], axis=1), jnp.sum(g[SHARED:, DSLOT:], axis=1)])
        return jnp.sum(g[:SHARED], axis=1), own

    gain_shared, gain_own = expert_sums(gain_rows_grad)
    shift_shared, shift_own = expert_sums(shift_rows_grad)
    gate_low = gate_logit_grad
    gate_grad = jnp.stack(
        [
            jnp.dot(inputs[:DSLOT].astype(F32).T, gate_low[:DSLOT], precision=lax.Precision.HIGHEST),
            jnp.dot(inputs[DSLOT:].astype(F32).T, gate_low[DSLOT:], precision=lax.Precision.HIGHEST),
        ]
    )
    inputs_gate_grad = jnp.concatenate(
        [
            jnp.dot(gate_low[:DSLOT], gate_two[0].astype(F32).T, precision=lax.Precision.HIGHEST),
            jnp.dot(gate_low[DSLOT:], gate_two[1].astype(F32).T, precision=lax.Precision.HIGHEST),
        ],
        axis=0,
    )
    out_low = out_grad.astype(BF)
    out_parts = [out_low[:SHARED], out_low[SHARED:, :DSLOT], out_low[SHARED:, DSLOT:]]
    act_grads = [
        jnp.einsum("krm,khm->krh", g, down[k], preferred_element_type=F32) for g, (k, r) in zip(out_parts, parts)
    ]
    pre_grads = [g[1](a)[0].astype(BF) for g, a in zip(gelus, act_grads)]
    down_grads = [
        jnp.einsum("krh,krm->khm", a, g, preferred_element_type=F32).astype(BF) for a, g in zip(acts, out_parts)
    ]
    up_grads = [
        jnp.einsum("rm,krh->kmh", inputs[r], g, preferred_element_type=F32).astype(BF)
        for g, (k, r) in zip(pre_grads, parts)
    ]
    input_parts = [
        jnp.einsum("krh,kmh->rm", g, up[k], preferred_element_type=F32) for g, (k, r) in zip(pre_grads, parts)
    ]
    input_sum = input_parts[0] + jnp.concatenate(input_parts[1:], axis=0) + inputs_gate_grad
    input_low = input_sum.astype(BF)

    embed_grad = dot(proj_full, input_low, 1, 1).astype(BF).reshape(narrow, fields * EMB, rows)
    embed_grad = lax.all_to_all(embed_grad, "narrow", 0, 0, tiled=True)
    embed_grad = embed_grad.transpose(1, 0, 2).reshape(fields, EMB, ev_rows)
    slot_rows = slots.transpose(1, 0, 2).reshape(fields, 1, ev_rows)
    returned = place(slot_rows, embed_grad, lo_n, hi_n)
    returned = returned.transpose(1, 0, 2).reshape(fields * EMB, owners, cap).transpose(1, 0, 2)
    row_grads = lax.all_to_all(returned, "wide", 0, 0, tiled=True)
    row_grads = row_grads.transpose(0, 2, 1).astype(F32)[None]

    up_g = jnp.concatenate(up_grads, axis=0).reshape(6, D, narrow, hid_here).transpose(2, 0, 1, 3)
    down_g = jnp.concatenate(down_grads, axis=0).reshape(6, narrow, hid_here, D).transpose(1, 0, 2, 3)
    down_g = down_g.reshape(narrow, 6, hid_here, 2, D // 2).transpose(0, 1, 3, 2, 4)
    grads = jnp.concatenate([up_g, down_g.reshape(narrow, 6, 2 * hid_here, D // 2)], axis=2)
    mine, theirs = grads[:2], swap(grads[2:], other_core)
    add = lambda a, b: (a.astype(F32) + b.astype(F32)).astype(BF)
    first = jnp.where(core == 0, mine[:, 2:4], theirs[:, 2:4])
    last = jnp.where(core == 0, theirs[:, 2:4], mine[:, 2:4])
    chip_sum = jnp.concatenate(
        [add(mine[:, :2], theirs[:, :2]), first, add(mine[:, 4:], theirs[:, 4:]), last], axis=1
    )
    part = lax.psum_scatter(chip_sum, "wide", scatter_dimension=2, tiled=True)
    far = swap(part[1], other_chip)
    near = part[0]
    low_half = jnp.where(chip == 0, near[2:], far[2:])
    high_half = jnp.where(chip == 0, far[2:], near[2:])
    part = jnp.concatenate([add(near[:2], far[:2]), low_half, high_half], axis=0)
    whole = lax.all_gather(part, "wide", axis=1, tiled=True)
    up_grad = whole[:, :D].astype(F32)
    down_grad = whole[:, D:].reshape(14, 2, hid_here, D // 2).transpose(0, 2, 1, 3)
    down_grad = down_grad.reshape(14, hid_here, D).astype(F32)

    proj_grad = dot(embedded, input_low, 1, 0)
    dense_grad = dot(dense_low, input_low, 0, 0)
    bias_grad = jnp.sum(input_low.astype(F32), axis=0)

    def put(pair):
        zero = jnp.zeros((DOMAINS,) + pair.shape[1:], F32)
        zero = lax.dynamic_update_index_in_dim(zero, pair[0], full, 0)
        return lax.dynamic_update_index_in_dim(zero, pair[1], half, 0)

    def put_experts(shared, own):
        return jnp.concatenate([shared, put(own).reshape(DOMAINS * DOM_EXP, D)], axis=0)

    proj_grad = lax.psum_scatter(proj_grad, "narrow", scatter_dimension=0, tiled=True)
    proj_grad = lax.psum(proj_grad, "wide")
    common = lax.psum(
        (
            dense_grad,
            bias_grad,
            put_experts(gain_shared, gain_own),
            put_experts(shift_shared, shift_own),
            put(gate_grad),
            put(tower_weight_grad),
            put(bias_tower_grad),
            put(out_vector_grad),
            put(out_bias_grad),
        ),
        ("wide", "narrow"),
    )
    logits = jnp.where(core == 1, jnp.roll(logits, HALF, axis=0), logits)
    return (
        logits,
        row_grads,
        proj_grad,
        common[0],
        common[1],
        up_grad,
        down_grad,
        common[2],
        common[3],
        common[4],
        common[5],
        common[6],
        common[7],
        common[8],
    )


def solution(mesh):
    placed = (
        P("wide", "narrow"),
        P("wide", None, None, "narrow"),
        P("wide", "narrow"),
        P(("wide", "narrow")),
        P(("wide", "narrow")),
        P(("wide", "narrow"), None),
        P("narrow", None),
        P(),
        P(),
        P(None, None, "narrow"),
        P(None, "narrow", None),
        P(),
        P(),
        P(),
        P(),
        P(),
        P(),
        P(),
    )
    return jax.shard_map(
        shards,
        mesh=mesh,
        in_specs=placed,
        out_specs=(
            P(("wide", "narrow")),
            P("wide", None, None, "narrow"),
            P("narrow", None),
            P(),
            P(),
            P(None, None, "narrow"),
            P(None, "narrow", None),
            P(),
            P(),
            P(),
            P(),
            P(),
            P(),
            P(),
        ),
        check_vma=False,
    )
```

time: 4230 us -> 1170 us (0.28)
  local copies, waits for them, and re-layouts: 2510 us -> 171 us
  waiting for transfers between devices: 1160 us -> 540 us
  matrix products: 215 us -> 124 us
  Pallas kernels: 0 us -> 80.5 us
  blocking collectives: 80.2 us -> 16.7 us
    gather x8 -> x0, local copies, waits for them, and re-layouts: 2100 us -> none  [the longest x5 1090 us: shards(): jnp.take_along_axis(rows_three, slot_index[:, :, None], axis=0)]
    reduce_scatter x3 -> x2, waiting for transfers between devices: 433 us -> 121 us  [the longest x1 121 us: shards(): part = lax.psum_scatter(chip_sum, 'wide', scatter_dimension=2, tiled=True)]
    all_gather x3 -> x1, waiting for transfers between devices: 193 us -> 1.07 us  [shards(): whole = lax.all_gather(part, 'wide', axis=1, tiled=True)]
    unnamed x151 -> x276, local copies, waits for them, and re-layouts: 206 us -> 28.7 us
    psum x3, waiting for transfers between devices: 408 us -> 297 us  [the longest x2 224 us: shards(): lax.psum((dense_grad, bias_grad, put_experts(gain_shared, gain_own), put_...]
    dot_general x37 -> x35, matrix products: 215 us -> 124 us  [the longest x3 30.2 us: shards(): jnp.einsum('krm,khm->krh', g, down[k], preferred_element_type=F32)]
    pallas_call x0 -> x3, Pallas kernels: none -> 80.5 us  [the longest x2 64.3 us: lookup(): pl.pallas_call(functools.partial(lookup_kernel, lo_n, hi_n, fields), grid...]
    psum x2 -> x0, blocking collectives: 80.2 us -> none  [the longest x1 42.2 us: shards(): spread = lax.psum(part_spread, ('wide', 'narrow')) / counts[:, None]]
  transfers between devices with their start and end apart: 12 -> 19, of which waited for: 8 -> 10; matrix products, arithmetic and copies ran while one was open for 10% -> 19% of each run, Pallas kernels for 0% -> 7%
where the time goes in v1:
time: 1170 us; the launch traced here: 1160 us
  waiting for transfers between devices  540 us (46%)
  other arithmetic  172 us (15%)
  local copies, waits for them, and re-layouts  171 us (15%)
  matrix products  124 us (11%)
  Pallas kernels  80.5 us (7%)
  starting transfers between devices  37.9 us (3%)
  between operations  19.6 us (2%)
  blocking collectives  16.7 us (1%)
    psum x2, waiting for transfers between devices, shards(): lax.psum((dense_grad, bias_grad, put_experts(gain_shared, gain_own), put_...  224 us
    reduce_scatter x1, waiting for transfers between devices, shards(): part = lax.psum_scatter(chip_sum, 'wide', scatter_dimension=2, tiled=True)  121 us
    psum x1, waiting for transfers between devices, shards(): proj_grad = lax.psum(proj_grad, 'wide')  73 us
    all_to_all x1, waiting for transfers between devices, shards(): row_grads = lax.all_to_all(returned, 'wide', 0, 0, tiled=True)  72.2 us
    pallas_call x2, Pallas kernels, lookup(): pl.pallas_call(functools.partial(lookup_kernel, lo_n, hi_n, fields), grid...  64.3 us
    dot_general x3, matrix products, shards(): jnp.einsum('krm,khm->krh', g, down[k], preferred_element_type=F32)  30.2 us
    unnamed x276, local copies, waits for them, and re-layouts  28.7 us
  transfers between devices with their start and end apart: 19, of which 10 were waited for; matrix products, arithmetic and copies ran while one was open for 19% of the time, Pallas kernels for 7%

profile of v1, /device:TPU:0, one launch (start us, length us, event | category | flops | bytes accessed | tf_op | source)
XLA Modules:
  0.0 1161.7 jit_solution(17305581265292344925)
XLA Ops:
  9.9 7.3 all-to-all-start
  65.0 41.8 %lookup_rows.1 = bf16[8,160,768]{2,1,0:T(8,128)(2,1)} custom-call(s32[8,10,768]{2,1,0:T(8,128)} %copy-done.56, bf16[32,160,512]{2,1,0:T(8,128)(2,1)} %bitcast.383), custom_call_target="tpu_custom_call" | custom-call | flops 32212254720 | bytes 8388608 | tf_op jit(solution)/shard_map/lookup_rows/pallas_call | solution.py:47
  112.8 16.7 %all_gather.6 = bf16[640,512]{1,0:T(8,128)(2,1)S(1)} all-gather(bf16[160,512]{1,0:T(8,128)(2,1)S(1)} %copy-done.78), channel_id=1, replica_groups=mesh['wide'=8,'narrow'=4] {'narrow'}, dimensions={0}, use_global_device_ids=true | all-gather | bytes 819200 | tf_op jit(solution)/shard_map/all_gather | solution.py:211
  144.7 13.3 %all-to-all-done.1 = bf16[8,160,768]{2,1,0:T(8,128)(2,1)} async-done(((bf16[8,160,768]{2,1,0:T(8,128)(2,1)}), bf16[8,160,768]{2,1,0:T(8,128)(2,1)}, u32[]{:S(2)}, u32[]{:S(2)}) %all-to-all-start.1) | async-done | bytes 1966112 | tf_op jit(solution)/shard_map/all_to_all | solution.py:241
  169.3 22.5 %order_rows.1 = bf16[12,160,512]{2,1,0:T(8,128)(2,1)} custom-call(s32[12,10,512]{2,1,0:T(8,128)} %bitcast.12.idx_ref, bf16[24,160,256]{2,1,0:T(8,128)(2,1)} %bitcast.392), custom_call_target="tpu_custom_call" | custom-call | flops 12079595520 | bytes 8388608 | tf_op jit(solution)/shard_map/order_rows/pallas_call | solution.py:47
  262.1 6.9 fusion.50
  271.0 6.7 fusion.161
  277.7 7.9 fusion.164
  298.6 12.9 %fusion.9 = f32[4,1536,512]{1,2,0:T(8,128)} fusion(f32[2,1536,512]{1,2,0:T(8,128)S(1)} %bitcast.360, f32[2,1536,512]{1,2,0:T(8,128)} %broadcast_in_dim.161, f32[2,1536,512]{1,2,0:T(8,128)} %maximum_bitcast_fusion.3, f32[2,1536,512]{1,2,0:T(8,128)} %broadcast_in_dim.164, f32[4,1536]{1,0:T(4,128)S(1)} %fusion.126, f32[4,1536]{1,0:T(4,128)S(1)} %broadcast_multiply_fusion.1, ...), kind=kLoop, calls=%fused_computation.18 | loop fusion | flops 25165824 | bytes 50380800 | tf_op jit(solution)/shard_map/jvp()/add | solution.py:106
  325.3 7.4 multiply_multiply_fusion.10
  332.8 12.6 %multiply_multiply_fusion.4 = (f32[4,1536,512]{1,2,0:T(8,128)}, f32[4,1536]{1,0:T(4,128)S(1)}) fusion(f32[4,1536]{1,0:T(4,128)S(1)} %fusion.126, f32[4,1536]{1,0:T(4,128)S(1)} %broadcast_multiply_fusion.1, f32[2,512,512]{1,2,0:T(8,128)S(1)} %copy-done.5, f32[2,1024,512]{1,2,0:T(8,128)S(1)} %fusion.161, f32[2,1536,512]{1,2,0:T(8,128)S(1)} %fusion.164, ...), kind=kLoop, calls=%fused_computation.30 | loop fusion | flops 37742592 | bytes 50405376 | tf_op jit(solution)/shard_map/transpose(jvp())/mul | solution.py:106
  345.4 13.4 %pad_add_fusion = (f32[4,1536,512]{1,2,0:T(8,128)}, f32[4,1536]{1,0:T(4,128)S(1)}) fusion(f32[1,1536,512]{1,2,0:T(8,128)} %get-tuple-element.95, f32[1,1536,512]{1,2,0:T(8,128)} %get-tuple-element.96, f32[1,1536,512]{1,2,0:T(8,128)} %get-tuple-element.92, f32[1,1536,512]{1,2,0:T(8,128)} %get-tuple-element.91, f32[4,1536]{1,0:T(4,128)S(1)} %multiply_multiply_fusion.14, ...), kind=kLoop, calls=%fused_computation.26 | loop fusion | flops 40888320 | bytes 50429952 | tf_op jit(solution)/shard_map/transpose(jvp())/add_any | solution.py:114
  358.8 11.7 %add_convert_fusion = bf16[4,1536,512]{1,2,0:T(8,128)(2,1)} fusion(f32[4,1536]{1,0:T(4,128)S(1)} %negate_multiply_fusion, f32[4,1536]{1,0:T(4,128)S(1)} %multiply_multiply_fusion.14, f32[4,1536]{1,0:T(4,128)S(1)} %broadcast_multiply_fusion.1, f32[4,1536]{1,0:T(4,128)S(1)} %fusion.126, f32[2,1536,512]{1,2,0:T(8,128)S(1)} %bitcast.360, ...), kind=kLoop, calls=%fused_computation.24 | loop fusion | flops 44040192 | bytes 44138496 | tf_op jit(solution)/shard_map/convert_element_type | solution.py:336
  370.6 6.7 fusion.30
  379.6 8.8 fusion.19
  388.5 9.0 convolution_convert_fusion.2
  397.5 8.7 fusion.44
  406.2 14.7 %fusion.6 = bf16[2,1536,1024]{1,2,0:T(8,128)(2,1)} fusion(f32[2,1024,1536]{2,1,0:T(8,128)} %fusion.50, bf16[4,1536,512]{1,2,0:T(8,128)(2,1)S(1)} %copy-done.24, bf16[2,1024,512]{1,2,0:T(8,128)(2,1)S(1)} %copy-done.44), kind=kOutput, calls=%fused_computation.13 | convolution fusion | flops 3284140032 | bytes 27262976 | tf_op jit(solution)/shard_map/krm,khm->krh/dot_general | solution.py:339
  431.3 8.7 copy.260
  445.5 9.8 reshape.591
  464.4 10.1 collective-permute-done.5
  502.3 7.2 convert_reduce_fusion
  514.1 121.4 %reduce-scatter.5.cloned.1.call-done = bf16[2,8,128,256]{3,2,1,0:T(8,128)(2,1)} async-done(((bf16[2,8,1024,256]{3,2,1,0:T(8,128)(2,1)}), bf16[2,8,128,256]{3,2,1,0:T(8,128)(2,1)}) %reduce-scatter.5.cloned.1.call-update) | async-done | bytes 1048592 | tf_op jit(solution)/shard_map/reduce_scatter | solution.py:375
  638.2 12.2 %collective-permute-done.6 = bf16[8,128,256]{2,1,0:T(8,128)(2,1)S(1)} collective-permute-done((bf16[8,128,256]{2,1,0:T(8,128)(2,1)S(1)}, bf16[8,128,256]{2,1,0:T(8,128)(2,1)S(1)}, u32[]{:S(2)}, u32[]{:S(2)}) %collective-permute-start.6) | collective-permute-done | bytes 524320 | tf_op jit(solution)/shard_map/ppermute | solution.py:186
  673.3 12.8 %all-to-all-done.4 = bf16[4,160,1536]{2,1,0:T(8,128)(2,1)S(1)} async-done(((bf16[4,160,1536]{2,1,0:T(8,128)(2,1)}), bf16[4,160,1536]{2,1,0:T(8,128)(2,1)S(1)}, u32[]{:S(2)}, u32[]{:S(2)}) %all-to-all-start.4) | async-done | bytes 1966112 | tf_op jit(solution)/shard_map/all_to_all | solution.py:356
  693.7 16.2 %place_rows.1 = bf16[24,160,256]{2,1,0:T(8,128)(2,1)} custom-call(s32[10,1,6144]{2,1,0:T(1,128)} %reshape.579.idx_ref, bf16[10,16,6144]{2,1,0:T(8,128)(2,1)} %reshape.587.grad_ref), custom_call_target="tpu_custom_call" | custom-call | flops 12079595520 | bytes 6291456 | tf_op jit(solution)/shard_map/place_rows/pallas_call | solution.py:85
  742.2 72.2 %all-to-all-done.5 = bf16[8,160,768]{2,1,0:T(8,128)(2,1)} async-done(((bf16[8,160,768]{2,1,0:T(8,128)(2,1)}), bf16[8,160,768]{2,1,0:T(8,128)(2,1)}, u32[]{:S(2)}, u32[]{:S(2)}) %all-to-all-start.5) | async-done | bytes 1966112 | tf_op jit(solution)/shard_map/all_to_all | solution.py:361
  819.2 7.2 fusion.173
  833.1 10.5 reshape.597
  843.6 81.5 %all-reduce.22.cloned.1.call-done = (f32[512]{0:T(512)}, f32[14,512]{1,0:T(8,128)}, f32[14,512]{1,0:T(8,128)}, f32[6,128]{1,0:T(8,128)}, f32[6,128]{1,0:T(8,128)}, /*index=5*/f32[6]{0:T(128)}) async-done(((f32[512]{0:T(512)}, f32[14,512]{1,0:T(8,128)}, f32[14,512]{1,0:T(8,128)}, f32[6,128]{1,0:T(8,128)}, f32[6,128]{1,0:T(8,128)}, /*index=5*/f32[6]{0:T(128)}), (f32[512]{0:T(512)}, f32[14,512]{1,0:T(8,128)}, ...) | async-done | bytes 65576 | tf_op jit(solution)/shard_map/psum | solution.py:400
  925.1 142.5 %all-reduce.24.cloned.1.call-done = (f32[128,512]{1,0:T(8,128)}, f32[6,512,6]{1,2,0:T(8,128)}, f32[6,512,128]{2,1,0:T(8,128)}) async-done(((f32[128,512]{1,0:T(8,128)}, f32[6,512,6]{1,2,0:T(8,128)}, f32[6,512,128]{2,1,0:T(8,128)}), (f32[128,512]{1,0:T(8,128)}, f32[6,512,6]{1,2,0:T(8,128)}, f32[6,512,128]{2,1,0:T(8,128)})) %all-reduce.24.cloned.1.call-update) | async-done | bytes 1908752 | tf_op jit(solution)/shard_map/psum | solution.py:400
  1067.6 73.0 %all-reduce.20.cloned.1.call-done = f32[160,512]{1,0:T(8,128)} async-done(((f32[160,512]{1,0:T(8,128)}), f32[160,512]{1,0:T(8,128)}) %all-reduce.20.cloned.1.call-update) | async-done | bytes 327696 | tf_op jit(solution)/shard_map/psum | solution.py:399
  (538 shorter events, 327.8 us)
Async XLA Ops:
  8.0 309.8 %copy-start = (bf16[6,512,128]{2,1,0:T(8,128)(2,1)S(1)}, bf16[6,512,128]{2,1,0:T(8,128)(2,1)}, u32[]{:S(2)}) copy-start(bf16[6,512,128]{2,1,0:T(8,128)(2,1)} %param.32) | copy-start | bytes 2359300
  9.9 48.4 %all-to-all-start = ((s32[8,10,768]{2,1,0:T(8,128)}), s32[8,10,768]{2,1,0:T(8,128)S(1)}, u32[]{:S(2)}, u32[]{:S(2)}) async-start(s32[8,10,768]{2,1,0:T(8,128)} %bitcast.358), calls=%async_computation | async-start | bytes 786432 | tf_op jit(solution)/shard_map/all_to_all | solution.py:188
  24.4 226.7 %copy-start.6 = (f32[1536,128]{1,0:T(8,128)}, f32[1536,128]{1,0:T(8,128)S(1)}, u32[]{:S(2)}) copy-start(f32[1536,128]{1,0:T(8,128)S(1)} %maximum_select_fusion) | copy-start | bytes 2359300
  27.2 31.0 %collective-permute-start = (f32[8,128]{1,0:T(8,128)S(1)}, f32[8,128]{1,0:T(8,128)S(1)}, u32[]{:S(2)}, u32[]{:S(2)}) collective-permute-start(f32[8,128]{1,0:T(8,128)S(1)} %concatenate.154), channel_id=1, source_target_pairs={{0,1},{1,0},{2,3},{3,2},{4,5},{5,4},{6,7},{7,6},{8,9},{9,8},{10,11... | collective-permute-start | bytes 12296 | tf_op jit(solution)/shard_map/ppermute | solution.py:186
  31.9 101.4 %collective-permute-start.1 = (bf16[8,512,256]{2,1,0:T(8,128)(2,1)}, bf16[8,512,256]{2,1,0:T(8,128)(2,1)}, u32[]{:S(2)}, u32[]{:S(2)}) collective-permute-start(bf16[8,512,256]{2,1,0:T(8,128)(2,1)} %get-tuple-element.100), channel_id=1, source_target_pairs={{0,2},{1,3},{2,0},{3,1},{4,6},{5,7},{6,4},{7,5},{8,10},{9,11},{10,... | collective-permute-start | bytes 6291464 | tf_op jit(solution)/shard_map/ppermute | solution.py:186
  36.1 101.9 %collective-permute-start.3 = (bf16[8,256,512]{2,1,0:T(8,128)(2,1)}, bf16[8,256,512]{2,1,0:T(8,128)(2,1)}, u32[]{:S(2)}, u32[]{:S(2)}) collective-permute-start(bf16[8,256,512]{2,1,0:T(8,128)(2,1)} %get-tuple-element.102), channel_id=1, source_target_pairs={{0,2},{1,3},{2,0},{3,1},{4,6},{5,7},{6,4},{7,5},{8,10},{9,11},{10,... | collective-permute-start | bytes 6291464 | tf_op jit(solution)/shard_map/ppermute | solution.py:186
  59.0 47.8 %all-to-all-start.3 = ((f32[8,16,128]{2,1,0:T(8,128)}), f32[8,16,128]{2,1,0:T(8,128)S(1)}, u32[]{:S(2)}, u32[]{:S(2)}) async-start(f32[8,16,128]{2,1,0:T(8,128)} %broadcast_in_dim.156), calls=%async_computation.3 | async-start | bytes 131072 | tf_op jit(solution)/shard_map/all_to_all | solution.py:223
  106.8 51.3 %all-to-all-start.1 = ((bf16[8,160,768]{2,1,0:T(8,128)(2,1)}), bf16[8,160,768]{2,1,0:T(8,128)(2,1)}, u32[]{:S(2)}, u32[]{:S(2)}) async-start(bf16[8,160,768]{2,1,0:T(8,128)(2,1)} %lookup_rows.1), calls=%async_computation.1 | async-start | bytes 3932160 | tf_op jit(solution)/shard_map/all_to_all | solution.py:241
  129.4 118.4 %copy-start.53 = (bf16[640,512]{1,0:T(8,128)(2,1)}, bf16[640,512]{1,0:T(8,128)(2,1)S(1)}, u32[]{:S(2)}) copy-start(bf16[640,512]{1,0:T(8,128)(2,1)S(1)} %all_gather.6) | copy-start | bytes 1966084
  137.6 70.0 %collective-permute-start.2 = (bf16[2,6,512,256]{3,2,1,0:T(8,128)(2,1)}, bf16[2,6,512,256]{3,2,1,0:T(8,128)(2,1)}, u32[]{:S(2)}, u32[]{:S(2)}) collective-permute-start(bf16[2,6,512,256]{3,2,1,0:T(8,128)(2,1)} %pad_maximum_fusion.5), channel_id=1, source_target_pairs={{0,1},{1,0},{2,3},{3,2},{4,5},{5,4},{6,7},{7,6},{8,9},{9,8},{10,11... | collective-permute-start | bytes 9437192 | tf_op jit(solution)/shard_map/ppermute | solution.py:186
  144.2 83.0 %collective-permute-start.4 = (bf16[2,6,256,512]{3,2,1,0:T(8,128)(2,1)}, bf16[2,6,256,512]{3,2,1,0:T(8,128)(2,1)}, u32[]{:S(2)}, u32[]{:S(2)}) collective-permute-start(bf16[2,6,256,512]{3,2,1,0:T(8,128)(2,1)} %pad_maximum_fusion.4), channel_id=1, source_target_pairs={{0,1},{1,0},{2,3},{3,2},{4,5},{5,4},{6,7},{7,6},{8,9},{9,8},{10,11... | collective-permute-start | bytes 9437192 | tf_op jit(solution)/shard_map/ppermute | solution.py:186
  203.0 44.9 %all-to-all-start.2 = ((bf16[4,160,1536]{2,1,0:T(8,128)(2,1)}), bf16[4,160,1536]{2,1,0:T(8,128)(2,1)}, u32[]{:S(2)}, u32[]{:S(2)}) async-start(bf16[4,160,1536]{2,1,0:T(8,128)(2,1)} %reshape.575), calls=%async_computation.2 | async-start | bytes 3932160 | tf_op jit(solution)/shard_map/all_to_all | solution.py:253
  207.4 428.2 %reduce-scatter.5.cloned.1.call-start = ((), (), s32[]{:S(2)}) async-start(), calls=%async_computation.10 | async-start | bytes 9437184 | tf_op jit(solution)/shard_map/reduce_scatter | solution.py:375
  254.7 70.6 %copy-start.80 = (f32[1536]{0:T(1024)}, f32[1536]{0:T(1024)S(1)}, u32[]{:S(2)}) copy-start(f32[1536]{0:T(1024)S(1)} %get-tuple-element.40) | copy-start | bytes 18436
  254.7 70.6 %copy-start.82 = (f32[1536]{0:T(1024)}, f32[1536]{0:T(1024)S(1)}, u32[]{:S(2)}) copy-start(f32[1536]{0:T(1024)S(1)} %get-tuple-element.41) | copy-start | bytes 18436
  254.8 70.4 %copy-start.84 = (f32[1536]{0:T(1024)}, f32[1536]{0:T(1024)S(1)}, u32[]{:S(2)}) copy-start(f32[1536]{0:T(1024)S(1)} %get-tuple-element.38) | copy-start | bytes 18436
  254.8 70.4 %copy-start.86 = (f32[1536]{0:T(1024)}, f32[1536]{0:T(1024)S(1)}, u32[]{:S(2)}) copy-start(f32[1536]{0:T(1024)S(1)} %get-tuple-element.39) | copy-start | bytes 18436
  464.0 10.6 collective-permute-start.5
  486.6 255.5 %reduce-scatter.3.cloned.1.call-start = ((), (), s32[]{:S(2)}) async-start(), calls=%async_computation.8 | async-start | bytes 1638400 | tf_op jit(solution)/shard_map/reduce_scatter | solution.py:398
  509.5 146.1 %copy-start.50 = (bf16[1536,512]{1,0:T(8,128)(2,1)}, bf16[1536,512]{1,0:T(8,128)(2,1)S(1)}, u32[]{:S(2)}) copy-start(bf16[1536,512]{1,0:T(8,128)(2,1)S(1)} %get-tuple-element.139) | copy-start | bytes 4718596
  513.9 141.8 %copy-start.54 = (bf16[640,512]{1,0:T(8,128)(2,1)S(1)}, bf16[640,512]{1,0:T(8,128)(2,1)}, u32[]{:S(2)}) copy-start(bf16[640,512]{1,0:T(8,128)(2,1)} %copy-done.53) | copy-start | bytes 1966084
  513.9 305.4 %all-gather.2.cloned.1.call-start = ((), (), s32[]{:S(2)}) async-start(), calls=%async_computation.11 | async-start | bytes 8257536 | tf_op jit(solution)/shard_map/all_gather | solution.py:381
  636.6 13.8 %collective-permute-start.6 = (bf16[8,128,256]{2,1,0:T(8,128)(2,1)S(1)}, bf16[8,128,256]{2,1,0:T(8,128)(2,1)S(1)}, u32[]{:S(2)}, u32[]{:S(2)}) collective-permute-start(bf16[8,128,256]{2,1,0:T(8,128)(2,1)S(1)} %slice_bitcast_fusion.4), channel_id=1, source_target_pairs={{0,2},{1,3},{2,0},{3,1},{4,6},{5,7},{6,4},{7,5},{8,10},{9,11},{10,... | collective-permute-start | bytes 1572872 | tf_op jit(solution)/shard_map/ppermute | solution.py:186
  658.1 27.9 %all-to-all-start.4 = ((bf16[4,160,1536]{2,1,0:T(8,128)(2,1)}), bf16[4,160,1536]{2,1,0:T(8,128)(2,1)S(1)}, u32[]{:S(2)}, u32[]{:S(2)}) async-start(bf16[4,160,1536]{2,1,0:T(8,128)(2,1)} %bitcast.390), calls=%async_computation.4 | async-start | bytes 3932160 | tf_op jit(solution)/shard_map/all_to_all | solution.py:356
  717.9 96.4 %all-to-all-start.5 = ((bf16[8,160,768]{2,1,0:T(8,128)(2,1)}), bf16[8,160,768]{2,1,0:T(8,128)(2,1)}, u32[]{:S(2)}, u32[]{:S(2)}) async-start(bf16[8,160,768]{2,1,0:T(8,128)(2,1)} %copy.259), calls=%async_computation.5 | async-start | bytes 3932160 | tf_op jit(solution)/shard_map/all_to_all | solution.py:361
  722.3 202.8 %all-reduce.22.cloned.1.call-start = ((), (), s32[]{:S(2)}) async-start(), calls=%async_computation.12 | async-start | bytes 152576 | tf_op jit(solution)/shard_map/psum | solution.py:400
  730.6 337.0 %all-reduce.24.cloned.1.call-start = ((), (), s32[]{:S(2)}) async-start(), calls=%async_computation.13 | async-start | bytes 3866624 | tf_op jit(solution)/shard_map/psum | solution.py:400
  739.4 401.2 %all-reduce.20.cloned.1.call-start = ((), (), s32[]{:S(2)}) async-start(), calls=%async_computation.9 | async-start | bytes 655360 | tf_op jit(solution)/shard_map/psum | solution.py:399
  833.1 320.8 %copy-start.1 = (bf16[6,512,128]{2,1,0:T(8,128)(2,1)S(1)}, bf16[6,512,128]{2,1,0:T(8,128)(2,1)}, u32[]{:S(2)}) copy-start(bf16[6,512,128]{2,1,0:T(8,128)(2,1)} %param.32) | copy-start | bytes 2359300
  925.1 227.1 %copy-start.110 = (f32[6,128]{1,0:T(8,128)S(1)}, f32[6,128]{1,0:T(8,128)}, u32[]{:S(2)}) copy-start(f32[6,128]{1,0:T(8,128)} %get-tuple-element.159) | copy-start | bytes 9220
  925.1 227.7 %copy-start.109 = (f32[6,128]{1,0:T(8,128)S(1)}, f32[6,128]{1,0:T(8,128)}, u32[]{:S(2)}) copy-start(f32[6,128]{1,0:T(8,128)} %get-tuple-element.160) | copy-start | bytes 9220
  925.1 228.3 %copy-start.120 = (f32[6]{0:T(128)S(1)}, f32[6]{0:T(128)}, u32[]{:S(2)}) copy-start(f32[6]{0:T(128)} %get-tuple-element.161) | copy-start | bytes 76
  (117 other events, 933.5 us)
Sparse Core Ops, SparseCore 0:
  486.7 148.8 reduce-scatter.4
  638.8 25.5 reduce-scatter.2
  666.8 152.3 all-gather.1
Sparse Core Ops, SparseCore 1:
  730.6 194.4 all-reduce.21
  931.9 135.7 all-reduce.23
  1070.8 69.7 all-reduce.19

commit v2 on v1

v2 whole, which is shorter than its diff:
```python
import functools

import jax
import jax.numpy as jnp
from jax import lax
from jax.experimental import pallas as pl
from jax.experimental.pallas import tpu as pltpu
from jax.sharding import PartitionSpec as P

D = 512
HID = 1024
EMB = 16
DENSE = 128
DOMAINS = 6
SHARED = 2
DOM_EXP = 2
DSLOT = 1024
HALF = DSLOT // 2
VMEM = 56 * 2**20
BF = jnp.bfloat16
F32 = jnp.float32
MESH = pl.DeviceIdType.MESH
UNITS = 9
ROWS_U = 1024
LANES = 256
PROJ_ROWS = 320
REP_ROWS = 704


def dot(a, b, ca, cb):
    return lax.dot_general(a, b, (((ca,), (cb,)), ((), ())), preferred_element_type=F32)


def lookup_kernel(lo_n, hi_n, fields, idx_ref, tab_ref, out_ref):
    length = idx_ref.shape[-1]
    shift = hi_n.bit_length() - 1
    for f in range(fields):
        idx = idx_ref[0, f : f + 1, :]
        hi = jnp.where(idx >= 0, idx & (hi_n - 1), -1)
        lo = lax.shift_right_logical(jnp.maximum(idx, 0), shift)
        hot = (lax.broadcasted_iota(jnp.int32, (hi_n, length), 0) == hi).astype(BF)
        cols = slice(f * EMB, (f + 1) * EMB)
        parts = [
            tab_ref[:, cols, j * hi_n : (j + 1) * hi_n].reshape(-1, hi_n) for j in range(tab_ref.shape[2] // hi_n)
        ]
        res = jnp.dot(jnp.concatenate(parts, axis=0), hot, preferred_element_type=F32)
        acc = res[0:EMB]
        for step in range(1, lo_n):
            acc = jnp.where(lo == step, res[step * EMB : (step + 1) * EMB], acc)
        out_ref[0, cols, :] = acc.astype(BF)


def lookup(idx, tab, hi_n, name, out_groups, order=lambda i: i):
    groups, fields, length = idx.shape
    outer, cols, inner = tab.shape
    lo_n = outer * inner // hi_n
    each = groups // out_groups
    return pl.pallas_call(
        functools.partial(lookup_kernel, lo_n, hi_n, fields),
        grid=(groups,),
        in_specs=[
            pl.BlockSpec((1, fields, length), lambda i: (order(i), 0, 0)),
            pl.BlockSpec(tab.shape, lambda i: (0, 0, 0)),
        ],
        out_specs=pl.BlockSpec((1, cols, length), lambda i: (i // each, 0, i % each)),
        out_shape=jax.ShapeDtypeStruct((out_groups, cols, length * each), BF),
        compiler_params=pltpu.CompilerParams(vmem_limit_bytes=VMEM),
        cost_estimate=pl.CostEstimate(
            flops=2 * groups * length * cols * lo_n * hi_n, bytes_accessed=8 * 2**20, transcendentals=0
        ),
        name=name,
    )(idx, tab)


def place_one(idx_ref, grad_ref, out_ref, field):
    outer, _, inner = out_ref.shape
    length = grad_ref.shape[2]
    hi_n = 256
    lo_n = outer * inner // hi_n
    cols = pl.ds(pl.multiple_of(field * EMB, EMB), EMB)
    total = None
    for s in range(grad_ref.shape[0]):
        idx = idx_ref[field, :, s * length : (s + 1) * length]
        hi = idx & (hi_n - 1)
        lo = lax.shift_right_logical(idx, hi_n.bit_length() - 1)
        grad = grad_ref[s, cols, :]
        hot = (lax.broadcasted_iota(jnp.int32, (hi_n, length), 0) == hi).astype(BF)
        lhs = jnp.concatenate(
            [jnp.where(lo == step, grad, jnp.zeros_like(grad)) for step in range(lo_n)], axis=0
        )
        part = dot(lhs, hot, 1, 1)
        total = part if total is None else total + part
    for j in range(inner // hi_n):
        piece = total[j * outer * EMB : (j + 1) * outer * EMB]
        out_ref[:, cols, j * hi_n : (j + 1) * hi_n] = piece.reshape(outer, EMB, hi_n).astype(BF)


def place_kernel(idx_ref, grad_ref, out_ref):
    place_one(idx_ref, grad_ref, out_ref, 0)


def place(idx, grad, hi_n, out_shape):
    fields, _, length = idx.shape
    parts, cols, each = grad.shape
    outer, _, inner = out_shape
    lo_n = outer * inner // hi_n
    return pl.pallas_call(
        place_kernel,
        grid=(fields,),
        in_specs=[
            pl.BlockSpec((1, 1, length), lambda i: (i, 0, 0)),
            pl.BlockSpec((parts, EMB, each), lambda i: (0, i, 0)),
        ],
        out_specs=pl.BlockSpec((outer, EMB, inner), lambda i: (0, i, 0)),
        out_shape=jax.ShapeDtypeStruct(out_shape, BF),
        compiler_params=pltpu.CompilerParams(vmem_limit_bytes=VMEM),
        cost_estimate=pl.CostEstimate(
            flops=2 * cols * length * lo_n * hi_n, bytes_accessed=6 * 2**20, transcendentals=0
        ),
        name="place_rows",
    )(idx, grad)


def reduce_kernel(bits, with_rows, own_ref, extra_ref, *refs):
    if with_rows:
        slot_ref, grad_ref, out_ref, rep_ref, back_ref = refs[:5]
        grads, placed, near_send, near_recv, far_send, far_recv, keep_sem = refs[-7:]
        refs = refs[5:-7]
    else:
        out_ref, rep_ref = refs[:2]
        refs = refs[2:]
    acc, stage_buf, halves, got, local_sem, send, recv, rep_send, rep_recv, out_sem = refs
    wide=lax.axis_index("wide"); me=lax.axis_index("narrow")
    chip=me//2; core=me%2
    block=ROWS_U>>bits
    mates=[{"narrow": me+1-2*core},{"narrow": me+2-4*chip}]
    pairs=[{"wide": wide+(1<<k)*(1-2*((wide//(1<<k))%2))} for k in range(bits)]
    far={"narrow": 3-me}
    barrier=pltpu.get_barrier_semaphore()
    owners=1<<bits
    others=[{"wide": (wide+d)%owners} for d in range(1,owners)] if with_rows else pairs
    for mate in mates+[far]+others:
        pl.semaphore_signal(barrier, inc=1, device_id=mate, device_id_type=MESH)
    pl.semaphore_wait(barrier, len(others)+3)
    def bit(k): return (wide//(1<<k))%2
    def start_of(k):
        at=0
        for j in range(k):
            at=at+bit(j)*(ROWS_U>>(j+1))
        return pl.multiple_of(at, 16) if k else 0
    stages=2*bits+2
    def copy(src,dst,s,u,mate):
        return pltpu.make_async_remote_copy(src_ref=src,dst_ref=dst,send_sem=send.at[s,u],recv_sem=recv.at[s,u],device_id=mate,device_id_type=MESH)
    def mine(u): return jnp.logical_or(jnp.logical_or(u<3,u>=7), jnp.logical_and(u<5,core==0)|jnp.logical_and(u>=5,core==1))
    def theirs(u): return jnp.logical_or(jnp.logical_or(u<3,u>=7), jnp.logical_and(u<5,core==1)|jnp.logical_and(u>=5,core==0))
    def local_at(u):
        return jnp.where(u<3,u-1,jnp.where(u<5,u-1,u-3))
    def core_copy(u, src):
        return copy(src, acc.at[u], 0, u, mates[0])
    def near_copy(u, src):
        return pltpu.make_async_copy(src, stage_buf.at[u%2], local_sem.at[u%2])
    def begin(u):
        @pl.when(u==0)
        def _():
            core_copy(u, extra_ref.at[pl.ds(2,2)]).start()
            near_copy(u, extra_ref.at[pl.ds(0,2)]).start()
        @pl.when(jnp.logical_and(u>0, mine(u)))
        def _():
            core_copy(u, own_ref.at[local_at(u), pl.ds(2,2)]).start()
            near_copy(u, own_ref.at[local_at(u), pl.ds(0,2)]).start()
    def add_region(u, sl, at, rows, src):
        tile=min(rows,64)
        def body(i,_):
            r=pl.multiple_of(at+i*tile,16); q=pl.multiple_of(i*tile,16)
            for h in sl:
                a=acc[u,h,pl.ds(r,tile),:].astype(F32)+src[h,pl.ds(q,tile),:].astype(F32)
                acc[u,h,pl.ds(r,tile),:]=a.astype(BF)
            return 0
        lax.fori_loop(0,rows//tile,body,0)
    half_at=[0]
    for k in range(bits): half_at.append(half_at[-1]+(ROWS_U>>(k+1)))
    def half_view(u,k):
        return halves.at[u,:,pl.ds(half_at[k],ROWS_U>>(k+1)),:]
    def send_half(u,k):
        size=ROWS_U>>(k+1)
        at=pl.multiple_of(start_of(k)+(1-bit(k))*size,16)
        return copy(acc.at[u,:,pl.ds(at,size),:], half_view(u,k), 1+k, u, pairs[k])
    def combine(u):
        @pl.when(theirs(u))
        def _():
            core_copy(u, acc.at[u]).wait_recv()
        @pl.when(mine(u))
        def _():
            near_copy(u, acc.at[u]).wait()
            sb=stage_buf.at[u%2]
            @pl.when(theirs(u))
            def _():
                add_region(u,(0,1),0,ROWS_U,sb)
            @pl.when(jnp.logical_not(theirs(u)))
            def _():
                def body(i,_):
                    r=pl.multiple_of(i*64,16)
                    for h in (0,1): acc[u,h,pl.ds(r,64),:]=sb[h,pl.ds(r,64),:]
                    return 0
                lax.fori_loop(0,ROWS_U//64,body,0)
        send_half(u,0).start()
    def halve(u,k):
        size=ROWS_U>>k
        copy(acc.at[u,:,pl.ds(0,size),:], half_view(u,k-1), k, u, pairs[k-1]).wait_recv()
        add_region(u,(0,1),start_of(k),size,halves.at[u,:,pl.ds(half_at[k-1],size),:])
        if k<bits:
            send_half(u,k).start()
        else:
            y_copy(u).start()
    def y_copy(u):
        at=start_of(bits)
        return copy(acc.at[u,1,pl.ds(at,block),:], got.at[u,1,pl.ds(at,block),:], bits+1, u, mates[1])
    def grow_copy(u,j,parts):
        size=ROWS_U>>(j+1)
        at=start_of(j+1)
        view=got.at[u,pl.ds(0,parts),pl.ds(at,size),:]
        return copy(view,view,bits+2+(bits-1-j),u,pairs[j])
    def each_kind(u,f):
        @pl.when(u<3)
        def _(): f(1)
        @pl.when(u>=3)
        def _(): f(2)
    def cross(u):
        y_copy(u).wait_recv()
        at=start_of(bits)
        @pl.when(u<3)
        def _():
            a=acc[u,0,pl.ds(at,block),:].astype(F32)+got[u,1,pl.ds(at,block),:].astype(F32)
            got[u,0,pl.ds(at,block),:]=a.astype(BF)
        @pl.when(u>=3)
        def _():
            got[u,0,pl.ds(at,block),:]=acc[u,0,pl.ds(at,block),:]
        each_kind(u,lambda parts: grow_copy(u,bits-1,parts).start())
    def out_copy(u,parts):
        return pltpu.make_async_copy(got.at[u,pl.ds(0,parts)], out_ref.at[u,pl.ds(0,parts)], out_sem.at[u])
    rep_mates=[mates[0],mates[1],far]
    rep_rows=rep_ref.shape[1]
    def rep_copy(i):
        return pltpu.make_async_remote_copy(src_ref=got.at[0,0,pl.ds(ROWS_U-rep_rows,rep_rows),:],dst_ref=rep_ref.at[i],send_sem=rep_send.at[i],recv_sem=rep_recv.at[i],device_id=rep_mates[i],device_id_type=MESH)
    def grow(u,j):
        each_kind(u,lambda parts: grow_copy(u,j,parts).wait_recv())
        if j>0:
            each_kind(u,lambda parts: grow_copy(u,j-1,parts).start())
        else:
            each_kind(u,lambda parts: out_copy(u,parts).start())
            @pl.when(u==0)
            def _():
                for i in range(3): rep_copy(i).start()
    quarters=mates+[far]
    def quarter_at(i):
        return [me+1-2*core, me+2-4*chip, 3-me][i]
    def near_row_copy(i):
        return pltpu.make_async_remote_copy(src_ref=grad_ref.at[quarter_at(i)],dst_ref=grads.at[me],send_sem=near_send.at[i],recv_sem=near_recv.at[i],device_id=quarters[i],device_id_type=MESH)
    def keep_copy():
        return pltpu.make_async_copy(grad_ref.at[me],grads.at[me],keep_sem.at[0])
    def back_copy(d):
        return pltpu.make_async_remote_copy(src_ref=placed.at[(wide+d)%owners],dst_ref=back_ref.at[wide],send_sem=far_send.at[d],recv_sem=far_recv.at[d],device_id=others[d-1],device_id_type=MESH)
    def keep_back():
        return pltpu.make_async_copy(placed.at[wide],back_ref.at[wide],keep_sem.at[1])
    def place_field(f, _):
        place_one(slot_ref, grads, placed, f)
        return 0
    def row_step(t):
        fields=slot_ref.shape[0]
        @pl.when(t==2)
        def _():
            keep_copy().wait()
            for i in range(3): near_row_copy(i).wait_recv()
        @pl.when(jnp.logical_and(t>=2,t<7))
        def _():
            lax.fori_loop((t-2)*(fields//5),(t-1)*(fields//5),place_field,0)
        @pl.when(t==6)
        def _():
            keep_back().start()
            for d in range(1,owners): back_copy(d).start()
    todo=[begin,combine]+[functools.partial(lambda k,u: halve(u,k),k) for k in range(1,bits+1)]+[cross]+[functools.partial(lambda j,u: grow(u,j),j) for j in reversed(range(bits))]
    def tick(t,_):
        for s in reversed(range(len(todo))):
            u=t-s
            @pl.when(jnp.logical_and(u>=0,u<UNITS))
            def _():
                todo[s](u)
        if with_rows:
            row_step(t)
        return 0
    if with_rows:
        keep_copy().start()
        for i in range(3): near_row_copy(i).start()
    lax.fori_loop(0,UNITS+len(todo)-1,tick,0)
    if with_rows:
        keep_back().wait()
        for i in range(3): near_row_copy(i).wait_send()
        for d in range(1,owners): back_copy(d).wait()
    def finish(u,_):
        @pl.when(mine(u))
        def _():
            core_copy(u, acc.at[u]).wait_send()
        for k in range(bits): send_half(u,k).wait_send()
        y_copy(u).wait_send()
        for j in range(bits): each_kind(u,lambda parts: grow_copy(u,j,parts).wait_send())
        each_kind(u,lambda parts: out_copy(u,parts).wait())
        return 0
    lax.fori_loop(0,UNITS,finish,0)
    for i in range(3):
        rep_copy(i).wait()

def reduce_all(own, extra, wide, rep_rows, rows=None):
    bits = wide.bit_length() - 1
    args = [own, extra]
    any_space = pl.BlockSpec(memory_space=pl.ANY)
    in_specs = [any_space] * 2
    out_shape = [
        jax.ShapeDtypeStruct((UNITS, 2, ROWS_U, LANES), BF),
        jax.ShapeDtypeStruct((3, rep_rows, LANES), BF),
    ]
    scratch = [
        pltpu.VMEM((UNITS, 2, ROWS_U, LANES), BF),
        pltpu.VMEM((2, 2, ROWS_U, LANES), BF),
        pltpu.VMEM((UNITS, 2, ROWS_U, LANES), BF),
        pltpu.VMEM((UNITS, 2, ROWS_U, LANES), BF),
        pltpu.SemaphoreType.DMA((2,)),
        pltpu.SemaphoreType.DMA((2 * bits + 2, UNITS)),
        pltpu.SemaphoreType.DMA((2 * bits + 2, UNITS)),
        pltpu.SemaphoreType.DMA((3,)),
        pltpu.SemaphoreType.DMA((3,)),
        pltpu.SemaphoreType.DMA((UNITS,)),
    ]
    if rows is not None:
        slots, grads, cap = rows
        args += [slots, grads]
        in_specs += [pl.BlockSpec(memory_space=pltpu.VMEM), any_space]
        back = (wide, grads.shape[1], cap)
        out_shape.append(jax.ShapeDtypeStruct(back, BF))
        scratch += [
            pltpu.VMEM(grads.shape, BF),
            pltpu.VMEM(back, BF),
            pltpu.SemaphoreType.DMA((3,)),
            pltpu.SemaphoreType.DMA((3,)),
            pltpu.SemaphoreType.DMA((wide,)),
            pltpu.SemaphoreType.DMA((wide,)),
            pltpu.SemaphoreType.DMA((2,)),
        ]
    return pl.pallas_call(
        functools.partial(reduce_kernel, bits, rows is not None),
        in_specs=in_specs,
        out_specs=[any_space] * len(out_shape),
        out_shape=out_shape,
        scratch_shapes=scratch,
        compiler_params=pltpu.CompilerParams(collective_id=0, has_side_effects=True, vmem_limit_bytes=VMEM),
        cost_estimate=pl.CostEstimate(flops=0, bytes_accessed=60 * 2**20, transcendentals=0),
        name="reduce_all",
    )(*args)


C0 = 0.7978845608028654
C1 = 0.044715


def gelu_both(x):
    square = x * x
    t = jnp.tanh(C0 * x * (1.0 + C1 * square))
    up = 0.5 * (1.0 + t)
    slope = up + 0.5 * x * (1.0 - t * t) * (C0 + (3.0 * C0 * C1) * square)
    return x * up, slope


def soft_pair(a, b):
    top = jnp.maximum(a, b)
    ea, eb = jnp.exp(a - top), jnp.exp(b - top)
    total = ea + eb
    return ea / total, eb / total


def soft_pair_back(pa, pb, ga, gb):
    mean = pa * ga + pb * gb
    return pa * (ga - mean), pb * (gb - mean)


def fold(x):
    return sum(x[:, i * 128 : (i + 1) * 128] for i in range(x.shape[1] // 128))


def wide_lanes(x, n):
    return jnp.concatenate([x] * n, axis=1)


def dense_kernel(
    ids_ref, emb_ref, feat_ref, projw_ref, featw_ref, up_a, up_b, up_c, down_a, down_b, down_c, gain_ref, shift_ref, gate_ref, tin_ref,
    tbias_ref, tout_ref, tob_ref, label_ref, live_ref,
    logit_ref, own_ref, emb_grad_ref, proj_grad_ref, feat_grad_ref, gain_acc, shift_acc, gate_acc, tin_acc,
    tbias_acc, tout_acc, tob_acc,
    xt, act, slope, outs, og, ing, hid, hg, stat, coef, inner, emb, emb_sem,
):
    ups = [up_a.at[0], up_b.at[0], up_c.at[0, 0], up_c.at[1, 0]]
    downs = [down_a.at[0], down_b.at[0], down_c.at[0, 0], down_c.at[1, 0]]
    step = pl.program_id(0)
    chunk, slot = step // 4, step % 4
    rows = xt.shape[1]

    @pl.when(step == 0)
    def _():
        fetch = pltpu.make_async_copy(emb_ref, emb, emb_sem)
        fetch.start()
        fetch.wait()
        for c in range(rows // HALF):
            cols = slice(c * HALF, (c + 1) * HALF)
            x = dot(projw_ref[...], emb[:, cols], 0, 0) + dot(featw_ref[...], feat_ref[:, cols], 0, 0)
            xt[:, cols] = x.astype(BF)
        for ref in (gain_acc, shift_acc, gate_acc, tin_acc, tbias_acc, tout_acc, tob_acc):
            ref[...] = jnp.zeros_like(ref)

    @pl.when(step < 12)
    def _():
        lanes = pl.ds(pl.multiple_of(chunk * HALF, HALF), HALF)

        def piece(s, total):
            pre = dot(ups[s][...], xt[:, lanes], 0, 0)
            a, g = gelu_both(pre)
            a = a.astype(BF)
            act[slot, s, :, lanes] = a
            slope[slot, s, :, lanes] = g.astype(BF)
            return dot(downs[s][...], a, 0, 0)

        outs[slot] = piece(0, None)
        for s in range(1, 4):
            outs[slot] += piece(s, None)

    def middle():
        lanes = pl.ds(pl.multiple_of(chunk * HALF, HALF), HALF)
        dom = chunk // 2
        x = xt[:, lanes]
        gates = dot(gate_ref[dom], x, 1, 0)
        s0, s1 = soft_pair(gates[0:1], gates[1:2])
        d0, d1 = soft_pair(gates[2:3], gates[3:4])
        t0, t1 = soft_pair(gates[4:5], gates[5:6])
        for k, row in enumerate((t0 * s0, t0 * s1, t1 * d0, t1 * d1)):
            coef[k : k + 1, :] = row
        expert = [0, 1, 2 + 2 * dom, 3 + 2 * dom]

        def normalize(t, _):
            cols = pl.ds(pl.multiple_of(t * 128, 128), 128)
            for k in range(4):
                v = outs[k, :, cols]
                mean = jnp.sum(v, axis=0, keepdims=True) * (1.0 / D)
                v = v - mean
                var = jnp.sum(v * v, axis=0, keepdims=True) * (1.0 / D)
                stat[k : k + 1, cols] = mean
                stat[4 + k : 5 + k, cols] = lax.rsqrt(var + 1e-05)
            for r in range(4):
                band = slice(r * 128, (r + 1) * 128)
                acc = None
                for k in range(4):
                    n = (outs[k, band, cols] - stat[k : k + 1, cols]) * stat[4 + k : 5 + k, cols]
                    n = (n * gain_ref[expert[k], band, :].astype(F32) + shift_ref[expert[k], band, :].astype(F32)) * coef[k : k + 1, cols]
                    acc = n if acc is None else acc + n
                hid[band, cols] = acc.astype(BF)
            return 0

        lax.fori_loop(0, 4, normalize, 0)
        h = hid[...]
        pre = dot(tin_ref[dom], h, 0, 0) + wide_lanes(tbias_ref[dom], 4)
        tact, tslope = gelu_both(pre)
        tout = wide_lanes(tout_ref[dom], 4)
        logit = jnp.sum(tact * tout, axis=0, keepdims=True) + wide_lanes(tob_ref[dom, 0:1, :], 4)
        logit_ref[:, lanes] = logit
        grad = (jax.nn.sigmoid(logit) - label_ref[:, lanes]) * live_ref[:, lanes]
        tob_acc[dom, 0:1, :] += fold(grad)
        tout_acc[dom] += fold(grad * tact)
        low = (grad * tout * tslope).astype(BF)
        tbias_acc[dom] += fold(low.astype(F32))
        tin_acc[dom] += dot(h, low, 1, 1)
        hg[...] = dot(tin_ref[dom], low, 1, 0)

        def denormalize(t, _):
            cols = pl.ds(pl.multiple_of(t * 128, 128), 128)
            place = pl.ds(pl.multiple_of(chunk * HALF + t * 128, 128), 128)
            for k in range(4):
                mean, rstd = stat[k : k + 1, cols], stat[4 + k : 5 + k, cols]
                c = coef[k : k + 1, cols]
                m1 = m2 = mb = 0.0
                for r in range(4):
                    band = slice(r * 128, (r + 1) * 128)
                    n = (outs[k, band, cols] - mean) * rstd
                    grad = hg[band, cols]
                    scaled = grad * gain_ref[expert[k], band, :].astype(F32)
                    m1 = m1 + jnp.sum(scaled, axis=0, keepdims=True)
                    m2 = m2 + jnp.sum(scaled * n, axis=0, keepdims=True)
                    mb = mb + jnp.sum(grad * shift_ref[expert[k], band, :].astype(F32), axis=0, keepdims=True)
                    part = c * grad
                    gain_acc[expert[k], band, :] += part * n
                    shift_acc[expert[k], band, :] += part
                inner[k : k + 1, cols] = m2 + mb
                m1, m2, cr = m1 * (1.0 / D), m2 * (1.0 / D), c * rstd
                for r in range(4):
                    band = slice(r * 128, (r + 1) * 128)
                    n = (outs[k, band, cols] - mean) * rstd
                    scaled = hg[band, cols] * gain_ref[expert[k], band, :].astype(F32)
                    og[k, band, place] = (cr * (scaled - m1 - n * m2)).astype(BF)
            return 0

        lax.fori_loop(0, 4, denormalize, 0)
        a = [inner[k : k + 1, :] for k in range(4)]
        g0, g1 = soft_pair_back(s0, s1, t0 * a[0], t0 * a[1])
        g2, g3 = soft_pair_back(d0, d1, t1 * a[2], t1 * a[3])
        g4, g5 = soft_pair_back(t0, t1, s0 * a[0] + s1 * a[1], d0 * a[2] + d1 * a[3])
        zero = jnp.zeros_like(g0)
        g = jnp.concatenate([g0, g1, g2, g3, g4, g5, zero, zero], axis=0)
        high = g.astype(BF).astype(F32)
        g = jnp.concatenate([high, g - high], axis=0).astype(BF)
        gate_acc[dom] += dot(g, x, 1, 1)
        ing[:, lanes] = dot(gate_ref[dom], g, 0, 0)

    @pl.when(jnp.logical_and(step < 12, slot == 3))
    def _():
        middle()

    def back(k, at, n):
        lanes = slice(at, at + n)

        for s in range(4):
            p = dot(downs[s][...], og[k, :, lanes], 1, 0) * slope[k, s, :, lanes].astype(F32)
            slope[k, s, :, lanes] = p.astype(BF)

        def piece(s, _):
            grad, p = og[k, :, lanes], slope[k, s, :, lanes]
            own_ref[0, s, 0:D, :] = dot(xt[:, lanes], p, 1, 1).astype(BF)
            d = dot(act[k, s, :, lanes], grad, 1, 1).astype(BF)
            own_ref[0, s, D : D + 256, :] = d[:, 0:256]
            own_ref[0, s, D + 256 : D + 512, :] = d[:, 256:512]
            return 0

        lax.fori_loop(0, 4, piece, 0)

        def grow(t, _):
            cols = pl.ds(pl.multiple_of(at + t * HALF, HALF), HALF)
            total = dot(ups[0][...], slope[k, 0, :, cols], 1, 0)
            for s in range(1, 4):
                total += dot(ups[s][...], slope[k, s, :, cols], 1, 0)
            ing[:, cols] += total
            return 0

        lax.fori_loop(0, n // HALF, grow, 0)

    expert = step - 12

    @pl.when(jnp.logical_and(expert >= 0, expert < 2))
    def _():
        back(expert, 0, rows)

    @pl.when(jnp.logical_and(expert >= 2, expert < 4))
    def _():
        back(expert, 0, DSLOT)

    @pl.when(expert >= 4)
    def _():
        back(expert - 2, DSLOT, rows - DSLOT)

    @pl.when(expert == 5)
    def _():
        low = ing[...].astype(BF)
        proj_grad_ref[...] = dot(emb[...], low, 1, 1).astype(BF)
        feat_grad_ref[...] = dot(feat_ref[...], low, 1, 1)
        for c in range(rows // HALF):
            cols = slice(c * HALF, (c + 1) * HALF)
            emb[:, cols] = dot(projw_ref[...], low[:, cols], 1, 0).astype(BF)
        put = pltpu.make_async_copy(emb, emb_grad_ref, emb_sem)
        put.start()
        put.wait()


def dense(ids, emb, feat, projw, featw, ups, downs, gains, shifts, gate, tin, tbias, tout, tob, label, live):
    rows = emb.shape[1]

    def ahead(i):
        c, j = i // 4, i % 4
        front = jnp.where(j < 2, j, jnp.where(c < 2, j, j + 2))
        return jnp.where(i < 12, front, i - 12)

    def whole(x):
        return pl.BlockSpec(x.shape, lambda i, ids: (0,) * len(x.shape), pipeline_mode=pl.Buffered(1))

    def shape(s, d):
        return jax.ShapeDtypeStruct(s, d)

    outs = [
        shape((1, rows), F32),
        shape((6, 4, 2 * D, 256), BF),
        shape(emb.shape, BF),
        shape(projw.shape, BF),
        shape(featw.shape, F32),
        shape(gains.shape, F32),
        shape(gains.shape, F32),
        shape(gate.shape, F32),
        shape(tin.shape, F32),
        shape(tbias.shape, F32),
        shape(tout.shape, F32),
        shape(tob.shape, F32),
    ]
    args = (emb, feat, projw, featw) + ups + downs + (gains, shifts, gate, tin, tbias, tout, tob, label, live)
    in_specs = [whole(x) for x in args]
    in_specs[0] = pl.BlockSpec(memory_space=pl.ANY)
    for at, group in ((4, ups), (7, downs)):
        block = group[0].shape[1:]
        in_specs[at] = pl.BlockSpec((1,) + block, lambda i, ids: (ids[ahead(i)], 0, 0))
        in_specs[at + 1] = pl.BlockSpec((1,) + block, lambda i, ids: (ids[6 + ahead(i)], 0, 0))
        in_specs[at + 2] = pl.BlockSpec((2, 1) + block, lambda i, ids: (0, ahead(i), 0, 0))
    out_specs = [whole(x) for x in outs]
    out_specs[2] = pl.BlockSpec(memory_space=pl.ANY)
    out_specs[1] = pl.BlockSpec((1, 4, 2 * D, 256), lambda i, ids: (jnp.maximum(i - 12, 0), 0, 0, 0))
    return pl.pallas_call(
        dense_kernel,
        grid_spec=pltpu.PrefetchScalarGridSpec(
            num_scalar_prefetch=1,
            grid=(18,),
            in_specs=in_specs,
            out_specs=out_specs,
            scratch_shapes=[
            pltpu.VMEM((D, rows), BF),
            pltpu.VMEM((4, 4, 256, rows), BF),
            pltpu.VMEM((4, 4, 256, rows), BF),
            pltpu.VMEM((4, D, HALF), F32),
            pltpu.VMEM((4, D, rows), BF),
            pltpu.VMEM((D, rows), F32),
            pltpu.VMEM((D, HALF), BF),
            pltpu.VMEM((D, HALF), F32),
            pltpu.VMEM((8, HALF), F32),
            pltpu.VMEM((8, HALF), F32),
            pltpu.VMEM((8, HALF), F32),
            pltpu.VMEM(emb.shape, BF),
            pltpu.SemaphoreType.DMA,
                    ]),
        out_shape=outs,
        compiler_params=pltpu.CompilerParams(vmem_limit_bytes=62 * 2**20),
        cost_estimate=pl.CostEstimate(flops=39 * 10**9, bytes_accessed=60 * 2**20, transcendentals=0),
        name="dense_all",
    )(ids, *args)


def own_stats(rows, weight):
    count = jnp.sum(weight)
    mean = jnp.sum(rows * weight, axis=1) / jnp.maximum(count, 1.0)
    off = rows - mean[:, None]
    return [mean, jnp.sum(off * off * weight, axis=1), jnp.broadcast_to(count, mean.shape)]


def pool(means, squares, counts):
    total = jnp.sum(counts, axis=0)
    mean = jnp.sum(counts * means, axis=0) / total
    off = means - mean
    return mean, (jnp.sum(squares, axis=0) + jnp.sum(counts * off * off, axis=0)) / total


def shards(
    embed_table,
    requests,
    slot_index,
    event_mask,
    labels,
    dense_feats,
    proj_weight,
    dense_weight,
    proj_bias,
    up_weight,
    down_weight,
    norm_gain,
    norm_shift,
    gate_weight,
    tower_in,
    tower_bias,
    tower_out,
    tower_out_bias,
):
    narrow = lax.axis_size("narrow")
    me = lax.axis_index("narrow")
    chip, core = me // 2, me % 2
    ev_rows, fields = slot_index.shape
    rows = ev_rows // narrow
    owners, cap = requests.shape[1], requests.shape[2]
    hid_here = up_weight.shape[2]
    other_chip = [(i, i ^ 2) for i in range(narrow)]
    other_core = [(i, i ^ 1) for i in range(narrow)]
    full = 3 * chip + 2 * core
    half = 3 * chip + 1

    def swap(x, pairs):
        return lax.ppermute(x, "narrow", pairs)

    asked = lax.all_to_all(requests[0].transpose(0, 2, 1), "wide", 0, 0, tiled=True)

    def chip_experts(w, which):
        return jnp.concatenate(
            [w[:SHARED], lax.dynamic_slice_in_dim(w, SHARED + 6 * which, 6, axis=0)], axis=0
        )

    def bring(w):
        far = swap(chip_experts(w, 1 - chip), other_chip)
        at = lambda x, start, size: lax.dynamic_slice_in_dim(x, start, size, axis=0)
        base = SHARED + 6 * chip
        away = 4 * (1 - core)
        theirs = jnp.stack(
            [
                jnp.concatenate([w[:SHARED], at(w, base + away, 2), at(w, base + 2, 2)], axis=0),
                jnp.concatenate([far[:SHARED], at(far, 2 + away, 2), far[4:6]], axis=0),
            ]
        )
        return w, far, swap(theirs, other_core)

    ups = bring(up_weight)
    downs = bring(down_weight)
    six = jnp.arange(6, dtype=jnp.int32)
    spot = jnp.where(six < 2, six, jnp.where(six < 4, six + 4 * core, six))
    ids = jnp.concatenate([jnp.where(six < 2, six, spot + 6 * chip), spot])

    def by_offset(x):
        x = x.reshape((2, 2) + x.shape[1:])
        x = jnp.where(chip == 1, x[::-1], x)
        x = jnp.where(core == 1, x[:, ::-1], x)
        return x.reshape((narrow,) + x.shape[2:])

    column = jnp.stack([proj_weight, swap(proj_weight, other_chip)])
    column = jnp.stack([column, swap(column, other_core)], axis=1)
    proj_full = by_offset(column.reshape((narrow,) + proj_weight.shape)).reshape(-1, D)

    def turned(x):
        return jnp.where(core == 1, jnp.roll(x, -HALF, axis=0), x)

    live = turned(event_mask).astype(F32)[None]
    label_rows = turned(labels).astype(F32)[None]
    feats = turned(dense_feats).T
    blank = jnp.zeros((2, DENSE), F32)
    stats = jnp.stack(
        own_stats(feats[:, :DSLOT], live[:, :DSLOT]) + own_stats(feats[:, DSLOT:], live[:, DSLOT:])
    )
    stats = jnp.concatenate([stats, blank], axis=0)
    stats = jnp.concatenate([stats, swap(stats, other_core)], axis=0)
    every = lax.all_to_all(
        jnp.broadcast_to(stats, (owners,) + stats.shape), "wide", 0, 0, tiled=True
    )
    full_mean, full_spread = pool(every[:, 0], every[:, 1], every[:, 2])
    both = jnp.concatenate([every[:, 3:6], every[:, 11:14]], axis=0)
    half_mean, half_spread = pool(both[:, 0], both[:, 1], both[:, 2])
    normal = lambda x, mean, spread: (x - mean[:, None]) * lax.rsqrt(spread + 1e-05)[:, None]
    feat = jnp.concatenate(
        [
            jnp.concatenate(
                [normal(feats[:, :DSLOT], full_mean, full_spread), normal(feats[:, DSLOT:], half_mean, half_spread)],
                axis=1,
            ),
            jnp.ones((1, rows), F32),
            jnp.zeros((15, rows), F32),
        ],
        axis=0,
    ).astype(BF)
    feat_weight = jnp.concatenate([dense_weight, proj_bias[None], jnp.zeros((15, D), BF)], axis=0)

    table_rows = embed_table.shape[0]
    cols = fields * EMB
    direct = cap % 256 == 0
    tab = embed_table.reshape(32, table_rows // 32, cols).transpose(0, 2, 1)
    hi_n = table_rows // 32
    if direct:
        found = lookup(asked, tab, hi_n, "lookup_rows", owners)
    else:
        flat = asked.transpose(1, 0, 2).reshape(fields, DOMAINS, DSLOT).transpose(1, 0, 2)
        found = lookup(flat, tab, hi_n, "lookup_rows", DOMAINS)
        found = found.transpose(1, 0, 2).reshape(cols, owners, cap).transpose(1, 0, 2)
    received = lax.all_to_all(found, "wide", 0, 0, tiled=True)

    hi_n = 256
    lo_n = ev_rows // hi_n
    blocks = ev_rows // HALF
    slots = slot_index
    if direct:
        owner, rest = slots // cap, slots % cap
        slots = ((rest // hi_n) * owners + owner) * hi_n + rest % hi_n
    else:
        received = received.transpose(1, 0, 2).reshape(cols, lo_n, hi_n).transpose(1, 0, 2)
    slots = slots.reshape(blocks, HALF, fields).transpose(0, 2, 1)
    turn = lambda i: (i // 3) * 3 + (i % 3 + (i // 3) % 2) % 3
    embedded = lookup(slots, received, hi_n, "order_rows", narrow, turn)
    embedded = lax.all_to_all(embedded, "narrow", 0, 0, tiled=True)
    embedded = embedded.reshape(narrow * cols, rows)

    def pick(w):
        return jnp.stack(
            [
                lax.dynamic_index_in_dim(w, full, keepdims=False),
                lax.dynamic_index_in_dim(w, half, keepdims=False),
            ]
        )

    def over_lanes(x):
        return jnp.broadcast_to(x.astype(F32)[..., None], x.shape + (128,))

    def expert_rows(w):
        own = pick(w[SHARED:].reshape(DOMAINS, DOM_EXP, D)).reshape(4, D)
        w = jnp.concatenate([w[:SHARED], own], axis=0)
        return jnp.broadcast_to(w[..., None], w.shape + (128,))

    gate = jnp.pad(pick(gate_weight).transpose(0, 2, 1), ((0, 0), (0, 2), (0, 0)))
    gate = jnp.concatenate([gate, gate], axis=1)
    (
        logits, own, embed_grad, proj_grad, feat_grad, gain_sum, shift_sum, gate_grad, tower_grad,
        tower_bias_sum, tower_out_sum, out_bias_sum,
    ) = dense(
        ids, embedded, feat, proj_full, feat_weight, ups, downs, expert_rows(norm_gain), expert_rows(norm_shift),
        gate, pick(tower_in), over_lanes(pick(tower_bias)), over_lanes(pick(tower_out)),
        jnp.broadcast_to(pick(tower_out_bias).astype(F32)[:, None, None], (2, 8, 128)), label_rows, live,
    )
    logits = logits[0]

    embed_grad = embed_grad.reshape(narrow, cols, rows)
    slot_rows = jnp.stack([slots[turn(i)] for i in range(blocks)]).transpose(1, 0, 2)
    slot_rows = slot_rows.reshape(fields, 1, ev_rows)
    if not direct:
        embed_grad = lax.all_to_all(embed_grad, "narrow", 0, 0, tiled=True)
        returned = place(slot_rows, embed_grad, hi_n, (lo_n, cols, hi_n))
        returned = returned.transpose(1, 0, 2).reshape(cols, owners, cap).transpose(1, 0, 2)
        row_grads = lax.all_to_all(returned, "wide", 0, 0, tiled=True)

    def put(pair):
        zero = jnp.zeros((DOMAINS,) + pair.shape[1:], F32)
        zero = lax.dynamic_update_index_in_dim(zero, pair[0], full, 0)
        return lax.dynamic_update_index_in_dim(zero, pair[1], half, 0)

    def put_experts(sums):
        sums = jnp.sum(sums, axis=-1)
        own = put(sums[SHARED:].reshape(2, DOM_EXP, D)).reshape(DOMAINS * DOM_EXP, D)
        return jnp.concatenate([sums[:SHARED], own], axis=0)

    def pack(x):
        return jnp.concatenate([x[:, :LANES], x[:, LANES:]], axis=0)

    def unpack(x):
        return jnp.concatenate([x[: x.shape[0] // 2], x[x.shape[0] // 2 :]], axis=1)

    tower_grad = put(tower_grad).reshape(DOMAINS * D, 128)
    small = [
        jnp.concatenate([tower_grad[: DOMAINS * D // 2], tower_grad[DOMAINS * D // 2 :]], axis=1),
        pack(feat_grad[:DENSE]),
        pack(put(gate_grad[:, :6] + gate_grad[:, 8:14]).reshape(DOMAINS * 6, D)),
        pack(put_experts(gain_sum)),
        pack(put_experts(shift_sum)),
        feat_grad[DENSE].reshape(2, LANES),
        put(jnp.sum(tower_bias_sum, axis=-1)).reshape(3, LANES),
        put(jnp.sum(tower_out_sum, axis=-1)).reshape(3, LANES),
        jnp.pad(put(jnp.sum(out_bias_sum[:, 0], axis=-1)), (0, LANES - DOMAINS))[None],
    ]
    sizes = [x.shape[0] for x in small]
    small = jnp.concatenate(small, axis=0).astype(BF)
    small = jnp.pad(small, ((0, narrow * REP_ROWS - small.shape[0]), (0, 0)))

    proj_rows = proj_grad.reshape(narrow, cols, 2, LANES).transpose(0, 2, 1, 3)
    extra = jnp.concatenate(
        [proj_rows.reshape(narrow, PROJ_ROWS, LANES), small.reshape(narrow, REP_ROWS, LANES)], axis=1
    )
    extra = by_offset(extra)
    extra = jnp.stack([extra[0], extra[2], extra[1], extra[3]])
    if direct:
        sums, others, row_grads = reduce_all(own, extra, owners, REP_ROWS, (slot_rows, embed_grad, cap))
    else:
        sums, others = reduce_all(own, extra, owners, REP_ROWS)
    row_grads = row_grads.transpose(0, 2, 1).astype(F32)[None]

    own_chip, far_chip = [
        jnp.concatenate([sums[3:5, p], sums[7:9, p], sums[5:7, p]], axis=0) for p in (0, 1)
    ]
    low_half = jnp.where(chip == 0, own_chip, far_chip)
    high_half = jnp.where(chip == 0, far_chip, own_chip)
    whole = jnp.concatenate([sums[1:3, 0], low_half, high_half], axis=0)
    up_grad = whole[:, :D].astype(F32)
    down_grad = whole[:, D:].reshape(14, 2, hid_here, D // 2).transpose(0, 2, 1, 3)
    down_grad = down_grad.reshape(14, hid_here, D).astype(F32)
    proj_grad = unpack(sums[0, 0, :PROJ_ROWS]).astype(F32)
    rep = jnp.concatenate([sums[0, 0, None, PROJ_ROWS:], others], axis=0)
    rep = by_offset(rep).reshape(narrow * REP_ROWS, LANES).astype(F32)
    rest, at = [], 0
    for size in sizes:
        rest.append(rep[at : at + size])
        at += size
    tower_grad = jnp.concatenate([rest[0][:, :128], rest[0][:, 128:]], axis=0)
    common = (
        unpack(rest[1]),
        rest[5].reshape(D),
        unpack(rest[3]),
        unpack(rest[4]),
        unpack(rest[2]).reshape(DOMAINS, 6, D).transpose(0, 2, 1),
        tower_grad.reshape(DOMAINS, D, 128),
        rest[6].reshape(DOMAINS, 128),
        rest[7].reshape(DOMAINS, 128),
        rest[8][0, :DOMAINS],
    )
    logits = jnp.where(core == 1, jnp.roll(logits, HALF, axis=0), logits)
    return (
        logits,
        row_grads,
        proj_grad,
        common[0],
        common[1],
        up_grad,
        down_grad,
        common[2],
        common[3],
        common[4],
        common[5],
        common[6],
        common[7],
        common[8],
    )


def solution(mesh):
    placed = (
        P("wide", "narrow"),
        P("wide", None, None, "narrow"),
        P("wide", "narrow"),
        P(("wide", "narrow")),
        P(("wide", "narrow")),
        P(("wide", "narrow"), None),
        P("narrow", None),
        P(),
        P(),
        P(None, None, "narrow"),
        P(None, "narrow", None),
        P(),
        P(),
        P(),
        P(),
        P(),
        P(),
        P(),
    )
    return jax.shard_map(
        shards,
        mesh=mesh,
        in_specs=placed,
        out_specs=(
            P(("wide", "narrow")),
            P("wide", None, None, "narrow"),
            P("narrow", None),
            P(),
            P(),
            P(None, None, "narrow"),
            P(None, "narrow", None),
            P(),
            P(),
            P(),
            P(),
            P(),
            P(),
            P(),
        ),
        check_vma=False,
    )
```

time: 1170 us -> 627 us (0.54)
  waiting for transfers between devices: 540 us -> 47.2 us
  Pallas kernels: 80.5 us -> 414 us
  other arithmetic: 172 us -> 47.8 us
  matrix products: 124 us -> 0 us
  local copies, waits for them, and re-layouts: 171 us -> 74.8 us
  blocking collectives: 16.7 us -> 0 us
  between operations: 19.6 us -> 3.43 us
    pallas_call x1 -> x2, Pallas kernels: 16.2 us -> 350 us  [the longest x1 231 us: reduce_all(): pl.pallas_call(functools.partial(reduce_kernel, bits, rows is not None),...]
    psum x3 -> x0, waiting for transfers between devices: 297 us -> none  [the longest x2 224 us: shards(): lax.psum((dense_grad, bias_grad, put_experts(gain_shared, gain_own), put_...]
    dot_general x35 -> x0, matrix products: 124 us -> none  [the longest x3 30.2 us: shards(): jnp.einsum('krm,khm->krh', g, down[k], preferred_element_type=F32)]
    reduce_scatter x2 -> x0, waiting for transfers between devices: 121 us -> none  [the longest x1 121 us: shards(): part = lax.psum_scatter(chip_sum, 'wide', scatter_dimension=2, tiled=True)]
    all_to_all x2 -> x0, waiting for transfers between devices: 84.9 us -> none  [the longest x1 72.2 us: shards(): row_grads = lax.all_to_all(returned, 'wide', 0, 0, tiled=True)]
    reshape x21 -> x16, local copies, waits for them, and re-layouts: 54.5 us -> 11.2 us  [the longest x1 5.56 us: shards(): tab = embed_table.reshape(32, table_rows // 32, cols).transpose(0, 2, 1)]
    reduce_sum x24 -> x9, other arithmetic: 30.5 us -> 4.41 us  [the longest x1 1.01 us: shards(): jnp.sum(tower_out_sum, axis=-1)]
    convert_element_type x10 -> x6, other arithmetic: 27.5 us -> 4.69 us  [the longest x1 1.88 us: shards(): pick(tower_out_bias).astype(F32)[:, None, None]]
  transfers between devices with their start and end apart: 19 -> 11, of which waited for: 10 -> 3; matrix products, arithmetic and copies ran while one was open for 19% -> 9% of each run, Pallas kernels for 7% -> 11%
where the time goes in v2:
time: 627 us; the launch traced here: 615 us
  Pallas kernels  414 us (66%)
  local copies, waits for them, and re-layouts  74.8 us (12%)
  other arithmetic  47.8 us (8%)
  waiting for transfers between devices  47.2 us (8%)
  starting transfers between devices  27.4 us (4%)
    pallas_call x1, Pallas kernels, reduce_all(): pl.pallas_call(functools.partial(reduce_kernel, bits, rows is not None),...  231 us
    pallas_call x1, Pallas kernels, dense(): pl.pallas_call(dense_kernel, grid_spec=pltpu.PrefetchScalarGridSpec(num_s...  118 us
    pallas_call x2, Pallas kernels, lookup(): pl.pallas_call(functools.partial(lookup_kernel, lo_n, hi_n, fields), grid...  64.5 us
    all_to_all x1, waiting for transfers between devices, shards(): received = lax.all_to_all(found, 'wide', 0, 0, tiled=True)  26.9 us
    all_to_all x1, waiting for transfers between devices, shards(): embedded = lax.all_to_all(embedded, 'narrow', 0, 0, tiled=True)  20 us
  transfers between devices with their start and end apart: 11, of which 3 were waited for; matrix products, arithmetic and copies ran while one was open for 9% of the time, Pallas kernels for 11%

profile of v2, /device:TPU:0, one launch (start us, length us, event | category | flops | bytes accessed | tf_op | source)
XLA Modules:
  0.0 614.7 jit_solution(4101938074926478217)
XLA Ops:
  0.6 1.8 copy.113
  2.4 7.4 %all-to-all-start = ((s32[8,10,768]{2,1,0:T(8,128)}), s32[8,10,768]{2,1,0:T(8,128)}, u32[]{:S(2)}, u32[]{:S(2)}) async-start(s32[8,10,768]{2,1,0:T(8,128)} %bitcast.120), calls=%async_computation | async-start | bytes 786432 | tf_op jit(solution)/shard_map/all_to_all | solution.py:693
  17.3 1.5 collective-permute-start.1
  18.9 1.5 constant_dynamic-slice_fusion.19
  20.5 2.3 constant_dynamic-slice_fusion.18
  22.7 1.5 pad_maximum_fusion.5
  26.8 1.5 pad_maximum_fusion.6
  29.6 1.7 fusion.4
  42.9 5.6 copy.112
  49.8 6.0 all-to-all-start.3
  55.8 41.7 %lookup_rows.1 = bf16[8,160,768]{2,1,0:T(8,128)(2,1)} custom-call(s32[8,10,768]{2,1,0:T(8,128)} %all-to-all-done.idx_ref, bf16[32,160,512]{2,1,0:T(8,128)(2,1)} %bitcast.128), custom_call_target="tpu_custom_call" | custom-call | flops 32212254720 | bytes 8388608 | tf_op jit(solution)/shard_map/lookup_rows/pallas_call | solution.py:58
  97.6 6.4 %all-to-all-start.1 = ((bf16[8,160,768]{2,1,0:T(8,128)(2,1)}), bf16[8,160,768]{2,1,0:T(8,128)(2,1)}, u32[]{:S(2)}, u32[]{:S(2)}) async-start(bf16[8,160,768]{2,1,0:T(8,128)(2,1)} %lookup_rows.1), calls=%async_computation.1 | async-start | bytes 3932160 | tf_op jit(solution)/shard_map/all_to_all | solution.py:772
  105.9 1.9 maximum_convert_fusion.5
  112.8 1.5 fusion.23
  115.7 1.9 pad_maximum_fusion.1
  117.6 1.5 fusion.22
  119.4 1.9 pad_maximum_fusion.2
  122.0 26.9 %all-to-all-done.1.tab_ref = bf16[8,160,768]{2,1,0:T(8,128)(2,1)} async-done(((bf16[8,160,768]{2,1,0:T(8,128)(2,1)}), bf16[8,160,768]{2,1,0:T(8,128)(2,1)}, u32[]{:S(2)}, u32[]{:S(2)}) %all-to-all-start.1) | async-done | bytes 1966112 | tf_op jit(solution)/shard_map/all_to_all | solution.py:772
  148.9 22.8 %order_rows.1 = bf16[4,160,1536]{2,1,0:T(8,128)(2,1)} custom-call(s32[12,10,512]{2,1,0:T(8,128)} %bitcast.140, bf16[8,160,768]{2,1,0:T(8,128)(2,1)} %all-to-all-done.1.tab_ref), custom_call_target="tpu_custom_call" | custom-call | flops 12079595520 | bytes 8388608 | tf_op jit(solution)/shard_map/order_rows/pallas_call | solution.py:58
  171.7 3.7 all-to-all-start.2
  179.6 20.0 %all-to-all-done.2 = bf16[4,160,1536]{2,1,0:T(8,128)(2,1)S(1)} async-done(((bf16[4,160,1536]{2,1,0:T(8,128)(2,1)}), bf16[4,160,1536]{2,1,0:T(8,128)(2,1)S(1)}, u32[]{:S(2)}, u32[]{:S(2)}) %all-to-all-start.2) | async-done | bytes 1966112 | tf_op jit(solution)/shard_map/all_to_all | solution.py:786
  199.7 1.5 broadcast_in_dim.104.gain_ref
  204.8 118.2 %dense_all.1 = (f32[1,1536]{1,0:T(1,128)}, bf16[6,4,1024,256]{3,2,1,0:T(8,128)(2,1)}, bf16[640,1536]{1,0:T(8,128)(2,1)}, bf16[640,512]{1,0:T(8,128)(2,1)}, f32[1...) custom-call(s32[12]{0:T(128)} %pad_add_fusion.ids_ref, ...), custom_call_target="tpu_custom_call" | custom-call | flops 38999998464 | bytes 62914560 | tf_op jit(solution)/shard_map/dense_all/pallas_call | solution.py:615
  341.0 2.4 concatenate.154
  344.9 1.6 pad_maximum_fusion.8.extra_ref
  346.5 231.4 %reduce_all.1 = (bf16[9,2,1024,256]{3,2,1,0:T(8,128)(2,1)}, bf16[3,704,256]{2,1,0:T(8,128)(2,1)}, bf16[8,160,768]{2,1,0:T(8,128)(2,1)}) custom-call(bf16[6,4,1024,256]{3,2,1,0:T(8,128)(2,1)} %get-tuple-element.30.own_ref, bf16[4,1024,256]{2,1,0:T(8,128)(2,1)} %pad_maximum_fusion.8.extra_ref, s32[10,1,6144]{2,1,0:T(1,128)} %reshape.251.refs_0_, ...), custom_call_target="tpu_custom_call" | custom-call | bytes 62914560 | tf_op jit(solution)/shard_map/reduce_all/pallas_call | solution.py:348
  578.0 1.6 slice_bitcast_fusion.9
  583.4 2.2 copy-done
  586.6 1.7 slice_bitcast_fusion.5
  592.7 4.0 convert_bitcast_fusion.1
  599.1 3.9 fusion.15
  604.0 4.0 copy.105
  (335 shorter events, 77.6 us)
Async XLA Ops:
  2.4 8.9 %copy-start.28 = (s32[1536]{0:T(1024)S(1)}, s32[1536]{0:T(1024)}, u32[]{:S(2)}) copy-start(s32[1536]{0:T(1024)} %param.21) | copy-start | bytes 18436
  2.4 8.9 %copy-start.29 = (s32[1536]{0:T(1024)S(1)}, s32[1536]{0:T(1024)}, u32[]{:S(2)}) copy-start(s32[1536]{0:T(1024)} %param.22) | copy-start | bytes 18436
  2.4 8.9 %slice-start = ((s32[1536]{0:T(1024)}), s32[512]{0:T(512)S(1)}, s32[]{:S(2)}) async-start(s32[1536]{0:T(1024)} %param.21), calls=%async_computation.4 | async-start | bytes 4096 | tf_op jit(solution)/shard_map/jit(_roll_static)/slice | solution.py:730
  2.4 8.9 %slice-start.1 = ((s32[1536]{0:T(1024)}), s32[512]{0:T(512)S(1)}, s32[]{:S(2)}) async-start(s32[1536]{0:T(1024)} %param.22), calls=%async_computation.5 | async-start | bytes 4096 | tf_op jit(solution)/shard_map/jit(_roll_static)/slice | solution.py:730
  2.4 46.8 %all-to-all-start = ((s32[8,10,768]{2,1,0:T(8,128)}), s32[8,10,768]{2,1,0:T(8,128)}, u32[]{:S(2)}, u32[]{:S(2)}) async-start(s32[8,10,768]{2,1,0:T(8,128)} %bitcast.120), calls=%async_computation | async-start | bytes 786432 | tf_op jit(solution)/shard_map/all_to_all | solution.py:693
  17.3 31.1 %collective-permute-start = (f32[8,128]{1,0:T(8,128)}, f32[8,128]{1,0:T(8,128)}, u32[]{:S(2)}, u32[]{:S(2)}) collective-permute-start(f32[8,128]{1,0:T(8,128)} %concatenate.133), channel_id=1, source_target_pairs={{0,1},{1,0},{2,3},{3,2},{4,5},{5,4},{6,7},{7,6},{8,9},{9,8},{10,11... | collective-permute-start | bytes 12296 | tf_op jit(solution)/shard_map/ppermute | solution.py:691
  17.3 158.2 %collective-permute-start.1 = (bf16[160,512]{1,0:T(8,128)(2,1)}, bf16[160,512]{1,0:T(8,128)(2,1)}, u32[]{:S(2)}, u32[]{:S(2)}) collective-permute-start(bf16[160,512]{1,0:T(8,128)(2,1)} %param.24), channel_id=1, source_target_pairs={{0,2},{1,3},{2,0},{3,1},{4,6},{5,7},{6,4},{7,5},{8,10},{9,11},{10,... | collective-permute-start | bytes 491528 | tf_op jit(solution)/shard_map/ppermute | solution.py:691
  24.2 88.6 %collective-permute-start.3 = (bf16[8,512,256]{2,1,0:T(8,128)(2,1)}, bf16[8,512,256]{2,1,0:T(8,128)(2,1)}, u32[]{:S(2)}, u32[]{:S(2)}) collective-permute-start(bf16[8,512,256]{2,1,0:T(8,128)(2,1)} %pad_maximum_fusion.5), channel_id=1, source_target_pairs={{0,2},{1,3},{2,0},{3,1},{4,6},{5,7},{6,4},{7,5},{8,10},{9,11},{10,... | collective-permute-start | bytes 6291464 | tf_op jit(solution)/shard_map/ppermute | solution.py:691
  28.3 10.7 %copy-start.9 = (bf16[2,512,256]{2,1,0:T(8,128)(2,1)S(1)}, bf16[2,512,256]{2,1,0:T(8,128)(2,1)}, u32[]{:S(2)}) copy-start(bf16[2,512,256]{2,1,0:T(8,128)(2,1)} %get-tuple-element.61) | copy-start | bytes 1572868
  28.3 89.3 %collective-permute-start.5 = (bf16[8,256,512]{2,1,0:T(8,128)(2,1)}, bf16[8,256,512]{2,1,0:T(8,128)(2,1)}, u32[]{:S(2)}, u32[]{:S(2)}) collective-permute-start(bf16[8,256,512]{2,1,0:T(8,128)(2,1)} %pad_maximum_fusion.6), channel_id=1, source_target_pairs={{0,2},{1,3},{2,0},{3,1},{4,6},{5,7},{6,4},{7,5},{8,10},{9,11},{10,... | collective-permute-start | bytes 6291464 | tf_op jit(solution)/shard_map/ppermute | solution.py:691
  33.3 72.0 %copy-start.15 = (s32[12,512,10]{1,2,0:T(8,128)}, s32[12,512,10]{1,2,0:T(8,128)S(1)}, u32[]{:S(2)}) copy-start(s32[12,512,10]{1,2,0:T(8,128)S(1)} %copy.114) | copy-start | bytes 737284
  49.8 47.8 %all-to-all-start.3 = ((f32[8,16,128]{2,1,0:T(8,128)}), f32[8,16,128]{2,1,0:T(8,128)S(1)}, u32[]{:S(2)}, u32[]{:S(2)}) async-start(f32[8,16,128]{2,1,0:T(8,128)} %broadcast_in_dim.99), calls=%async_computation.3 | async-start | bytes 131072 | tf_op jit(solution)/shard_map/all_to_all | solution.py:741
  97.6 7.1 %copy-start.49 = (bf16[6]{0:T(256)(128)(2,1)S(1)}, bf16[6]{0:T(256)(128)(2,1)}, u32[]{:S(2)}) copy-start(bf16[6]{0:T(256)(128)(2,1)} %param.35) | copy-start | bytes 40
  97.6 10.8 %copy-start.58 = (bf16[512]{0:T(512)(128)(2,1)S(1)}, bf16[512]{0:T(512)(128)(2,1)}, u32[]{:S(2)}) copy-start(bf16[512]{0:T(512)(128)(2,1)} %param.26) | copy-start | bytes 3076
  97.6 10.8 %copy-start.27 = (f32[1536]{0:T(1024)S(1)}, f32[1536]{0:T(1024)}, u32[]{:S(2)}) copy-start(f32[1536]{0:T(1024)} %get-tuple-element.129) | copy-start | bytes 18436
  97.6 14.2 %copy-start.20 = (bf16[128,512]{1,0:T(8,128)(2,1)S(1)}, bf16[128,512]{1,0:T(8,128)(2,1)}, u32[]{:S(2)}) copy-start(bf16[128,512]{1,0:T(8,128)(2,1)} %param.25) | copy-start | bytes 393220
  97.6 51.2 %all-to-all-start.1 = ((bf16[8,160,768]{2,1,0:T(8,128)(2,1)}), bf16[8,160,768]{2,1,0:T(8,128)(2,1)}, u32[]{:S(2)}, u32[]{:S(2)}) async-start(bf16[8,160,768]{2,1,0:T(8,128)(2,1)} %lookup_rows.1), calls=%async_computation.1 | async-start | bytes 3932160 | tf_op jit(solution)/shard_map/all_to_all | solution.py:772
  117.6 62.0 %collective-permute-start.4 = (bf16[2,6,512,256]{3,2,1,0:T(8,128)(2,1)}, bf16[2,6,512,256]{3,2,1,0:T(8,128)(2,1)}, u32[]{:S(2)}, u32[]{:S(2)}) collective-permute-start(bf16[2,6,512,256]{3,2,1,0:T(8,128)(2,1)} %pad_maximum_fusion.1), channel_id=1, source_target_pairs={{0,1},{1,0},{2,3},{3,2},{4,5},{5,4},{6,7},{7,6},{8,9},{9,8},{10,11... | collective-permute-start | bytes 9437192 | tf_op jit(solution)/shard_map/ppermute | solution.py:691
  121.3 58.3 %collective-permute-start.6 = (bf16[2,6,256,512]{3,2,1,0:T(8,128)(2,1)}, bf16[2,6,256,512]{3,2,1,0:T(8,128)(2,1)}, u32[]{:S(2)}, u32[]{:S(2)}) collective-permute-start(bf16[2,6,256,512]{3,2,1,0:T(8,128)(2,1)} %pad_maximum_fusion.2), channel_id=1, source_target_pairs={{0,1},{1,0},{2,3},{3,2},{4,5},{5,4},{6,7},{7,6},{8,9},{9,8},{10,11... | collective-permute-start | bytes 9437192 | tf_op jit(solution)/shard_map/ppermute | solution.py:691
  171.7 28.0 %all-to-all-start.2 = ((bf16[4,160,1536]{2,1,0:T(8,128)(2,1)}), bf16[4,160,1536]{2,1,0:T(8,128)(2,1)S(1)}, u32[]{:S(2)}, u32[]{:S(2)}) async-start(bf16[4,160,1536]{2,1,0:T(8,128)(2,1)} %order_rows.1), calls=%async_computation.2 | async-start | bytes 3932160 | tf_op jit(solution)/shard_map/all_to_all | solution.py:786
  176.6 1.8 collective-permute-start.2
  178.6 24.1 %copy-start.43 = (f32[2,128]{1,0:T(2,128)S(1)}, f32[2,128]{1,0:T(2,128)}, u32[]{:S(2)}) copy-start(f32[2,128]{1,0:T(2,128)} %maximum_convert_fusion.3) | copy-start | bytes 3076
  178.6 24.8 %copy-start.44 = (f32[2,128]{1,0:T(2,128)S(1)}, f32[2,128]{1,0:T(2,128)}, u32[]{:S(2)}) copy-start(f32[2,128]{1,0:T(2,128)} %maximum_convert_fusion.4) | copy-start | bytes 3076
  178.6 25.6 %copy-start.62 = (f32[2]{0:T(128)S(1)}, f32[2]{0:T(128)}, u32[]{:S(2)}) copy-start(f32[2]{0:T(128)} %maximum_convert_fusion.5) | copy-start | bytes 28
  323.0 7.9 %copy-start.23 = (f32[2,16,512]{2,1,0:T(8,128)S(1)}, f32[2,16,512]{2,1,0:T(8,128)}, u32[]{:S(2)}) copy-start(f32[2,16,512]{2,1,0:T(8,128)} %get-tuple-element.34) | copy-start | bytes 196612
  323.0 12.5 %copy-start.14 = (f32[6,512,128]{2,1,0:T(8,128)S(1)}, f32[6,512,128]{2,1,0:T(8,128)}, u32[]{:S(2)}) copy-start(f32[6,512,128]{2,1,0:T(8,128)} %get-tuple-element.35) | copy-start | bytes 4718596
  328.0 8.2 %copy-start.13 = (f32[6,512,128]{2,1,0:T(8,128)S(1)}, f32[6,512,128]{2,1,0:T(8,128)}, u32[]{:S(2)}) copy-start(f32[6,512,128]{2,1,0:T(8,128)} %get-tuple-element.36) | copy-start | bytes 4718596
  604.0 7.5 %copy-start.25 = (f32[14,256]{1,0:T(8,128)S(1)}, f32[14,256]{1,0:T(8,128)}, u32[]{:S(2)}) copy-start(f32[14,256]{1,0:T(8,128)} %get-tuple-element.70) | copy-start | bytes 43012
  604.0 7.4 %copy-start.26 = (f32[14,256]{1,0:T(8,128)S(1)}, f32[14,256]{1,0:T(8,128)}, u32[]{:S(2)}) copy-start(f32[14,256]{1,0:T(8,128)} %get-tuple-element.71) | copy-start | bytes 43012
  604.0 8.1 %copy-start.24 = (f32[14,256]{1,0:T(8,128)S(1)}, f32[14,256]{1,0:T(8,128)}, u32[]{:S(2)}) copy-start(f32[14,256]{1,0:T(8,128)} %get-tuple-element.69) | copy-start | bytes 43012
  604.0 8.7 %copy-start.6 = (f32[1536,128]{1,0:T(8,128)S(1)}, f32[1536,128]{1,0:T(8,128)}, u32[]{:S(2)}) copy-start(f32[1536,128]{1,0:T(8,128)} %get-tuple-element.64) | copy-start | bytes 2359300
  604.0 8.7 %copy-start.7 = (f32[1536,128]{1,0:T(8,128)S(1)}, f32[1536,128]{1,0:T(8,128)}, u32[]{:S(2)}) copy-start(f32[1536,128]{1,0:T(8,128)} %get-tuple-element.65) | copy-start | bytes 2359300
  (48 other events, 209.8 us)

commit v3 on v2

--- a/solution.py
+++ b/solution.py
@@ -80,7 +80,7 @@
     cols = pl.ds(pl.multiple_of(field * EMB, EMB), EMB)
     total = None
     for s in range(grad_ref.shape[0]):
-        idx = idx_ref[field, :, s * length : (s + 1) * length]
+        idx = idx_ref[s, pl.ds(field, 1), :]
         hi = idx & (hi_n - 1)
         lo = lax.shift_right_logical(idx, hi_n.bit_length() - 1)
         grad = grad_ref[s, cols, :]
@@ -96,29 +96,336 @@
 
 
 def place_kernel(idx_ref, grad_ref, out_ref):
-    place_one(idx_ref, grad_ref, out_ref, 0)
-
-
-def place(idx, grad, hi_n, out_shape):
-    fields, _, length = idx.shape
-    parts, cols, each = grad.shape
-    outer, _, inner = out_shape
-    lo_n = outer * inner // hi_n
+    def one(field, _):
+        place_one(idx_ref, grad_ref, out_ref, field)
+        return 0
+
+    lax.fori_loop(0, idx_ref.shape[1], one, 0)
+
+
+def place(idx, grad, out_shape):
     return pl.pallas_call(
         place_kernel,
-        grid=(fields,),
-        in_specs=[
-            pl.BlockSpec((1, 1, length), lambda i: (i, 0, 0)),
-            pl.BlockSpec((parts, EMB, each), lambda i: (0, i, 0)),
-        ],
-        out_specs=pl.BlockSpec((outer, EMB, inner), lambda i: (0, i, 0)),
         out_shape=jax.ShapeDtypeStruct(out_shape, BF),
         compiler_params=pltpu.CompilerParams(vmem_limit_bytes=VMEM),
-        cost_estimate=pl.CostEstimate(
-            flops=2 * cols * length * lo_n * hi_n, bytes_accessed=6 * 2**20, transcendentals=0
-        ),
         name="place_rows",
     )(idx, grad)
+
+
+def front_kernel(
+    groups, req_ref, tab_ref, slot_ref, stat_ref, up_ref, down_ref, proj_ref,
+    emb_ref, far_up, far_down, their_up, their_down, proj_out, every_ref,
+    asked, found, received, ordered, both,
+    req_send, req_recv, row_send, row_recv, near_send, near_recv, keep_sem,
+    far_send, far_recv, side_send, own_send, own_recv, their_send, their_recv, proj_send, proj_recv,
+    stat_send, stat_recv,
+):
+    wide, me = lax.axis_index("wide"), lax.axis_index("narrow")
+    chip, core = me // 2, me % 2
+    owners, fields, cap = req_ref.shape
+    share = fields // groups
+    parity = wide % 2
+    near = [{"narrow": me + 1 - 2 * core}, {"narrow": me + 2 - 4 * chip}, {"narrow": 3 - me}]
+    near_at = [me + 1 - 2 * core, me + 2 - 4 * chip, 3 - me]
+    peers = [None] + [{"wide": (wide + d) % owners} for d in range(1, owners)]
+    side = {"wide": wide + 1 - 2 * parity}
+    barrier = pltpu.get_barrier_semaphore()
+    for mate in near + peers[1:]:
+        pl.semaphore_signal(barrier, inc=1, device_id=mate, device_id_type=MESH)
+    pl.semaphore_wait(barrier, len(near) + len(peers) - 1)
+
+    def remote(src, dst, send, recv, mate):
+        return pltpu.make_async_remote_copy(
+            src_ref=src, dst_ref=dst, send_sem=send, recv_sem=recv, device_id=mate, device_id_type=MESH
+        )
+
+    def req_copy(d):
+        return remote(req_ref.at[(wide + d) % owners], asked.at[wide], req_send.at[d], req_recv.at[d], peers[d])
+
+    for d in range(1, owners):
+        req_copy(d).start()
+    mine = pltpu.make_async_copy(req_ref.at[wide], asked.at[wide], keep_sem.at[0])
+    mine.start()
+
+    def stat_core():
+        return remote(stat_ref, both.at[pl.ds(8, 8)], stat_send.at[0], stat_recv.at[0], near[0])
+
+    def stat_copy(d):
+        return remote(both, every_ref.at[wide], stat_send.at[d], stat_recv.at[d], peers[d])
+
+    stat_core().start()
+    both[0:8, :] = stat_ref[...]
+
+    weights = ((up_ref, far_up, their_up), (down_ref, far_down, their_down))
+
+    def far_copy(j, a):
+        p = 2 * j + parity
+        expert = jnp.where(j == 0, parity, 6 * (1 - chip) + p)
+        return remote(weights[a][0].at[expert], weights[a][1].at[p], far_send.at[a, j], far_recv.at[a, p], near[1])
+
+    def side_copy(p, a):
+        view = weights[a][1].at[p]
+        return remote(view, view, side_send.at[a, p // 2], far_recv.at[a, p], side)
+
+    def own_copy(i, a):
+        expert = jnp.where(i < 2, i, 6 * chip + jnp.where(i < 4, i + 4 * (1 - core), i))
+        return remote(weights[a][0].at[expert], weights[a][2].at[0, i], own_send.at[a, i], own_recv.at[a, i], near[0])
+
+    def their_copy(p, a):
+        i = jnp.where(p < 6, p, p - 4)
+        return remote(weights[a][1].at[p], weights[a][2].at[1, i], their_send.at[a, i], their_recv.at[a, i], near[0])
+
+    def wanted(p):
+        ends = jnp.logical_or(jnp.logical_and(p < 4, core == 1), jnp.logical_and(p >= 6, core == 0))
+        return jnp.logical_or(jnp.logical_or(p < 2, jnp.logical_and(p >= 4, p < 6)), ends)
+
+    def for_all(n, f):
+        def body(i, _):
+            for a in range(2):
+                f(i, a)
+            return 0
+
+        lax.fori_loop(0, n, body, 0)
+
+    for_all(4, lambda j, a: far_copy(j, a).start())
+
+    def proj_copy(i):
+        return remote(proj_ref, proj_out.at[me], proj_send.at[i], proj_recv.at[i], near[i])
+
+    keep_proj = pltpu.make_async_copy(proj_ref, proj_out.at[me], keep_sem.at[1])
+    keep_proj.start()
+    for i in range(3):
+        proj_copy(i).start()
+    for_all(6, lambda i, a: own_copy(i, a).start())
+    stat_core().wait_recv()
+    for d in range(1, owners):
+        stat_copy(d).start()
+    keep_stat = pltpu.make_async_copy(both, every_ref.at[wide], keep_sem.at[2])
+    keep_stat.start()
+
+    def far_step(j):
+        p = 2 * j + parity
+        for a in range(2):
+            far_copy(j, a).wait_recv()
+            side_copy(p, a).start()
+        pass_on(p)
+
+    def pass_on(p):
+        @pl.when(wanted(p))
+        def _():
+            for a in range(2):
+                their_copy(p, a).start()
+
+    def side_step(j):
+        p = 2 * j + 1 - parity
+        for a in range(2):
+            side_copy(p, a).wait_recv()
+        pass_on(p)
+
+    lo_n, _, hi_n = tab_ref.shape
+
+    def find(f, owner_idx):
+        idx = asked[owner_idx, pl.ds(f, 1), :]
+        hi = jnp.where(idx >= 0, idx & (hi_n - 1), -1)
+        lo = lax.shift_right_logical(jnp.maximum(idx, 0), hi_n.bit_length() - 1)
+        hot = (lax.broadcasted_iota(jnp.int32, (hi_n, cap), 0) == hi).astype(BF)
+        cols = pl.ds(pl.multiple_of(f * EMB, EMB), EMB)
+        res = jnp.dot(tab_ref[:, cols, :].reshape(lo_n * EMB, hi_n), hot, preferred_element_type=F32)
+        acc = res[0:EMB]
+        for step in range(1, lo_n):
+            acc = jnp.where(lo == step, res[step * EMB : (step + 1) * EMB], acc)
+        return cols, acc.astype(BF)
+
+    def group_rows(g):
+        return pl.ds(pl.multiple_of(g * share * EMB, share * EMB), share * EMB)
+
+    def row_copy(g, d, mate):
+        rows = group_rows(g)
+        return remote(
+            found.at[(wide + d) % owners, rows], received.at[wide, rows], row_send.at[g, d], row_recv.at[g, d], mate
+        )
+
+    def look(g):
+        def one(d, _):
+            sender = (wide + d) % owners
+
+            @pl.when(jnp.logical_and(g == 0, d > 0))
+            def _():
+                remote(req_ref.at[0], asked.at[sender], req_send.at[d], req_recv.at[owners - d], peers[1]).wait_recv()
+
+            for k in range(share):
+                cols, block = find(g * share + k, sender)
+
+                @pl.when(d == 0)
+                def _():
+                    received[wide, cols, :] = block
+
+                @pl.when(d > 0)
+                def _():
+                    found[sender, cols, :] = block
+
+            @pl.when(d > 0)
+            def _():
+                row_copy(g, d, {"wide": sender}).start()
+
+            return 0
+
+        lax.fori_loop(0, owners, one, 0)
+
+    hi_e = 256
+    outer = owners * cap // hi_e
+
+    def near_copy(g, i):
+        rows = group_rows(g)
+        return remote(
+            ordered.at[near_at[i], rows], emb_ref.at[me, rows], near_send.at[g, i], near_recv.at[g, i], near[i]
+        )
+
+    def keep_copy(g):
+        rows = group_rows(g)
+        return pltpu.make_async_copy(ordered.at[me, rows], emb_ref.at[me, rows], keep_sem.at[3 + g])
+
+    def order(g):
+        def arrive(d, _):
+            row_copy(g, d, {"wide": (wide + d) % owners}).wait_recv()
+            return 0
+
+        lax.fori_loop(1, owners, arrive, 0)
+        tables = []
+        for k in range(share):
+            cols = pl.ds(pl.multiple_of((g * share + k) * EMB, EMB), EMB)
+            parts = [
+                received[:, cols, j * hi_e : (j + 1) * hi_e].reshape(owners * EMB, hi_e) for j in range(cap // hi_e)
+            ]
+            tables.append((cols, jnp.concatenate(parts, axis=0)))
+
+        def quarter(q):
+            for k, (cols, table) in enumerate(tables):
+                idx = slot_ref[q, pl.ds(g * share + k, 1), :]
+                hi = idx & (hi_e - 1)
+                lo = lax.shift_right_logical(idx, hi_e.bit_length() - 1)
+                hot = (lax.broadcasted_iota(jnp.int32, (hi_e, idx.shape[1]), 0) == hi).astype(BF)
+                res = jnp.dot(table, hot, preferred_element_type=F32)
+                acc = res[0:EMB]
+                for step in range(1, outer):
+                    acc = jnp.where(lo == step, res[step * EMB : (step + 1) * EMB], acc)
+                ordered[q, cols, :] = acc.astype(BF)
+
+        for i in (2, 1, 0):
+            quarter(near_at[i])
+            near_copy(g, i).start()
+        quarter(me)
+        keep_copy(g).start()
+
+    mine.wait()
+
+    def tick(t, _):
+        @pl.when(t < groups)
+        def _():
+            look(t)
+
+        @pl.when(jnp.logical_and(t >= 1, t < 5))
+        def _():
+            far_step(t - 1)
+
+        @pl.when(t >= 2)
+        def _():
+            order(t - 2)
+
+        @pl.when(t >= 3)
+        def _():
+            side_step(t - 3)
+
+        return 0
+
+    lax.fori_loop(0, groups + 2, tick, 0)
+
+    for d in range(1, owners):
+        req_copy(d).wait_send()
+        stat_copy(d).wait()
+    stat_core().wait_send()
+    keep_stat.wait()
+    keep_proj.wait()
+    for i in range(3):
+        proj_copy(i).wait()
+
+    def rows_left(g, _):
+        def one(d, _):
+            row_copy(g, d, {"wide": (wide + d) % owners}).wait_send()
+            return 0
+
+        lax.fori_loop(1, owners, one, 0)
+        for i in range(3):
+            near_copy(g, i).wait()
+        keep_copy(g).wait()
+        return 0
+
+    lax.fori_loop(0, groups, rows_left, 0)
+
+    def weights_left(j, a):
+        far_copy(j, a).wait_send()
+        side_copy(2 * j + parity, a).wait_send()
+
+    for_all(4, weights_left)
+    for_all(6, lambda i, a: own_copy(i, a).wait())
+
+    def passed(p, a):
+        @pl.when(wanted(p))
+        def _():
+            their_copy(p, a).wait_send()
+
+    for_all(8, passed)
+    for_all(6, lambda i, a: their_copy(i, a).wait_recv())
+
+
+def front(req, tab, slots, stats, up, down, proj, groups=5):
+    owners, fields, cap = req.shape
+    cols = fields * EMB
+    quarters, _, rows = slots.shape
+    any_space, vmem = pl.BlockSpec(memory_space=pl.ANY), pl.BlockSpec(memory_space=pltpu.VMEM)
+    dma = pltpu.SemaphoreType.DMA
+    return pl.pallas_call(
+        functools.partial(front_kernel, groups),
+        in_specs=[vmem] * 4 + [any_space] * 3,
+        out_specs=[any_space] * 7,
+        out_shape=[
+            jax.ShapeDtypeStruct((quarters, cols, rows), BF),
+            jax.ShapeDtypeStruct((8,) + up.shape[1:], BF),
+            jax.ShapeDtypeStruct((8,) + down.shape[1:], BF),
+            jax.ShapeDtypeStruct((2, 6) + up.shape[1:], BF),
+            jax.ShapeDtypeStruct((2, 6) + down.shape[1:], BF),
+            jax.ShapeDtypeStruct((quarters,) + proj.shape, BF),
+            jax.ShapeDtypeStruct((owners, 16, DENSE), F32),
+        ],
+        scratch_shapes=[
+            pltpu.VMEM((owners, fields, cap), jnp.int32),
+            pltpu.VMEM((owners, cols, cap), BF),
+            pltpu.VMEM((owners, cols, cap), BF),
+            pltpu.VMEM((quarters, cols, rows), BF),
+            pltpu.VMEM((16, DENSE), F32),
+            dma((owners,)),
+            dma((owners,)),
+            dma((groups, owners)),
+            dma((groups, owners)),
+            dma((groups, 3)),
+            dma((groups, 3)),
+            dma((3 + groups,)),
+            dma((2, 4)),
+            dma((2, 8)),
+            dma((2, 4)),
+            dma((2, 6)),
+            dma((2, 6)),
+            dma((2, 6)),
+            dma((2, 6)),
+            dma((3,)),
+            dma((3,)),
+            dma((owners,)),
+            dma((owners,)),
+        ],
+        compiler_params=pltpu.CompilerParams(collective_id=1, has_side_effects=True, vmem_limit_bytes=VMEM),
+        cost_estimate=pl.CostEstimate(flops=45 * 10**9, bytes_accessed=40 * 2**20, transcendentals=0),
+        name="front",
+    )(req, tab, slots, stats, up, down, proj)
 
 
 def reduce_kernel(bits, with_rows, own_ref, extra_ref, *refs):
@@ -266,7 +573,7 @@
         place_one(slot_ref, grads, placed, f)
         return 0
     def row_step(t):
-        fields=slot_ref.shape[0]
+        fields=slot_ref.shape[1]
         @pl.when(t==2)
         def _():
             keep_copy().wait()
@@ -690,8 +997,6 @@
     def swap(x, pairs):
         return lax.ppermute(x, "narrow", pairs)
 
-    asked = lax.all_to_all(requests[0].transpose(0, 2, 1), "wide", 0, 0, tiled=True)
-
     def chip_experts(w, which):
         return jnp.concatenate(
             [w[:SHARED], lax.dynamic_slice_in_dim(w, SHARED + 6 * which, 6, axis=0)], axis=0
@@ -710,8 +1015,6 @@
         )
         return w, far, swap(theirs, other_core)
 
-    ups = bring(up_weight)
-    downs = bring(down_weight)
     six = jnp.arange(6, dtype=jnp.int32)
     spot = jnp.where(six < 2, six, jnp.where(six < 4, six + 4 * core, six))
     ids = jnp.concatenate([jnp.where(six < 2, six, spot + 6 * chip), spot])
@@ -721,10 +1024,6 @@
         x = jnp.where(chip == 1, x[::-1], x)
         x = jnp.where(core == 1, x[:, ::-1], x)
         return x.reshape((narrow,) + x.shape[2:])
-
-    column = jnp.stack([proj_weight, swap(proj_weight, other_chip)])
-    column = jnp.stack([column, swap(column, other_core)], axis=1)
-    proj_full = by_offset(column.reshape((narrow,) + proj_weight.shape)).reshape(-1, D)
 
     def turned(x):
         return jnp.where(core == 1, jnp.roll(x, -HALF, axis=0), x)
@@ -737,10 +1036,45 @@
         own_stats(feats[:, :DSLOT], live[:, :DSLOT]) + own_stats(feats[:, DSLOT:], live[:, DSLOT:])
     )
     stats = jnp.concatenate([stats, blank], axis=0)
-    stats = jnp.concatenate([stats, swap(stats, other_core)], axis=0)
-    every = lax.all_to_all(
-        jnp.broadcast_to(stats, (owners,) + stats.shape), "wide", 0, 0, tiled=True
-    )
+
+    turn = lambda i: (i // 3) * 3 + (i % 3 + (i // 3) % 2) % 3
+    table_rows = embed_table.shape[0]
+    cols = fields * EMB
+    blocks = ev_rows // HALF
+    hi_n = 256
+    lo_n = ev_rows // hi_n
+    direct = cap % hi_n == 0
+    tab = embed_table.reshape(32, table_rows // 32, cols).transpose(0, 2, 1)
+    slots = slot_index
+    if direct:
+        owner, rest = slots // cap, slots % cap
+        slots = ((rest // hi_n) * owners + owner) * hi_n + rest % hi_n
+    slots = slots.reshape(blocks, HALF, fields).transpose(0, 2, 1)
+    slot_rows = jnp.stack([slots[turn(i)] for i in range(blocks)]).reshape(narrow, 3, fields, HALF)
+    slot_rows = slot_rows.transpose(0, 2, 1, 3).reshape(narrow, fields, rows)
+    asked = requests[0].transpose(0, 2, 1)
+    if direct:
+        embedded, far_up, far_down, their_up, their_down, proj_full, every = front(
+            asked, tab, slot_rows, stats, up_weight, down_weight, proj_weight
+        )
+        ups, downs = (up_weight, far_up, their_up), (down_weight, far_down, their_down)
+    else:
+        asked = lax.all_to_all(asked, "wide", 0, 0, tiled=True)
+        ups, downs = bring(up_weight), bring(down_weight)
+        proj_full = lax.all_gather(proj_weight, "narrow", axis=0)
+        stats = jnp.concatenate([stats, swap(stats, other_core)], axis=0)
+        every = lax.all_to_all(
+            jnp.broadcast_to(stats, (owners,) + stats.shape), "wide", 0, 0, tiled=True
+        )
+        flat = asked.transpose(1, 0, 2).reshape(fields, DOMAINS, DSLOT).transpose(1, 0, 2)
+        found = lookup(flat, tab, table_rows // 32, "lookup_rows", DOMAINS)
+        found = found.transpose(1, 0, 2).reshape(cols, owners, cap).transpose(1, 0, 2)
+        received = lax.all_to_all(found, "wide", 0, 0, tiled=True)
+        received = received.transpose(1, 0, 2).reshape(cols, lo_n, hi_n).transpose(1, 0, 2)
+        embedded = lookup(slots, received, hi_n, "order_rows", narrow, turn)
+        embedded = lax.all_to_all(embedded, "narrow", 0, 0, tiled=True)
+    embedded = embedded.reshape(narrow * cols, rows)
+    proj_full = proj_full.reshape(narrow * cols, D)
     full_mean, full_spread = pool(every[:, 0], every[:, 1], every[:, 2])
     both = jnp.concatenate([every[:, 3:6], every[:, 11:14]], axis=0)
     half_mean, half_spread = pool(both[:, 0], both[:, 1], both[:, 2])
@@ -758,34 +1092,6 @@
     ).astype(BF)
     feat_weight = jnp.concatenate([dense_weight, proj_bias[None], jnp.zeros((15, D), BF)], axis=0)
 
-    table_rows = embed_table.shape[0]
-    cols = fields * EMB
-    direct = cap % 256 == 0
-    tab = embed_table.reshape(32, table_rows // 32, cols).transpose(0, 2, 1)
-    hi_n = table_rows // 32
-    if direct:
-        found = lookup(asked, tab, hi_n, "lookup_rows", owners)
-    else:
-        flat = asked.transpose(1, 0, 2).reshape(fields, DOMAINS, DSLOT).transpose(1, 0, 2)
-        found = lookup(flat, tab, hi_n, "lookup_rows", DOMAINS)
-        found = found.transpose(1, 0, 2).reshape(cols, owners, cap).transpose(1, 0, 2)
-    received = lax.all_to_all(found, "wide", 0, 0, tiled=True)
-
-    hi_n = 256
-    lo_n = ev_rows // hi_n
-    blocks = ev_rows // HALF
-    slots = slot_index
-    if direct:
-        owner, rest = slots // cap, slots % cap
-        slots = ((rest // hi_n) * owners + owner) * hi_n + rest % hi_n
-    else:
-        received = received.transpose(1, 0, 2).reshape(cols, lo_n, hi_n).transpose(1, 0, 2)
-    slots = slots.reshape(blocks, HALF, fields).transpose(0, 2, 1)
-    turn = lambda i: (i // 3) * 3 + (i % 3 + (i // 3) % 2) % 3
-    embedded = lookup(slots, received, hi_n, "order_rows", narrow, turn)
-    embedded = lax.all_to_all(embedded, "narrow", 0, 0, tiled=True)
-    embedded = embedded.reshape(narrow * cols, rows)
-
     def pick(w):
         return jnp.stack(
             [
@@ -815,11 +1121,9 @@
     logits = logits[0]
 
     embed_grad = embed_grad.reshape(narrow, cols, rows)
-    slot_rows = jnp.stack([slots[turn(i)] for i in range(blocks)]).transpose(1, 0, 2)
-    slot_rows = slot_rows.reshape(fields, 1, ev_rows)
     if not direct:
         embed_grad = lax.all_to_all(embed_grad, "narrow", 0, 0, tiled=True)
-        returned = place(slot_rows, embed_grad, hi_n, (lo_n, cols, hi_n))
+        returned = place(slot_rows, embed_grad, (lo_n, cols, hi_n))
         returned = returned.transpose(1, 0, 2).reshape(cols, owners, cap).transpose(1, 0, 2)
         row_grads = lax.all_to_all(returned, "wide", 0, 0, tiled=True)
 

time: 627 us -> 524 us (0.84); the launches traced: 615 us -> 521 us
  waiting for transfers between devices: 47.2 us -> 0 us
  local copies, waits for them, and re-layouts: 74.8 us -> 40.2 us
  Pallas kernels: 414 us -> 445 us
  starting transfers between devices: 27.4 us -> 0 us
  other arithmetic: 47.8 us -> 33.1 us
    all_to_all x4 -> x0, waiting for transfers between devices: 47 us -> none  [the longest x1 26.9 us: shards(): received = lax.all_to_all(found, 'wide', 0, 0, tiled=True)]
    pallas_call x2 -> x1, Pallas kernels: 64.5 us -> 103 us  [front(): pl.pallas_call(functools.partial(front_kernel, groups), in_specs=[vmem] *...]
    all_to_all x4 -> x0, starting transfers between devices: 23.6 us -> none  [the longest x1 7.4 us: shards(): lax.all_to_all(requests[0].transpose(0, 2, 1), 'wide', 0, 0, tiled=True)]
    unnamed x139 -> x40, local copies, waits for them, and re-layouts: 12 us -> 2.94 us
    another operation x14 -> x6, other arithmetic: 8.04 us -> 0.29 us  [the longest x6 5.7 us: bring(): jnp.stack([jnp.concatenate([w[:SHARED], at(w, base + away, 2), at(w, base...]
    pallas_call x1, Pallas kernels: 118 us -> 110 us  [dense(): pl.pallas_call(dense_kernel, grid_spec=pltpu.PrefetchScalarGridSpec(num_s...]
  transfers between devices with their start and end apart: 11 -> 0, of which waited for: 3 -> 0; matrix products, arithmetic and copies ran while one was open for 9% -> 0% of each run, Pallas kernels for 11% -> 0%
where the time goes in v3:
time: 524 us; the launch traced here: 521 us
  Pallas kernels  445 us (85%)
  local copies, waits for them, and re-layouts  40.2 us (8%)
  other arithmetic  33.1 us (6%)
    pallas_call x1, Pallas kernels, reduce_all(): pl.pallas_call(functools.partial(reduce_kernel, bits, rows is not None),...  232 us
    pallas_call x1, Pallas kernels, dense(): pl.pallas_call(dense_kernel, grid_spec=pltpu.PrefetchScalarGridSpec(num_s...  110 us
    pallas_call x1, Pallas kernels, front(): pl.pallas_call(functools.partial(front_kernel, groups), in_specs=[vmem] *...  103 us

profile of v3, /device:TPU:0, one launch (start us, length us, event | category | flops | bytes accessed | tf_op | source)
XLA Modules:
  0.0 521.2 jit_solution(17761412897210968382)
XLA Ops:
  1.3 1.8 copy.72
  3.0 5.6 %copy.71 = bf16[20,32,8,512]{3,2,0,1:T(8,128)(2,1)} copy(bf16[20,32,8,512]{3,2,1,0:T(8,128)(2,1)} %bitcast.116) | data formatting | bytes 10485760 | tf_op jit(solution)/shard_map/reshape | solution.py:1047
  10.4 0.8 copy.51.slot_ref.refs_0_
  17.2 102.8 %front.1 = (bf16[4,160,1536]{2,1,0:T(8,128)(2,1)}, bf16[8,512,256]{2,1,0:T(8,128)(2,1)}, bf16[8,256,512]{2,1,0:T(8,128)(2,1)}, bf16[2,6,512,256]{3,2,1,0:T(8,128...) custom-call(s32[8,10,768]{2,1,0:T(8,128)} %bitcast.128, ...), custom_call_target="tpu_custom_call" | custom-call | flops 44999999488 | bytes 41943040 | tf_op jit(solution)/shard_map/front/pallas_call | solution.py:387
  120.1 0.8 fusion.29
  121.1 0.9 copy.52
  122.0 0.9 fusion.28
  123.1 1.0 maximum_maximum_fusion.feat_ref
  125.1 1.4 broadcast_in_dim.100.gain_ref
  126.5 1.4 broadcast_in_dim.101.shift_ref
  129.3 1.0 constant_dynamic-slice_fusion.5
  133.2 1.4 maximum_convert_fusion.5
  135.8 110.4 %dense_all.1 = (f32[1,1536]{1,0:T(1,128)}, bf16[6,4,1024,256]{3,2,1,0:T(8,128)(2,1)}, bf16[640,1536]{1,0:T(8,128)(2,1)}, bf16[640,512]{1,0:T(8,128)(2,1)}, f32[1...) custom-call(s32[12]{0:T(128)} %pad_add_fusion.ids_ref, ...), custom_call_target="tpu_custom_call" | custom-call | flops 38999998464 | bytes 62914560 | tf_op jit(solution)/shard_map/dense_all/pallas_call | solution.py:922
  249.0 1.0 slice_dynamic-update-slice_fusion.1
  250.0 1.0 slice_dynamic-update-slice_fusion
  251.3 2.1 reduce_sum.185
  254.2 1.0 reduce_sum.187
  255.5 0.8 slice_reduce_fusion.3
  258.9 1.6 pad_maximum_fusion.4.extra_ref
  260.5 231.8 %reduce_all.1 = (bf16[9,2,1024,256]{3,2,1,0:T(8,128)(2,1)}, bf16[3,704,256]{2,1,0:T(8,128)(2,1)}, bf16[8,160,768]{2,1,0:T(8,128)(2,1)}) custom-call(bf16[6,4,1024,256]{3,2,1,0:T(8,128)(2,1)} %get-tuple-element.44.own_ref, bf16[4,1024,256]{2,1,0:T(8,128)(2,1)} %pad_maximum_fusion.4.extra_ref, s32[4,10,1536]{2,1,0:T(8,128)} %copy.51.slot_ref.refs_0_, ...), custom_call_target="tpu_custom_call" | custom-call | bytes 62914560 | tf_op jit(solution)/shard_map/reduce_all/pallas_call | solution.py:655
  492.3 3.9 convert_bitcast_fusion.1
  496.2 0.9 slice_bitcast_fusion.9
  497.2 0.8 maximum_convert_fusion
  497.9 1.0 slice_bitcast_fusion.7
  501.4 1.3 slice_bitcast_fusion.6
  502.7 3.0 slice_bitcast_fusion.5
  505.7 0.8 broadcast_select_fusion.1
  506.5 0.8 pad_maximum_fusion
  507.3 3.9 fusion.16
  511.3 0.9 convert_bitcast_fusion
  512.2 4.0 copy.65
  518.3 1.2 pad_maximum_fusion.5
  (194 shorter events, 26.4 us)
Async XLA Ops:
  3.0 5.6 %copy-start.4 = (s32[6144,10]{0,1:T(8,128)S(1)}, s32[6144,10]{0,1:T(8,128)}, u32[]{:S(2)}) copy-start(s32[6144,10]{0,1:T(8,128)} %param.20) | copy-start | bytes 737284
  8.6 2.6 copy-start.2
  11.3 0.7 copy-start.9
  11.3 0.7 copy-start.10
  11.3 0.8 slice-start
  11.3 0.8 slice-start.1
  12.1 108.0 %copy-start.11 = (f32[1,1536]{1,0:T(1,128)}, f32[1,1536]{1,0:T(1,128)S(1)}, u32[]{:S(2)}) copy-start(f32[1,1536]{1,0:T(1,128)S(1)} %broadcast_in_dim.94.live_ref) | copy-start | bytes 18436
  17.2 106.9 %copy-start.15 = (bf16[512]{0:T(512)(128)(2,1)S(1)}, bf16[512]{0:T(512)(128)(2,1)}, u32[]{:S(2)}) copy-start(bf16[512]{0:T(512)(128)(2,1)} %param.26) | copy-start | bytes 3076
  17.2 107.0 %copy-start.6 = (bf16[128,512]{1,0:T(8,128)(2,1)S(1)}, bf16[128,512]{1,0:T(8,128)(2,1)}, u32[]{:S(2)}) copy-start(bf16[128,512]{1,0:T(8,128)(2,1)} %param.25) | copy-start | bytes 393220
  17.2 107.7 %copy-start.13 = (bf16[14,512]{1,0:T(8,128)(2,1)S(1)}, bf16[14,512]{1,0:T(8,128)(2,1)}, u32[]{:S(2)}) copy-start(bf16[14,512]{1,0:T(8,128)(2,1)} %param.30) | copy-start | bytes 43012
  17.2 107.7 %copy-start.12 = (bf16[14,512]{1,0:T(8,128)(2,1)S(1)}, bf16[14,512]{1,0:T(8,128)(2,1)}, u32[]{:S(2)}) copy-start(bf16[14,512]{1,0:T(8,128)(2,1)} %param.29) | copy-start | bytes 43012
  17.2 107.8 %slice-start.2 = ((bf16[14,512]{1,0:T(8,128)(2,1)}), bf16[2,512]{1,0:T(2,128)(2,1)S(1)}, s32[]{:S(2)}) async-start(bf16[14,512]{1,0:T(8,128)(2,1)} %param.29), calls=%async_computation.2 | async-start | bytes 4096 | tf_op jit(solution)/shard_map/slice | solution.py:1108
  120.0 6.5 %slice-start.3 = ((bf16[14,512]{1,0:T(8,128)(2,1)}), bf16[2,512]{1,0:T(2,128)(2,1)S(1)}, s32[]{:S(2)}) async-start(bf16[14,512]{1,0:T(8,128)(2,1)} %param.30), calls=%async_computation.3 | async-start | bytes 4096 | tf_op jit(solution)/shard_map/slice | solution.py:1108
  120.0 11.0 %copy-start.16 = (bf16[6,128]{1,0:T(8,128)(2,1)S(1)}, bf16[6,128]{1,0:T(8,128)(2,1)}, u32[]{:S(2)}) copy-start(bf16[6,128]{1,0:T(8,128)(2,1)} %param.34) | copy-start | bytes 4612
  120.0 11.0 %copy-start.17 = (bf16[6,128]{1,0:T(8,128)(2,1)S(1)}, bf16[6,128]{1,0:T(8,128)(2,1)}, u32[]{:S(2)}) copy-start(bf16[6,128]{1,0:T(8,128)(2,1)} %param.33) | copy-start | bytes 4612
  121.0 11.6 %copy-start.14 = (bf16[6]{0:T(256)(128)(2,1)S(1)}, bf16[6]{0:T(256)(128)(2,1)}, u32[]{:S(2)}) copy-start(bf16[6]{0:T(256)(128)(2,1)} %param.35) | copy-start | bytes 40
  246.2 5.0 copy-start.5
  246.2 5.0 copy-start.8
  251.0 2.5 copy-start
  251.1 4.3 copy-start.7
  253.5 3.9 copy-start.3
  492.3 6.6 %copy-start.1 = (bf16[3,704,256]{2,1,0:T(8,128)(2,1)S(1)}, bf16[3,704,256]{2,1,0:T(8,128)(2,1)}, u32[]{:S(2)}) copy-start(bf16[3,704,256]{2,1,0:T(8,128)(2,1)} %get-tuple-element.57) | copy-start | bytes 3244036

commit v4 on v3

v4 whole, which is shorter than its diff:
```python
import functools

import jax
import jax.numpy as jnp
from jax import lax
from jax.experimental import pallas as pl
from jax.experimental.pallas import tpu as pltpu
from jax.sharding import PartitionSpec as P

D = 512
HID = 1024
EMB = 16
DENSE = 128
DOMAINS = 6
SHARED = 2
DOM_EXP = 2
DSLOT = 1024
HALF = DSLOT // 2
VMEM = 56 * 2**20
BF = jnp.bfloat16
F32 = jnp.float32
MESH = pl.DeviceIdType.MESH
UNITS = 9
TURNED = 0
ROW_AT = 5
ROW_STEP = 1
ROWS_U = 1024
LANES = 256


def dot(a, b, ca, cb):
    return lax.dot_general(a, b, (((ca,), (cb,)), ((), ())), preferred_element_type=F32)


def lookup_kernel(lo_n, hi_n, fields, idx_ref, tab_ref, out_ref):
    length = idx_ref.shape[-1]
    shift = hi_n.bit_length() - 1
    for f in range(fields):
        idx = idx_ref[0, f : f + 1, :]
        hi = jnp.where(idx >= 0, idx & (hi_n - 1), -1)
        lo = lax.shift_right_logical(jnp.maximum(idx, 0), shift)
        hot = (lax.broadcasted_iota(jnp.int32, (hi_n, length), 0) == hi).astype(BF)
        cols = slice(f * EMB, (f + 1) * EMB)
        parts = [
            tab_ref[:, cols, j * hi_n : (j + 1) * hi_n].reshape(-1, hi_n) for j in range(tab_ref.shape[2] // hi_n)
        ]
        res = jnp.dot(jnp.concatenate(parts, axis=0), hot, preferred_element_type=F32)
        acc = res[0:EMB]
        for step in range(1, lo_n):
            acc = jnp.where(lo == step, res[step * EMB : (step + 1) * EMB], acc)
        out_ref[0, cols, :] = acc.astype(BF)


def lookup(idx, tab, hi_n, name, out_groups, order=lambda i: i):
    groups, fields, length = idx.shape
    outer, cols, inner = tab.shape
    lo_n = outer * inner // hi_n
    each = groups // out_groups
    return pl.pallas_call(
        functools.partial(lookup_kernel, lo_n, hi_n, fields),
        grid=(groups,),
        in_specs=[
            pl.BlockSpec((1, fields, length), lambda i: (order(i), 0, 0)),
            pl.BlockSpec(tab.shape, lambda i: (0, 0, 0)),
        ],
        out_specs=pl.BlockSpec((1, cols, length), lambda i: (i // each, 0, i % each)),
        out_shape=jax.ShapeDtypeStruct((out_groups, cols, length * each), BF),
        compiler_params=pltpu.CompilerParams(vmem_limit_bytes=VMEM),
        cost_estimate=pl.CostEstimate(
            flops=2 * groups * length * cols * lo_n * hi_n, bytes_accessed=8 * 2**20, transcendentals=0
        ),
        name=name,
    )(idx, tab)


def quarter_slots(slot_ref, q, field):
    half = slot_ref.shape[1] // 12
    parts = []
    for c in range(3):
        at = q * 3 * half + ((c + q % 2) % 3) * half
        at = at if isinstance(at, int) else pl.multiple_of(at, half)
        parts.append(slot_ref[pl.ds(field, 1), pl.ds(at, half)])
    return jnp.concatenate(parts, axis=1)


def place_one(idx_ref, grad_ref, out_ref, field):
    outer, _, inner = out_ref.shape
    length = grad_ref.shape[2]
    hi_n = 256
    lo_n = outer * inner // hi_n
    cols = pl.ds(pl.multiple_of(field * EMB, EMB), EMB)
    total = None
    for s in range(grad_ref.shape[0]):
        idx = quarter_slots(idx_ref, s, field)
        hi = idx & (hi_n - 1)
        lo = lax.shift_right_logical(idx, hi_n.bit_length() - 1)
        grad = grad_ref[s, cols, :]
        hot = (lax.broadcasted_iota(jnp.int32, (hi_n, length), 0) == hi).astype(BF)
        lhs = jnp.concatenate(
            [jnp.where(lo == step, grad, jnp.zeros_like(grad)) for step in range(lo_n)], axis=0
        )
        part = dot(lhs, hot, 1, 1)
        total = part if total is None else total + part
    total = total.astype(BF)
    each = inner // hi_n
    for i in range(outer * each):
        out_ref[i // each, cols, (i % each) * hi_n : (i % each + 1) * hi_n] = total[i * EMB : (i + 1) * EMB]


def place_kernel(idx_ref, grad_ref, out_ref):
    def one(field, _):
        place_one(idx_ref, grad_ref, out_ref, field)
        return 0

    lax.fori_loop(0, idx_ref.shape[0], one, 0)


def place(idx, grad, out_shape):
    return pl.pallas_call(
        place_kernel,
        out_shape=jax.ShapeDtypeStruct(out_shape, BF),
        compiler_params=pltpu.CompilerParams(vmem_limit_bytes=VMEM),
        name="place_rows",
    )(idx, grad)


def own_stats(feats_ref, mask_ref, out_ref, core):
    highest = lax.Precision.HIGHEST

    def block(c):
        at = pl.ds(pl.multiple_of(((c + core) % 3) * HALF, HALF), HALF)
        weight = jnp.broadcast_to(mask_ref[:, at].astype(F32), (8, HALF))
        return feats_ref[at, :], weight

    def total(weight, x):
        return jnp.dot(weight, x, preferred_element_type=F32, precision=highest)[0:1]

    for row, chunks in ((0, (0, 1)), (3, (2,))):
        count = sum(jnp.sum(block(c)[1][0:1], axis=1, keepdims=True) for c in chunks)
        mean = sum(total(block(c)[1], block(c)[0]) for c in chunks) / jnp.maximum(count, 1.0)
        off = lambda c: block(c)[0] - mean
        out_ref[row : row + 1, :] = mean
        out_ref[row + 1 : row + 2, :] = sum(total(block(c)[1], off(c) * off(c)) for c in chunks)
        out_ref[row + 2 : row + 3, :] = jnp.broadcast_to(count, mean.shape)


def stats_kernel(core_ref, feats_ref, mask_ref, out_ref):
    out_ref[...] = jnp.zeros_like(out_ref)
    own_stats(feats_ref, mask_ref, out_ref, core_ref[0])


def local_stats(core, feats, mask):
    return pl.pallas_call(
        stats_kernel,
        in_specs=[pl.BlockSpec(memory_space=pltpu.SMEM)] + [pl.BlockSpec(memory_space=pltpu.VMEM)] * 2,
        out_shape=jax.ShapeDtypeStruct((8, DENSE), F32),
        compiler_params=pltpu.CompilerParams(vmem_limit_bytes=VMEM),
        name="local_stats",
    )(core, feats, mask)


def front_kernel(
    groups, req_ref, table_ref, slot_ref, feats_ref, mask_ref, up_ref, down_ref, proj_ref,
    emb_ref, far_up, far_down, their_up, their_down, proj_out, every_ref,
    asked, found, received, ordered, both,
    req_send, req_recv, row_send, row_recv, near_send, near_recv, keep_sem,
    far_send, far_recv, side_send, own_send, own_recv, their_send, their_recv, proj_send, proj_recv,
    stat_send, stat_recv,
):
    wide, me = lax.axis_index("wide"), lax.axis_index("narrow")
    chip, core = me // 2, me % 2
    owners, fields, cap = req_ref.shape
    share = fields // groups
    parity = wide % 2
    near = [{"narrow": me + 1 - 2 * core}, {"narrow": me + 2 - 4 * chip}, {"narrow": 3 - me}]
    near_at = [me + 1 - 2 * core, me + 2 - 4 * chip, 3 - me]
    peers = [None] + [{"wide": (wide + d) % owners} for d in range(1, owners)]
    side = {"wide": wide + 1 - 2 * parity}
    barrier = pltpu.get_barrier_semaphore()
    for mate in near + peers[1:]:
        pl.semaphore_signal(barrier, inc=1, device_id=mate, device_id_type=MESH)
    pl.semaphore_wait(barrier, len(near) + len(peers) - 1)

    def remote(src, dst, send, recv, mate):
        return pltpu.make_async_remote_copy(
            src_ref=src, dst_ref=dst, send_sem=send, recv_sem=recv, device_id=mate, device_id_type=MESH
        )

    def req_copy(d):
        return remote(req_ref.at[(wide + d) % owners], asked.at[wide], req_send.at[d], req_recv.at[d], peers[d])

    for d in range(1, owners):
        req_copy(d).start()
    mine = pltpu.make_async_copy(req_ref.at[wide], asked.at[wide], keep_sem.at[0])
    mine.start()

    weights = ((up_ref, far_up, their_up), (down_ref, far_down, their_down))

    def far_copy(j, a):
        p = 2 * j + parity
        expert = jnp.where(j == 0, parity, 6 * (1 - chip) + p)
        return remote(weights[a][0].at[expert], weights[a][1].at[p], far_send.at[a, j], far_recv.at[a, p], near[1])

    def side_copy(p, a):
        view = weights[a][1].at[p]
        return remote(view, view, side_send.at[a, p // 2], far_recv.at[a, p], side)

    def own_copy(i, a):
        expert = jnp.where(i < 2, i, 6 * chip + jnp.where(i < 4, i + 4 * (1 - core), i))
        return remote(weights[a][0].at[expert], weights[a][2].at[0, i], own_send.at[a, i], own_recv.at[a, i], near[0])

    def their_copy(p, a):
        i = jnp.where(p < 6, p, p - 4)
        return remote(weights[a][1].at[p], weights[a][2].at[1, i], their_send.at[a, i], their_recv.at[a, i], near[0])

    def wanted(p):
        ends = jnp.logical_or(jnp.logical_and(p < 4, core == 1), jnp.logical_and(p >= 6, core == 0))
        return jnp.logical_or(jnp.logical_or(p < 2, jnp.logical_and(p >= 4, p < 6)), ends)

    def for_all(n, f):
        def body(i, _):
            for a in range(2):
                f(i, a)
            return 0

        lax.fori_loop(0, n, body, 0)


    for_all(4, lambda j, a: far_copy(j, a).start())

    def stat_core():
        return remote(both.at[pl.ds(0, 8)], both.at[pl.ds(8, 8)], stat_send.at[0], stat_recv.at[0], near[0])

    def stat_copy(d):
        return remote(both, every_ref.at[wide], stat_send.at[d], stat_recv.at[d], peers[d])

    both[0:8, :] = jnp.zeros((8, DENSE), F32)
    own_stats(feats_ref, mask_ref, both, core)
    stat_core().start()

    def proj_copy(i):
        return remote(proj_ref, proj_out.at[me], proj_send.at[i], proj_recv.at[i], near[i])

    keep_proj = pltpu.make_async_copy(proj_ref, proj_out.at[me], keep_sem.at[1])
    keep_proj.start()
    for i in range(3):
        proj_copy(i).start()
    for_all(6, lambda i, a: own_copy(i, a).start())
    stat_core().wait_recv()
    for d in range(1, owners):
        stat_copy(d).start()
    keep_stat = pltpu.make_async_copy(both, every_ref.at[wide], keep_sem.at[2])
    keep_stat.start()

    def far_step(j):
        p = 2 * j + parity
        for a in range(2):
            far_copy(j, a).wait_recv()
            side_copy(p, a).start()
        pass_on(p)

    def pass_on(p):
        @pl.when(wanted(p))
        def _():
            for a in range(2):
                their_copy(p, a).start()

    def side_step(j):
        p = 2 * j + 1 - parity
        for a in range(2):
            side_copy(p, a).wait_recv()
        pass_on(p)

    hi_n = 512
    lo_n = table_ref.shape[1] // hi_n

    def find(f, owner_idx):
        idx = asked[owner_idx, pl.ds(f, 1), :]
        hi = jnp.where(idx >= 0, idx & (hi_n - 1), -1)
        lo = lax.shift_right_logical(jnp.maximum(idx, 0), hi_n.bit_length() - 1)
        hot = (lax.broadcasted_iota(jnp.int32, (hi_n, cap), 0) == hi).astype(BF)
        cols = pl.ds(pl.multiple_of(f * EMB, EMB), EMB)
        part = jnp.concatenate([table_ref[cols, l * hi_n : (l + 1) * hi_n] for l in range(lo_n)], axis=0)
        res = jnp.dot(part, hot, preferred_element_type=F32)
        acc = res[0:EMB]
        for step in range(1, lo_n):
            acc = jnp.where(lo == step, res[step * EMB : (step + 1) * EMB], acc)
        return cols, acc.astype(BF)

    def group_rows(g):
        return pl.ds(pl.multiple_of(g * share * EMB, share * EMB), share * EMB)

    def row_copy(g, d, mate):
        rows = group_rows(g)
        return remote(
            found.at[(wide + d) % owners, rows], received.at[wide, rows], row_send.at[g, d], row_recv.at[g, d], mate
        )

    def look(g):
        def one(d, _):
            sender = (wide + d) % owners

            @pl.when(jnp.logical_and(g == 0, d > 0))
            def _():
                remote(req_ref.at[0], asked.at[sender], req_send.at[d], req_recv.at[owners - d], peers[1]).wait_recv()

            for k in range(share):
                cols, block = find(g * share + k, sender)

                @pl.when(d == 0)
                def _():
                    received[wide, cols, :] = block

                @pl.when(d > 0)
                def _():
                    found[sender, cols, :] = block

            @pl.when(d > 0)
            def _():
                row_copy(g, d, {"wide": sender}).start()

            return 0

        lax.fori_loop(0, owners, one, 0)

    hi_e = 256
    outer = owners * cap // hi_e

    def near_copy(g, i):
        rows = group_rows(g)
        return remote(
            ordered.at[near_at[i], rows], emb_ref.at[me, rows], near_send.at[g, i], near_recv.at[g, i], near[i]
        )

    def keep_copy(g):
        rows = group_rows(g)
        return pltpu.make_async_copy(ordered.at[me, rows], emb_ref.at[me, rows], keep_sem.at[3 + g])

    def order(g):
        def arrive(d, _):
            row_copy(g, d, {"wide": (wide + d) % owners}).wait_recv()
            return 0

        lax.fori_loop(1, owners, arrive, 0)
        tables = []
        for k in range(share):
            cols = pl.ds(pl.multiple_of((g * share + k) * EMB, EMB), EMB)
            parts = [
                received[o, cols, j * hi_e : (j + 1) * hi_e] for o in range(owners) for j in range(cap // hi_e)
            ]
            tables.append((cols, jnp.concatenate(parts, axis=0)))

        def quarter(q):
            for k, (cols, table) in enumerate(tables):
                idx = quarter_slots(slot_ref, q, g * share + k)
                hi = idx & (hi_e - 1)
                lo = lax.shift_right_logical(idx, hi_e.bit_length() - 1)
                hot = (lax.broadcasted_iota(jnp.int32, (hi_e, idx.shape[1]), 0) == hi).astype(BF)
                res = jnp.dot(table, hot, preferred_element_type=F32)
                acc = res[0:EMB]
                for step in range(1, outer):
                    acc = jnp.where(lo == step, res[step * EMB : (step + 1) * EMB], acc)
                ordered[q, cols, :] = acc.astype(BF)

        for i in (2, 1, 0):
            quarter(near_at[i])
            near_copy(g, i).start()
        quarter(me)
        keep_copy(g).start()

    mine.wait()

    def tick(t, _):
        @pl.when(t < groups)
        def _():
            look(t)

        @pl.when(jnp.logical_and(t >= 1, t < 5))
        def _():
            far_step(t - 1)

        @pl.when(t >= 2)
        def _():
            order(t - 2)

        @pl.when(t >= 3)
        def _():
            side_step(t - 3)

        return 0

    lax.fori_loop(0, groups + 2, tick, 0)

    for d in range(1, owners):
        req_copy(d).wait_send()
        stat_copy(d).wait()
    stat_core().wait_send()
    keep_stat.wait()
    keep_proj.wait()
    for i in range(3):
        proj_copy(i).wait()

    def rows_left(g, _):
        def one(d, _):
            row_copy(g, d, {"wide": (wide + d) % owners}).wait_send()
            return 0

        lax.fori_loop(1, owners, one, 0)
        for i in range(3):
            near_copy(g, i).wait()
        keep_copy(g).wait()
        return 0

    lax.fori_loop(0, groups, rows_left, 0)

    def weights_left(j, a):
        far_copy(j, a).wait_send()
        side_copy(2 * j + parity, a).wait_send()

    for_all(4, weights_left)
    for_all(6, lambda i, a: own_copy(i, a).wait())

    def passed(p, a):
        @pl.when(wanted(p))
        def _():
            their_copy(p, a).wait_send()

    for_all(8, passed)
    for_all(6, lambda i, a: their_copy(i, a).wait_recv())


def front(req, table, slots, feats, mask, up, down, proj, groups=5):
    owners, fields, cap = req.shape
    cols = fields * EMB
    quarters = 4
    rows = slots.shape[1] // quarters
    any_space, vmem = pl.BlockSpec(memory_space=pl.ANY), pl.BlockSpec(memory_space=pltpu.VMEM)
    dma = pltpu.SemaphoreType.DMA
    return pl.pallas_call(
        functools.partial(front_kernel, groups),
        in_specs=[vmem] * 5 + [any_space] * 3,
        out_specs=[any_space] * 7,
        out_shape=[
            jax.ShapeDtypeStruct((quarters, cols, rows), BF),
            jax.ShapeDtypeStruct((8,) + up.shape[1:], BF),
            jax.ShapeDtypeStruct((8,) + down.shape[1:], BF),
            jax.ShapeDtypeStruct((2, 6) + up.shape[1:], BF),
            jax.ShapeDtypeStruct((2, 6) + down.shape[1:], BF),
            jax.ShapeDtypeStruct((quarters,) + proj.shape, BF),
            jax.ShapeDtypeStruct((owners, 16, DENSE), F32),
        ],
        scratch_shapes=[
            pltpu.VMEM((owners, fields, cap), jnp.int32),
            pltpu.VMEM((owners, cols, cap), BF),
            pltpu.VMEM((owners, cols, cap), BF),
            pltpu.VMEM((quarters, cols, rows), BF),
            pltpu.VMEM((16, DENSE), F32),
            dma((owners,)),
            dma((owners,)),
            dma((groups, owners)),
            dma((groups, owners)),
            dma((groups, 3)),
            dma((groups, 3)),
            dma((3 + groups,)),
            dma((2, 4)),
            dma((2, 8)),
            dma((2, 4)),
            dma((2, 6)),
            dma((2, 6)),
            dma((2, 6)),
            dma((2, 6)),
            dma((3,)),
            dma((3,)),
            dma((owners,)),
            dma((owners,)),
        ],
        compiler_params=pltpu.CompilerParams(collective_id=1, has_side_effects=True, vmem_limit_bytes=VMEM),
        cost_estimate=pl.CostEstimate(flops=45 * 10**9, bytes_accessed=40 * 2**20, transcendentals=0),
        name="front",
    )(req, table, slots, feats, mask, up, down, proj)


def reduce_kernel(bits, with_rows, own_ref, extra_ref, *refs):
    if with_rows:
        slot_ref, grad_ref, out_ref, rep_ref, back_ref = refs[:5]
        grads, placed, near_send, near_recv, far_send, far_recv, keep_sem = refs[-7:]
        refs = refs[5:-7]
    else:
        out_ref, rep_ref = refs[:2]
        refs = refs[2:]
    acc, stage_buf, halves, got, local_sem, send, recv, rep_send, rep_recv, out_sem = refs
    wide=lax.axis_index("wide"); me=lax.axis_index("narrow")
    chip=me//2; core=me%2
    block=ROWS_U>>bits
    mates=[{"narrow": me+1-2*core},{"narrow": me+2-4*chip}]
    pairs=[{"wide": wide+(1<<k)*(1-2*((wide//(1<<k))%2))} for k in range(bits)]
    far={"narrow": 3-me}
    barrier=pltpu.get_barrier_semaphore()
    owners=1<<bits
    others=[{"wide": (wide+d)%owners} for d in range(1,owners)] if with_rows else pairs
    for mate in mates+[far]+others:
        pl.semaphore_signal(barrier, inc=1, device_id=mate, device_id_type=MESH)
    pl.semaphore_wait(barrier, len(others)+3)
    def power(k):
        return 1 << k, 1 << ((k + 1) % bits)

    def bit(u, k):
        here, there = power(k)
        return jnp.where(u == TURNED, (wide // there) % 2, (wide // here) % 2)

    def pair(u, k):
        here, there = power(k)
        step = jnp.where(u == TURNED, there, here)
        return {"wide": wide + step * (1 - 2 * bit(u, k))}

    def start_of(u, k):
        at = 0
        for j in range(k):
            at = at + bit(u, j) * (ROWS_U >> (j + 1))
        return pl.multiple_of(at, 16) if k else 0

    def copy(src, dst, s, u, mate):
        return pltpu.make_async_remote_copy(
            src_ref=src, dst_ref=dst, send_sem=send.at[s, u], recv_sem=recv.at[s, u], device_id=mate, device_id_type=MESH
        )

    def mine(u):
        return jnp.logical_or(u >= 4, jnp.where(u < 2, core == 0, core == 1))

    def theirs(u):
        return jnp.logical_or(u >= 4, jnp.where(u < 2, core == 1, core == 0))

    def domain_unit(u):
        return u < 6

    def local_at(u):
        return jnp.where(u < 2, u + 2, jnp.where(u < 6, u, u - 7))

    def core_copy(u, src):
        return copy(src, acc.at[u], 0, u, mates[0])

    def near_copy(u, src):
        return pltpu.make_async_copy(src, stage_buf.at[u % 2], local_sem.at[u % 2])

    def begin(u):
        @pl.when(u == 6)
        def _():
            core_copy(u, extra_ref.at[pl.ds(2, 2)]).start()
            near_copy(u, extra_ref.at[pl.ds(0, 2)]).start()

        @pl.when(jnp.logical_and(u != 6, mine(u)))
        def _():
            core_copy(u, own_ref.at[local_at(u), pl.ds(2, 2)]).start()
            near_copy(u, own_ref.at[local_at(u), pl.ds(0, 2)]).start()

    def add_region(u, sl, at, rows, src):
        tile = min(rows, 64)

        def body(i, _):
            r = pl.multiple_of(at + i * tile, 16)
            q = pl.multiple_of(i * tile, 16)
            for h in range(sl):
                a = acc[u, h, pl.ds(r, tile), :].astype(F32) + src[h, pl.ds(q, tile), :].astype(F32)
                acc[u, h, pl.ds(r, tile), :] = a.astype(BF)
            return 0

        lax.fori_loop(0, rows // tile, body, 0)

    half_at = [0]
    for k in range(bits):
        half_at.append(half_at[-1] + (ROWS_U >> (k + 1)))

    def half_view(u, k, parts):
        return halves.at[u, pl.ds(0, parts), pl.ds(half_at[k], ROWS_U >> (k + 1)), :]

    def send_half(u, k, parts):
        size = ROWS_U >> (k + 1)
        at = pl.multiple_of(start_of(u, k) + (1 - bit(u, k)) * size, 16)
        return copy(acc.at[u, pl.ds(0, parts), pl.ds(at, size), :], half_view(u, k, parts), 1 + k, u, pair(u, k))

    def take_half(u, k, parts):
        size = ROWS_U >> k
        copy(acc.at[u, pl.ds(0, parts), pl.ds(0, size), :], half_view(u, k - 1, parts), k, u, pair(u, k - 1)).wait_recv()
        add_region(u, parts, start_of(u, k), size, halves.at[u, :, pl.ds(half_at[k - 1], size), :])

    def y_whole(u):
        return copy(acc.at[u, 1], got.at[u, 1], bits + 1, u, mates[1])

    def y_block(u):
        at = start_of(u, bits)
        return copy(
            acc.at[u, 1, pl.ds(at, block), :], got.at[u, 1, pl.ds(at, block), :], bits + 1, u, mates[1]
        )

    def combine(u):
        @pl.when(theirs(u))
        def _():
            core_copy(u, acc.at[u]).wait_recv()

        @pl.when(mine(u))
        def _():
            near_copy(u, acc.at[u]).wait()
            sb = stage_buf.at[u % 2]

            @pl.when(theirs(u))
            def _():
                add_region(u, 2, 0, ROWS_U, sb)

            @pl.when(jnp.logical_not(theirs(u)))
            def _():
                def body(i, _):
                    r = pl.multiple_of(i * 64, 16)
                    for h in (0, 1):
                        acc[u, h, pl.ds(r, 64), :] = sb[h, pl.ds(r, 64), :]
                    return 0

                lax.fori_loop(0, ROWS_U // 64, body, 0)

    def grow_copy(u, j, parts):
        size = ROWS_U >> (j + 1)
        view = got.at[u, pl.ds(0, parts), pl.ds(start_of(u, j + 1), size), :]
        return copy(view, view, bits + 2 + (bits - 1 - j), u, pair(u, j))

    def out_copy(u, parts):
        return pltpu.make_async_copy(got.at[u, pl.ds(0, parts)], out_ref.at[u, pl.ds(0, parts)], out_sem.at[u])

    rep_mates = [mates[0], mates[1], far]
    rep_rows = rep_ref.shape[1]

    def rep_copy(i):
        return pltpu.make_async_remote_copy(
            src_ref=got.at[6, 0, pl.ds(0, rep_rows), :], dst_ref=rep_ref.at[i], send_sem=rep_send.at[i],
            recv_sem=rep_recv.at[i], device_id=rep_mates[i], device_id_type=MESH,
        )

    def by_kind(u, domain, shared):
        pl.when(domain_unit(u))(domain)
        pl.when(jnp.logical_not(domain_unit(u)))(shared)

    def start_grow(u):
        by_kind(u, lambda: grow_copy(u, bits - 1, 2).start(), lambda: grow_copy(u, bits - 1, 1).start())

    def stage_one(u):
        combine(u)
        by_kind(u, lambda: send_half(u, 0, 2).start(), lambda: y_whole(u).start())

    def halving(k, u):
        def domain():
            take_half(u, k, 2)
            if k < bits:
                send_half(u, k, 2).start()
            else:
                y_block(u).start()

        def shared():
            if k == 1:
                y_whole(u).wait_recv()
                add_region(u, 1, 0, ROWS_U, got.at[u, pl.ds(1, 1)])
            else:
                take_half(u, k - 1, 1)
            send_half(u, k - 1, 1).start()

        by_kind(u, domain, shared)

    def cross(u):
        at = start_of(u, bits)

        def domain():
            y_block(u).wait_recv()

        def shared():
            take_half(u, bits, 1)

        by_kind(u, domain, shared)
        got[u, 0, pl.ds(at, block), :] = acc[u, 0, pl.ds(at, block), :]
        start_grow(u)

    def grow(u, j):
        by_kind(u, lambda: grow_copy(u, j, 2).wait_recv(), lambda: grow_copy(u, j, 1).wait_recv())
        if j > 0:
            by_kind(u, lambda: grow_copy(u, j - 1, 2).start(), lambda: grow_copy(u, j - 1, 1).start())
        else:
            by_kind(u, lambda: out_copy(u, 2).start(), lambda: out_copy(u, 1).start())

            @pl.when(u == 6)
            def _():
                for i in range(3):
                    rep_copy(i).start()

    quarters=mates+[far]
    def quarter_at(i):
        return [me+1-2*core, me+2-4*chip, 3-me][i]
    def near_row_copy(i):
        return pltpu.make_async_remote_copy(src_ref=grad_ref.at[quarter_at(i)],dst_ref=grads.at[me],send_sem=near_send.at[i],recv_sem=near_recv.at[i],device_id=quarters[i],device_id_type=MESH)
    def keep_copy():
        return pltpu.make_async_copy(grad_ref.at[me],grads.at[me],keep_sem.at[0])
    def back_copy(d):
        return pltpu.make_async_remote_copy(src_ref=placed.at[(wide+d)%owners],dst_ref=back_ref.at[wide],send_sem=far_send.at[d],recv_sem=far_recv.at[d],device_id=others[d-1],device_id_type=MESH)
    def keep_back():
        return pltpu.make_async_copy(placed.at[wide],back_ref.at[wide],keep_sem.at[1])
    def place_field(f, _):
        place_one(slot_ref, grads, placed, f)
        return 0
    def row_step(t):
        fields=slot_ref.shape[0]
        @pl.when(t==ROW_AT)
        def _():
            keep_copy().wait()
            for i in range(3): near_row_copy(i).wait_recv()
        @pl.when(jnp.logical_and(t>=ROW_AT,t<ROW_AT+5))
        def _():
            lax.fori_loop((t-ROW_AT)*(fields//5),(t-ROW_AT+1)*(fields//5),place_field,0)
        for d in range(owners):
            @pl.when(t==ROW_AT+4+int(d*ROW_STEP))
            def _():
                if d==0: keep_back().start()
                else: back_copy(d).start()
    todo = [begin, stage_one]
    todo += [functools.partial(halving, k) for k in range(1, bits + 1)] + [cross]
    todo += [functools.partial(lambda j, u: grow(u, j), j) for j in reversed(range(bits))]
    plain_gaps = [0, 1, 2] + [1] * (len(todo) - 4) + [2]
    turned_gaps = [0, 1, 3, 4] + [1] * (len(todo) - 6) + [3, 3]
    plain_lag = [sum(plain_gaps[: i + 1]) for i in range(len(todo))]
    turned_lag = [sum(turned_gaps[: i + 1]) for i in range(len(todo))]

    def tick(t,_):
        for s in reversed(range(len(todo))):
            def stage(c, _):
                plain = t - plain_lag[s]
                u = jnp.where(c == 0, plain, TURNED)
                fits = jnp.logical_and(jnp.logical_and(plain >= 0, plain < UNITS), plain != TURNED)
                due = jnp.where(c == 0, fits, t == TURNED + turned_lag[s])

                @pl.when(due)
                def _():
                    todo[s](u)

                return 0

            lax.fori_loop(0, 2, stage, 0)
        if with_rows:
            row_step(t)
        return 0
    if with_rows:
        keep_copy().start()
        for i in range(3): near_row_copy(i).start()
    lax.fori_loop(0, max(UNITS + plain_lag[-1], TURNED + turned_lag[-1] + 1), tick, 0)
    if with_rows:
        keep_back().wait()
        for i in range(3): near_row_copy(i).wait_send()
        for d in range(1,owners): back_copy(d).wait()
    def finish(u,_):
        @pl.when(mine(u))
        def _():
            core_copy(u, acc.at[u]).wait_send()

        def left(parts):
            for k in range(bits):
                send_half(u, k, parts).wait_send()
            (y_block if parts == 2 else y_whole)(u).wait_send()
            for j in range(bits):
                grow_copy(u, j, parts).wait_send()
            out_copy(u, parts).wait()

        by_kind(u, lambda: left(2), lambda: left(1))
        return 0
    lax.fori_loop(0,UNITS,finish,0)
    for i in range(3):
        rep_copy(i).wait()

def reduce_all(own, extra, wide, rep_rows, rows=None):
    bits = wide.bit_length() - 1
    args = [own, extra]
    any_space = pl.BlockSpec(memory_space=pl.ANY)
    in_specs = [any_space] * 2
    out_shape = [
        jax.ShapeDtypeStruct((UNITS, 2, ROWS_U, LANES), BF),
        jax.ShapeDtypeStruct((3, rep_rows, LANES), BF),
    ]
    scratch = [
        pltpu.VMEM((UNITS, 2, ROWS_U, LANES), BF),
        pltpu.VMEM((2, 2, ROWS_U, LANES), BF),
        pltpu.VMEM((UNITS, 2, ROWS_U, LANES), BF),
        pltpu.VMEM((UNITS, 2, ROWS_U, LANES), BF),
        pltpu.SemaphoreType.DMA((2,)),
        pltpu.SemaphoreType.DMA((2 * bits + 2, UNITS)),
        pltpu.SemaphoreType.DMA((2 * bits + 2, UNITS)),
        pltpu.SemaphoreType.DMA((3,)),
        pltpu.SemaphoreType.DMA((3,)),
        pltpu.SemaphoreType.DMA((UNITS,)),
    ]
    if rows is not None:
        slots, grads, cap = rows
        args += [slots, grads]
        in_specs += [pl.BlockSpec(memory_space=pltpu.VMEM), any_space]
        back = (wide, grads.shape[1], cap)
        out_shape.append(jax.ShapeDtypeStruct(back, BF))
        scratch += [
            pltpu.VMEM(grads.shape, BF),
            pltpu.VMEM(back, BF),
            pltpu.SemaphoreType.DMA((3,)),
            pltpu.SemaphoreType.DMA((3,)),
            pltpu.SemaphoreType.DMA((wide,)),
            pltpu.SemaphoreType.DMA((wide,)),
            pltpu.SemaphoreType.DMA((2,)),
        ]
    return pl.pallas_call(
        functools.partial(reduce_kernel, bits, rows is not None),
        in_specs=in_specs,
        out_specs=[any_space] * len(out_shape),
        out_shape=out_shape,
        scratch_shapes=scratch,
        compiler_params=pltpu.CompilerParams(collective_id=0, has_side_effects=True, vmem_limit_bytes=VMEM),
        cost_estimate=pl.CostEstimate(flops=0, bytes_accessed=60 * 2**20, transcendentals=0),
        name="reduce_all",
    )(*args)


C0 = 0.7978845608028654
C1 = 0.044715
REP_ROWS = 512
GATE_AT = 256
GAIN_AT = 352
SHIFT_AT = 384
MISC_AT = 416


def gelu_both(x):
    square = x * x
    up = 0.5 * jnp.tanh(x * (square * (C0 * C1) + C0)) + 0.5
    act = x * up
    return act, up + (act - act * up) * (square * (6.0 * C0 * C1) + 2.0 * C0)


def soft_pair(a, b):
    top = jnp.maximum(a, b)
    ea, eb = jnp.exp(a - top), jnp.exp(b - top)
    total = ea + eb
    return ea / total, eb / total


def soft_pair_back(pa, pb, ga, gb):
    mean = pa * ga + pb * gb
    return pa * (ga - mean), pb * (gb - mean)


def fold(x):
    return sum(x[:, i * 128 : (i + 1) * 128] for i in range(x.shape[1] // 128))


def wide_lanes(x, n):
    return jnp.concatenate([x] * n, axis=1)


def split_low(x):
    high = x.astype(BF)
    return high, (x - high.astype(F32)).astype(BF)


def iota(shape, axis):
    return lax.broadcasted_iota(jnp.int32, shape, axis)


def row_of(rows, at):
    return (iota((rows, 128), 0) == at).astype(BF)


def dense_kernel(
    ids_ref, emb_ref, feats_ref, every_ref, mask_ref, label_ref, projw_ref, featw_ref, bias_ref,
    up_a, up_b, up_c, down_a, down_b, down_c, gain_ref, shift_ref, gate_f, gate_h, tin_f, tin_h,
    tower_ref,
    logit_ref, own_ref, emb_grad_ref, extra_ref,
    xt, act, slope, outs, og, ing, hid, hg, stat, inner, emb, feat, featw, gains, mixed, shifts, gates, tin,
    tbias, tout, tob, gain_acc, shift_acc, gate_acc, tin_acc, tbias_acc, tout_acc, tob_acc, emb_sem, extra_sem,
):
    ups = [up_a.at[0], up_b.at[0], up_c.at[0, 0], up_c.at[1, 0]]
    downs = [down_a.at[0], down_b.at[0], down_c.at[0, 0], down_c.at[1, 0]]
    step = pl.program_id(0)
    chunk, slot = step // 4, step % 4
    rows = xt.shape[1]
    core = ids_ref[14]
    owners = every_ref.shape[0]

    def expert_of(dom, k):
        return k if k < 2 else ids_ref[2 * dom + k]

    def raw_lanes(c):
        return pl.ds(pl.multiple_of(((c + core) % 3) * HALF, HALF), HALF)

    def pooled(sets):
        def sums(w, carry):
            total, mean = carry
            for at in sets:
                count = every_ref[w, at + 2 : at + 3, :]
                total, mean = total + count, mean + count * every_ref[w, at : at + 1, :]
            return total, mean

        zero = jnp.zeros((1, 128), F32)
        total, mean = lax.fori_loop(0, owners, sums, (zero, zero))
        mean = mean / total

        def squares(w, acc):
            for at in sets:
                off = every_ref[w, at : at + 1, :] - mean
                acc = acc + every_ref[w, at + 1 : at + 2, :] + every_ref[w, at + 2 : at + 3, :] * off * off
            return acc

        return mean, lax.rsqrt(lax.fori_loop(0, owners, squares, zero) / total + 1e-05)

    @pl.when(step == 0)
    def _():
        fetch = pltpu.make_async_copy(emb_ref, emb, emb_sem)
        fetch.start()
        for e in range(6):
            gains[e] = dot(gain_ref[...], row_of(14, ids_ref[e]), 0, 0).astype(BF)
        for dom, (gate, tower) in enumerate(((gate_f, tin_f), (gate_h, tin_h))):
            tin[dom] = tower[0]
            pick = (iota((16, 6), 0) % 8 == iota((16, 6), 1)).astype(BF)
            gates[dom] = dot(pick, gate[0], 1, 0).astype(BF)
            place = iota((16, 14), 0)
            ident = place % 4
            for k in range(4):
                ident = jnp.where(place % 4 == k, expert_of(dom, k), ident)
            same = ident == iota((16, 14), 1)
            first, second = jnp.logical_and(same, place < 4), jnp.logical_and(same, place < 8)
            third = jnp.logical_and(second, place >= 4)
            mixed[dom] = (
                dot(first.astype(BF), gain_ref[...], 1, 0) + dot(third.astype(BF), shift_ref[...], 1, 0)
            ).astype(BF)
            shifts[dom] = dot(second.astype(BF), shift_ref[...], 1, 0).astype(BF)
            d = ids_ref[12 + dom]
            tbias[dom] = dot(tower_ref[...], row_of(16, d), 0, 0)
            tout[dom] = dot(tower_ref[...], row_of(16, 6 + d), 0, 0)
            tob[dom] = dot(tower_ref[...], row_of(128, d), 1, 0)
        featw[0:128, :] = featw_ref[...]
        featw[128:144, :] = jnp.where(iota((16, D), 0) == 0, bias_ref[...].astype(F32), 0.0).astype(BF)
        feat[128:144, :] = (iota((16, rows), 0) == 0).astype(BF)
        moments = [pooled((0,)), pooled((3, 11))]
        for c in range(rows // HALF):
            mean, scale = moments[c // 2]
            x = (feats_ref[raw_lanes(c), :] - mean) * scale
            feat[0:128, c * HALF : (c + 1) * HALF] = x.T.astype(BF)
        for ref in (gain_acc, shift_acc, gate_acc, tin_acc, tbias_acc, tout_acc, tob_acc):
            ref[...] = jnp.zeros_like(ref)
        fetch.wait()
        for c in range(rows // HALF):
            cols = slice(c * HALF, (c + 1) * HALF)
            x = dot(projw_ref[...], emb[:, cols], 0, 0) + dot(featw[...], feat[:, cols], 0, 0)
            xt[:, cols] = x.astype(BF)

    @pl.when(step < 12)
    def _():
        lanes = pl.ds(pl.multiple_of(chunk * HALF, HALF), HALF)

        def piece(s):
            pre = dot(ups[s][...], xt[:, lanes], 0, 0)
            a, g = gelu_both(pre)
            a = a.astype(BF)
            act[slot, s, :, lanes] = a
            slope[slot, s, :, lanes] = g.astype(BF)
            return dot(downs[s][...], a, 0, 0)

        outs[slot] = piece(0)
        for s in range(1, 4):
            outs[slot] += piece(s)

    def middle():
        lanes = pl.ds(pl.multiple_of(chunk * HALF, HALF), HALF)
        dom = chunk // 2
        x = xt[:, lanes]
        logit_gates = dot(gates[dom], x, 1, 0)
        s0, s1 = soft_pair(logit_gates[0:1], logit_gates[1:2])
        d0, d1 = soft_pair(logit_gates[2:3], logit_gates[3:4])
        t0, t1 = soft_pair(logit_gates[4:5], logit_gates[5:6])
        coef = jnp.concatenate([t0 * s0, t0 * s1, t1 * d0, t1 * d1], axis=0)
        high = coef.astype(BF).astype(F32)
        spare = jnp.zeros((8, HALF), F32)
        coef_low = jnp.concatenate([high, coef - high, spare], axis=0).astype(BF)
        hg[...] = dot(shifts[dom], coef_low, 0, 0)
        stat[8:12, :] = coef
        expert = [0, 1, 2 + 2 * dom, 3 + 2 * dom]

        def normalize(t, _):
            cols = pl.ds(pl.multiple_of(t * 128, 128), 128)
            for k in range(4):
                v = outs[k, :, cols]
                mean = jnp.sum(v, axis=0, keepdims=True) * (1.0 / D)
                v = v - mean
                var = jnp.sum(v * v, axis=0, keepdims=True) * (1.0 / D)
                stat[k : k + 1, cols] = mean
                stat[4 + k : 5 + k, cols] = lax.rsqrt(var + 1e-05)
            scale = [stat[4 + k : 5 + k, cols] * stat[8 + k : 9 + k, cols] for k in range(4)]
            for r in range(4):
                band = slice(r * 128, (r + 1) * 128)
                acc = hg[band, cols]
                for k in range(4):
                    n = (outs[k, band, cols] - stat[k : k + 1, cols]) * scale[k]
                    acc = acc + n * gains[expert[k], band, :].astype(F32)
                hid[band, cols] = acc.astype(BF)
            return 0

        lax.fori_loop(0, 4, normalize, 0)
        h = hid[...]
        pre = dot(tin[dom], h, 0, 0) + wide_lanes(tbias[dom], 4)
        tact, tslope = gelu_both(pre)
        weight = wide_lanes(tout[dom], 4)
        logit = jnp.sum(tact * weight, axis=0, keepdims=True) + wide_lanes(tob[dom, 12:13, :], 4)
        logit_ref[:, raw_lanes(chunk)] = logit
        live, label = mask_ref[:, raw_lanes(chunk)].astype(F32), label_ref[:, raw_lanes(chunk)].astype(F32)
        grad = (jax.nn.sigmoid(logit) - label) * live
        tob_acc[dom, 0:1, :] += fold(grad)
        tout_acc[dom] += fold(grad * tact)
        low = (grad * weight * tslope).astype(BF)
        tbias_acc[dom] += fold(low.astype(F32))
        tin_acc[dom] += dot(h, low, 1, 1)
        back = dot(tin[dom], low, 1, 0)
        hg[...] = back
        back_high, back_low = split_low(back)
        shift_acc[dom] += dot(back_high, coef_low, 1, 1) + dot(back_low, coef_low, 1, 1)
        inner[...] = dot(mixed[dom], back_high, 1, 0) + dot(mixed[dom], back_low, 1, 0)

        def denormalize(t, _):
            cols = pl.ds(pl.multiple_of(t * 128, 128), 128)
            place = pl.ds(pl.multiple_of(chunk * HALF + t * 128, 128), 128)
            for k in range(4):
                mean, rstd = stat[k : k + 1, cols], stat[4 + k : 5 + k, cols]
                c = stat[8 + k : 9 + k, cols]
                m2 = 0.0
                for r in range(4):
                    band = slice(r * 128, (r + 1) * 128)
                    w = (outs[k, band, cols] - mean) * rstd * hg[band, cols]
                    m2 = m2 + jnp.sum(w * gains[expert[k], band, :].astype(F32), axis=0, keepdims=True)
                    gain_acc[expert[k], band, :] += w * c
                m1 = inner[k : k + 1, cols]
                inner[4 + k : 5 + k, cols] += m2
                cr = c * rstd
                slant = cr * rstd * m2 * (1.0 / D)
                level = mean * slant - cr * m1 * (1.0 / D)
                for r in range(4):
                    band = slice(r * 128, (r + 1) * 128)
                    scaled = hg[band, cols] * gains[expert[k], band, :].astype(F32)
                    og[k, band, place] = (scaled * cr - outs[k, band, cols] * slant + level).astype(BF)
            return 0

        lax.fori_loop(0, 4, denormalize, 0)
        a = [inner[4 + k : 5 + k, :] for k in range(4)]
        g0, g1 = soft_pair_back(s0, s1, t0 * a[0], t0 * a[1])
        g2, g3 = soft_pair_back(d0, d1, t1 * a[2], t1 * a[3])
        g4, g5 = soft_pair_back(t0, t1, s0 * a[0] + s1 * a[1], d0 * a[2] + d1 * a[3])
        zero = jnp.zeros_like(g0)
        g = jnp.concatenate([g0, g1, g2, g3, g4, g5, zero, zero], axis=0)
        high = g.astype(BF).astype(F32)
        g = jnp.concatenate([high, g - high], axis=0).astype(BF)
        gate_acc[dom] += dot(g, x, 1, 1)
        ing[:, lanes] = dot(gates[dom], g, 0, 0)

    @pl.when(jnp.logical_and(step < 12, slot == 3))
    def _():
        middle()

    def back(k, at, n):
        lanes = slice(at, at + n)
        for s in range(4):
            p = dot(downs[s][...], og[k, :, lanes], 1, 0) * slope[k, s, :, lanes].astype(F32)
            slope[k, s, :, lanes] = p.astype(BF)

        def piece(s, _):
            grad, p = og[k, :, lanes], slope[k, s, :, lanes]
            own_ref[0, s, 0:D, :] = dot(xt[:, lanes], p, 1, 1).astype(BF)
            d = dot(act[k, s, :, lanes], grad, 1, 1).astype(BF)
            own_ref[0, s, D : D + 256, :] = d[:, 0:256]
            own_ref[0, s, D + 256 : D + 512, :] = d[:, 256:512]
            return 0

        lax.fori_loop(0, 4, piece, 0)

        def grow(t, _):
            cols = pl.ds(pl.multiple_of(at + t * HALF, HALF), HALF)
            total = dot(ups[0][...], slope[k, 0, :, cols], 1, 0)
            for s in range(1, 4):
                total += dot(ups[s][...], slope[k, s, :, cols], 1, 0)
            ing[:, cols] += total
            return 0

        lax.fori_loop(0, n // HALF, grow, 0)

    expert = step - 12

    @pl.when(jnp.logical_and(expert >= 0, expert < 2))
    def _():
        back(expert, 0, rows)

    @pl.when(jnp.logical_and(expert >= 2, expert < 4))
    def _():
        back(expert, 0, DSLOT)

    @pl.when(expert >= 4)
    def _():
        back(expert - 2, DSLOT, rows - DSLOT)

    def exact(select, x):
        high, low = split_low(x)
        return dot(select, high, 1, 1) + dot(select, low, 1, 1)

    @pl.when(expert == 5)
    def _():
        low = ing[...].astype(BF)
        proj = dot(emb[...], low, 1, 1).astype(BF)
        feat_grad = dot(feat[...], low, 1, 1)
        for c in range(rows // HALF):
            cols = slice(c * HALF, (c + 1) * HALF)
            emb[:, cols] = dot(projw_ref[...], low[:, cols], 1, 0).astype(BF)
        put = pltpu.make_async_copy(emb, emb_grad_ref, emb_sem)
        put.start()
        unit = act.at[:, :, :, 0:256]
        act[:, :, :, 0:256] = jnp.zeros((4, 4, 256, 256), BF)
        spots = [ids_ref[15 + q] for q in range(4)]
        for q in range(4):
            part = proj[q * 160 : (q + 1) * 160]
            act[spots[q], 2, 0:160, 0:256] = part[:, 0:256]
            act[spots[q], 2, 160:256, 0:256] = part[0:96, 256:512]
            act[spots[q], 3, 0:64, 0:256] = part[96:160, 256:512]
        for dom in range(2):
            d = ids_ref[12 + dom]
            tower = tin_acc[dom].astype(BF)
            act[ids_ref[15 + d // 2], d % 2, :, 0:128] = tower[0:256]
            act[ids_ref[15 + d // 2], d % 2, :, 128:256] = tower[256:512]
            g = gate_acc[dom]
            g = g[0:8] + g[8:16]
            place = pl.ds(pl.multiple_of(d * 16, 16), 16)
            act[spots[3], 1, place, 0:256] = jnp.concatenate([g[:, 0:256], g[:, 256:512]], axis=0).astype(BF)
        act[spots[3], 0, 0:128, 0:256] = feat_grad[0:128, 0:256].astype(BF)
        act[spots[3], 0, 128:256, 0:256] = feat_grad[0:128, 256:512].astype(BF)
        total = 0.0
        for e in range(6):
            total = total + exact(row_of(16, ids_ref[e]), gain_acc[e])
        offset = 0.0
        misc_a = misc_b = 0.0
        line = iota((16, 128), 0)
        lane = iota((16, 128), 1)
        for dom in range(2):
            col = iota((16, 16), 1)
            ident = col % 4
            for k in range(4):
                ident = jnp.where(col % 4 == k, expert_of(dom, k), ident)
            choose = jnp.logical_and(ident == iota((16, 16), 0), col < 8).astype(BF)
            offset = offset + exact(choose, shift_acc[dom])
            d = ids_ref[12 + dom]
            misc_a = misc_a + exact(row_of(16, d), tbias_acc[dom])
            misc_b = misc_b + exact(row_of(16, d), tout_acc[dom])
            bias = jnp.sum(tob_acc[dom, 0:1, :], axis=1, keepdims=True)
            misc_a = misc_a + jnp.where(jnp.logical_and(line == 8, lane == d), bias, 0.0)
        misc = jnp.concatenate([misc_a, misc_b], axis=1)
        line = iota((16, 256), 0)
        misc = misc + jnp.where(line == 6, feat_grad[128:129, 0:256], 0.0)
        misc = misc + jnp.where(line == 7, feat_grad[128:129, 256:512], 0.0)
        for at, x in ((GAIN_AT, total), (SHIFT_AT, offset)):
            act[spots[3], 1, at - 256 : at - 240, 0:256] = x[:, 0:256].astype(BF)
            act[spots[3], 1, at - 240 : at - 224, 0:256] = x[:, 256:512].astype(BF)
        act[spots[3], 1, MISC_AT - 256 : MISC_AT - 240, 0:256] = misc.astype(BF)
        out = pltpu.make_async_copy(unit, extra_ref, extra_sem)
        out.start()
        out.wait()
        put.wait()


def dense(ids, emb, feats, every, mask, label, projw, featw, bias, ups, downs, gains, shifts, gate, tin, tower):
    rows = emb.shape[1]

    def ahead(i):
        c, j = i // 4, i % 4
        front = jnp.where(j < 2, j, jnp.where(c < 2, j, j + 2))
        return jnp.where(i < 12, front, i - 12)

    def whole(x):
        return pl.BlockSpec(x.shape, lambda i, ids: (0,) * len(x.shape), pipeline_mode=pl.Buffered(1))

    any_space = pl.BlockSpec(memory_space=pl.ANY)
    in_specs = [any_space] + [whole(x) for x in (feats, every, mask, label, projw, featw, bias)]
    for group in (ups, downs):
        block = group[0].shape[1:]
        in_specs += [
            pl.BlockSpec((1,) + block, lambda i, ids: (ids[ahead(i)], 0, 0)),
            pl.BlockSpec((1,) + block, lambda i, ids: (ids[6 + ahead(i)], 0, 0)),
            pl.BlockSpec((2, 1) + block, lambda i, ids: (0, ahead(i), 0, 0)),
        ]
    in_specs += [whole(gains), whole(shifts)]
    for x in (gate, tin):
        for dom in range(2):
            in_specs.append(
                pl.BlockSpec(
                    (1,) + x.shape[1:], lambda i, ids, at=12 + dom: (ids[at], 0, 0), pipeline_mode=pl.Buffered(1)
                )
            )
    in_specs.append(whole(tower))
    return pl.pallas_call(
        dense_kernel,
        grid_spec=pltpu.PrefetchScalarGridSpec(
            num_scalar_prefetch=1,
            grid=(18,),
            in_specs=in_specs,
            out_specs=[
                pl.BlockSpec((1, rows), lambda i, ids: (0, 0)),
                pl.BlockSpec((1, 4, 2 * D, 256), lambda i, ids: (jnp.maximum(i - 12, 0), 0, 0, 0)),
                any_space,
                any_space,
            ],
            scratch_shapes=[
                pltpu.VMEM((D, rows), BF),
                pltpu.VMEM((4, 4, 256, rows), BF),
                pltpu.VMEM((4, 4, 256, rows), BF),
                pltpu.VMEM((4, D, HALF), F32),
                pltpu.VMEM((4, D, rows), BF),
                pltpu.VMEM((D, rows), F32),
                pltpu.VMEM((D, HALF), BF),
                pltpu.VMEM((D, HALF), F32),
                pltpu.VMEM((16, HALF), F32),
                pltpu.VMEM((16, HALF), F32),
                pltpu.VMEM(emb.shape, BF),
                pltpu.VMEM((144, rows), BF),
                pltpu.VMEM((144, D), BF),
                pltpu.VMEM((6, D, 128), BF),
                pltpu.VMEM((2, 16, D), BF),
                pltpu.VMEM((2, 16, D), BF),
                pltpu.VMEM((2, 16, D), BF),
                pltpu.VMEM((2, D, 128), BF),
                pltpu.VMEM((2, 128, 128), F32),
                pltpu.VMEM((2, 128, 128), F32),
                pltpu.VMEM((2, 16, 128), F32),
                pltpu.VMEM((6, D, 128), F32),
                pltpu.VMEM((2, D, 16), F32),
                pltpu.VMEM((2, 16, D), F32),
                pltpu.VMEM((2, D, 128), F32),
                pltpu.VMEM((2, 128, 128), F32),
                pltpu.VMEM((2, 128, 128), F32),
                pltpu.VMEM((2, 8, 128), F32),
                pltpu.SemaphoreType.DMA,
                pltpu.SemaphoreType.DMA,
            ],
        ),
        out_shape=[
            jax.ShapeDtypeStruct((1, rows), F32),
            jax.ShapeDtypeStruct((6, 4, 2 * D, 256), BF),
            jax.ShapeDtypeStruct(emb.shape, BF),
            jax.ShapeDtypeStruct((4, 4, 256, 256), BF),
        ],
        compiler_params=pltpu.CompilerParams(vmem_limit_bytes=62 * 2**20),
        cost_estimate=pl.CostEstimate(flops=39 * 10**9, bytes_accessed=60 * 2**20, transcendentals=0),
        name="dense_all",
    )(ids, emb, feats, every, mask, label, projw, featw, bias, *ups, *downs, gains, shifts, gate, gate, tin, tin, tower)


def finish_kernel(with_rows, ids_ref, sums_ref, unit_ref, others_ref, *refs):
    if with_rows:
        back_ref, row_ref = refs[0], refs[1]
        refs = refs[2:]
    (up_ref, down_ref, proj_ref, feat_ref, bias_ref, gain_ref, shift_ref, gate_ref, tin_ref, tbias_ref,
     tout_ref, tob_ref, quarters) = refs
    step = pl.program_id(0)
    up_ref[0] = sums_ref[0, 0, 0:D, :].astype(F32)
    down_ref[0, :, 0:256] = sums_ref[0, 0, D : D + 256, :].astype(F32)
    down_ref[0, :, 256:512] = sums_ref[0, 0, D + 256 : D + 512, :].astype(F32)
    if with_rows:
        @pl.when(step < with_rows)
        def _():
            row_ref[0, 0] = back_ref[0].astype(F32)

    @pl.when(step == 0)
    def _():
        me = ids_ref[14]
        quarters[me] = unit_ref[0, 0, 0:REP_ROWS, :].astype(F32)
        for i in range(3):
            quarters[ids_ref[15 + i]] = others_ref[i].astype(F32)
        cols = proj_ref.shape[0]
        proj_ref[:, 0:256] = unit_ref[0, 0, REP_ROWS : REP_ROWS + cols, :].astype(F32)
        proj_ref[:, 256:512] = unit_ref[0, 0, REP_ROWS + cols : REP_ROWS + 2 * cols, :].astype(F32)
        for d in range(DOMAINS):
            band = slice((d % 2) * 256, (d % 2) * 256 + 256)
            tin_ref[d, 0:256, :] = quarters[d // 2, band, 0:128]
            tin_ref[d, 256:512, :] = quarters[d // 2, band, 128:256]
            g = quarters[3, GATE_AT + 16 * d : GATE_AT + 16 * d + 16, :]
            g = jnp.concatenate([g[0:8], g[8:16]], axis=1)
            gate_ref[d] = g[0:6]
        feat_ref[:, 0:256] = quarters[3, 0:128, :]
        feat_ref[:, 256:512] = quarters[3, 128:256, :]
        for at, ref in ((GAIN_AT, gain_ref), (SHIFT_AT, shift_ref)):
            ref[:, 0:256] = quarters[3, at : at + 14, :]
            ref[:, 256:512] = quarters[3, at + 16 : at + 30, :]
        tbias_ref[...] = quarters[3, MISC_AT : MISC_AT + 6, 0:128]
        tout_ref[...] = quarters[3, MISC_AT : MISC_AT + 6, 128:256]
        bias_ref[:, 0:256] = quarters[3, MISC_AT + 6 : MISC_AT + 7, :]
        bias_ref[:, 256:512] = quarters[3, MISC_AT + 7 : MISC_AT + 8, :]
        tob_ref[...] = quarters[3, MISC_AT + 8 : MISC_AT + 9, 0:128]


def finish(ids, sums, others, proj_cols, back=None):
    def whole(s):
        return pl.BlockSpec(s, lambda i, ids: (0,) * len(s))

    def unit(i, ids):
        return (ids[i] % 16, ids[i] // 16, 0, 0)

    in_specs = [
        pl.BlockSpec((1, 1, ROWS_U, LANES), unit),
        pl.BlockSpec((1, 1, ROWS_U, LANES), lambda i, ids: (6, 0, 0, 0)),
        whole(others.shape),
    ]
    args = [sums, sums, others]
    shapes = [
        (14, D, 256), (14, 256, D), (proj_cols, D), (DENSE, D), (1, D), (14, D), (14, D), (DOMAINS, 6, D),
        (DOMAINS, D, 128), (DOMAINS, 128), (DOMAINS, 128), (1, 128),
    ]
    out_specs = [
        pl.BlockSpec((1, D, 256), lambda i, ids: (i, 0, 0)),
        pl.BlockSpec((1, 256, D), lambda i, ids: (i, 0, 0)),
    ] + [whole(s) for s in shapes[2:]]
    if back is not None:
        blocks, cols, cap = back.shape
        last = lambda i: jnp.minimum(i, blocks - 1)
        args.append(back)
        in_specs.append(pl.BlockSpec((1, cols, cap), lambda i, ids: (last(i), 0, 0)))
        shapes.insert(0, (1, blocks, cols, cap))
        out_specs.insert(0, pl.BlockSpec((1, 1, cols, cap), lambda i, ids: (0, last(i), 0, 0)))
    return pl.pallas_call(
        functools.partial(finish_kernel, 0 if back is None else back.shape[0]),
        grid_spec=pltpu.PrefetchScalarGridSpec(
            num_scalar_prefetch=1,
            grid=(14,),
            in_specs=in_specs,
            out_specs=out_specs,
            scratch_shapes=[pltpu.VMEM((4, REP_ROWS, LANES), F32)],
        ),
        out_shape=[jax.ShapeDtypeStruct(s, F32) for s in shapes],
        compiler_params=pltpu.CompilerParams(vmem_limit_bytes=VMEM),
        cost_estimate=pl.CostEstimate(flops=0, bytes_accessed=32 * 2**20, transcendentals=0),
        name="finish",
    )(ids, *args)


def shards(
    embed_table,
    requests,
    slot_index,
    event_mask,
    labels,
    dense_feats,
    proj_weight,
    dense_weight,
    proj_bias,
    up_weight,
    down_weight,
    norm_gain,
    norm_shift,
    gate_weight,
    tower_in,
    tower_bias,
    tower_out,
    tower_out_bias,
):
    narrow = lax.axis_size("narrow")
    me = lax.axis_index("narrow")
    chip, core = me // 2, me % 2
    ev_rows, fields = slot_index.shape
    rows = ev_rows // narrow
    owners, cap = requests.shape[1], requests.shape[2]
    hid_here = up_weight.shape[2]
    other_chip = [(i, i ^ 2) for i in range(narrow)]
    other_core = [(i, i ^ 1) for i in range(narrow)]
    full = 3 * chip + 2 * core
    half = 3 * chip + 1

    def swap(x, pairs):
        return lax.ppermute(x, "narrow", pairs)

    def chip_experts(w, which):
        return jnp.concatenate(
            [w[:SHARED], lax.dynamic_slice_in_dim(w, SHARED + 6 * which, 6, axis=0)], axis=0
        )

    def bring(w):
        far = swap(chip_experts(w, 1 - chip), other_chip)
        at = lambda x, start, size: lax.dynamic_slice_in_dim(x, start, size, axis=0)
        base = SHARED + 6 * chip
        away = 4 * (1 - core)
        theirs = jnp.stack(
            [
                jnp.concatenate([w[:SHARED], at(w, base + away, 2), at(w, base + 2, 2)], axis=0),
                jnp.concatenate([far[:SHARED], at(far, 2 + away, 2), far[4:6]], axis=0),
            ]
        )
        return w, far, swap(theirs, other_core)

    six = jnp.arange(6, dtype=jnp.int32)
    spot = jnp.where(six < 2, six, jnp.where(six < 4, six + 4 * core, six))
    offset = jnp.arange(narrow, dtype=jnp.int32)
    offset = jnp.where(chip == 1, (offset + 2) % 4, offset)
    offset = jnp.where(core == 1, offset + 1 - 2 * (offset % 2), offset)
    ids = jnp.concatenate(
        [
            jnp.where(six < 2, six, spot + 6 * chip),
            spot,
            jnp.stack([full, half, core]),
            (offset % 2) * 2 + offset // 2,
        ]
    ).astype(jnp.int32)
    mask_row, label_row = event_mask[None], labels[None]

    turn = lambda i: (i // 3) * 3 + (i % 3 + (i // 3) % 2) % 3
    table_rows = embed_table.shape[0]
    cols = fields * EMB
    blocks = ev_rows // HALF
    hi_n = 256
    lo_n = ev_rows // hi_n
    direct = cap % hi_n == 0
    asked = requests[0].transpose(0, 2, 1)
    if direct:
        embedded, far_up, far_down, their_up, their_down, proj_full, every = front(
            asked, embed_table.T, slot_index.T, dense_feats, mask_row, up_weight, down_weight, proj_weight
        )
        ups, downs = (up_weight, far_up, their_up), (down_weight, far_down, their_down)
    else:
        asked = lax.all_to_all(asked, "wide", 0, 0, tiled=True)
        ups, downs = bring(up_weight), bring(down_weight)
        proj_full = lax.all_gather(proj_weight, "narrow", axis=0)
        stats = local_stats(core[None], dense_feats, mask_row)
        stats = jnp.concatenate([stats, swap(stats, other_core)], axis=0)
        every = lax.all_to_all(
            jnp.broadcast_to(stats, (owners,) + stats.shape), "wide", 0, 0, tiled=True
        )
        tab = embed_table.reshape(32, table_rows // 32, cols).transpose(0, 2, 1)
        flat = asked.transpose(1, 0, 2).reshape(fields, DOMAINS, DSLOT).transpose(1, 0, 2)
        found = lookup(flat, tab, table_rows // 32, "lookup_rows", DOMAINS)
        found = found.transpose(1, 0, 2).reshape(cols, owners, cap).transpose(1, 0, 2)
        received = lax.all_to_all(found, "wide", 0, 0, tiled=True)
        received = received.transpose(1, 0, 2).reshape(cols, lo_n, hi_n).transpose(1, 0, 2)
        slots = slot_index.reshape(blocks, HALF, fields).transpose(0, 2, 1)
        embedded = lookup(slots, received, hi_n, "order_rows", narrow, turn)
        embedded = lax.all_to_all(embedded, "narrow", 0, 0, tiled=True)
    embedded = embedded.reshape(narrow * cols, rows)
    proj_full = proj_full.reshape(narrow * cols, D)

    tower = jnp.concatenate(
        [tower_bias, tower_out, jnp.pad(tower_out_bias[None], ((0, 3), (0, 128 - DOMAINS)))], axis=0
    )
    logits, own, embed_grad, extra = dense(
        ids, embedded, dense_feats, every, mask_row, label_row, proj_full, dense_weight, proj_bias[None],
        ups, downs, norm_gain, norm_shift, gate_weight.transpose(0, 2, 1), tower_in, tower,
    )
    extra = extra.reshape(narrow, ROWS_U, LANES)

    embed_grad = embed_grad.reshape(narrow, cols, rows)
    if not direct:
        embed_grad = lax.all_to_all(embed_grad, "narrow", 0, 0, tiled=True)
        returned = place(slot_index.T, embed_grad, (lo_n, cols, hi_n))
        returned = returned.transpose(1, 0, 2).reshape(cols, owners, cap).transpose(1, 0, 2)
        row_grads = lax.all_to_all(returned, "wide", 0, 0, tiled=True)

    if direct:
        sums, others, row_grads = reduce_all(own, extra, owners, REP_ROWS, (slot_index.T, embed_grad, cap))
    else:
        sums, others = reduce_all(own, extra, owners, REP_ROWS)
    expert = jnp.arange(14, dtype=jnp.int32)
    domain = (expert - SHARED) // DOM_EXP
    unit = jnp.where(domain % 3 == 0, 0, jnp.where(domain % 3 == 1, 4, 2)) + expert % 2
    away = jnp.where(domain // 3 == chip, 0, 16)
    unit = jnp.where(expert < SHARED, expert + 7, unit + away)
    marks = jnp.concatenate([unit, jnp.stack([me, me + 1 - 2 * core, me + 2 - 4 * chip, 3 - me])])
    outs = finish(marks.astype(jnp.int32), sums, others, cols, row_grads if direct else None)
    if not direct:
        outs = [row_grads.astype(F32)[None]] + list(outs)
    (row_grads, up_grad, down_grad, proj_grad, feat_grad, bias_grad, gain_grad, shift_grad, gate_grad, tower_grad,
     tower_bias_grad, tower_out_grad, out_bias_grad) = outs
    return (
        logits[0],
        row_grads.transpose(0, 1, 3, 2),
        proj_grad,
        feat_grad,
        bias_grad[0],
        up_grad,
        down_grad,
        gain_grad,
        shift_grad,
        gate_grad.transpose(0, 2, 1),
        tower_grad,
        tower_bias_grad,
        tower_out_grad,
        out_bias_grad[0, :DOMAINS],
    )


def solution(mesh):
    placed = (
        P("wide", "narrow"),
        P("wide", None, None, "narrow"),
        P("wide", "narrow"),
        P(("wide", "narrow")),
        P(("wide", "narrow")),
        P(("wide", "narrow"), None),
        P("narrow", None),
        P(),
        P(),
        P(None, None, "narrow"),
        P(None, "narrow", None),
        P(),
        P(),
        P(),
        P(),
        P(),
        P(),
        P(),
    )
    return jax.shard_map(
        shards,
        mesh=mesh,
        in_specs=placed,
        out_specs=(
            P(("wide", "narrow")),
            P("wide", None, None, "narrow"),
            P("narrow", None),
            P(),
            P(),
            P(None, None, "narrow"),
            P(None, "narrow", None),
            P(),
            P(),
            P(),
            P(),
            P(),
            P(),
            P(),
        ),
        check_vma=False,
    )
```

time: 524 us -> 435 us (0.83)
  local copies, waits for them, and re-layouts: 40.2 us -> 6.65 us
  other arithmetic: 33.1 us -> 1.28 us
  Pallas kernels: 445 us -> 425 us
    pallas_call x1, Pallas kernels: 232 us -> 203 us  [reduce_all(): pl.pallas_call(functools.partial(reduce_kernel, bits, rows is not None),...]
    pallas_call x0 -> x1, Pallas kernels: none -> 15.7 us  [finish(): pl.pallas_call(functools.partial(finish_kernel, 0 if back is None else ba...]
    reshape x17 -> x0, local copies, waits for them, and re-layouts: 8.95 us -> none  [the longest x1 5.59 us: shards(): tab = embed_table.reshape(32, table_rows // 32, cols).transpose(0, 2, 1)]
    pallas_call x1, Pallas kernels: 110 us -> 103 us  [dense(): pl.pallas_call(dense_kernel, grid_spec=pltpu.PrefetchScalarGridSpec(num_s...]
    concatenate x15 -> x1, other arithmetic: 7.4 us -> 0.6 us  [shards(): jnp.concatenate([tower_bias, tower_out, jnp.pad(tower_out_bias[None], ((0...]
    reduce_sum x17 -> x0, other arithmetic: 6.41 us -> none  [the longest x2 2.54 us: put_experts(): sums = jnp.sum(sums, axis=-1)]
where the time goes in v4:
time: 435 us; the launch traced here: 434 us
  Pallas kernels  425 us (98%)
  local copies, waits for them, and re-layouts  6.65 us (2%)
    pallas_call x1, Pallas kernels, reduce_all(): pl.pallas_call(functools.partial(reduce_kernel, bits, rows is not None),...  203 us
    pallas_call x1, Pallas kernels, dense(): pl.pallas_call(dense_kernel, grid_spec=pltpu.PrefetchScalarGridSpec(num_s...  103 us
    pallas_call x1, Pallas kernels, front(): pl.pallas_call(functools.partial(front_kernel, groups), in_specs=[vmem] *...  103 us
    pallas_call x1, Pallas kernels, finish(): pl.pallas_call(functools.partial(finish_kernel, 0 if back is None else ba...  15.7 us

profile of v4, /device:TPU:0, one launch (start us, length us, event | category | flops | bytes accessed | tf_op | source)
XLA Modules:
  0.0 433.9 jit_solution(877693668016946344)
XLA Ops:
  0.7 0.6 concatenate.9.ids_ref
  1.3 1.3 broadcast_in_dim.24.mask_ref
  2.6 1.8 copy.34
  4.4 0.0 copy-start
  4.4 0.0 copy-start.2
  4.4 0.0 copy-start.3
  4.4 0.0 copy-start.5
  4.4 0.0 copy-start.4
  4.4 103.0 %front.1 = (bf16[4,160,1536]{2,1,0:T(8,128)(2,1)}, bf16[8,512,256]{2,1,0:T(8,128)(2,1)}, bf16[8,256,512]{2,1,0:T(8,128)(2,1)}, bf16[2,6,512,256]{3,2,1,0:T(8,128...) custom-call(s32[8,10,768]{2,1,0:T(8,128)} %bitcast.27, ...), custom_call_target="tpu_custom_call" | custom-call | flops 44999999488 | bytes 41943040 | tf_op jit(solution)/shard_map/front/pallas_call | solution.py:439
  107.4 0.0 copy-done
  107.5 0.6 broadcast_in_dim.25.label_ref
  108.1 0.0 copy-done.2
  108.1 0.0 copy-done.3
  108.1 0.0 copy-done.5
  108.1 0.6 fusion.1.tower_ref
  108.7 0.0 copy-done.4
  108.7 0.6 broadcast_in_dim.26.bias_ref
  109.2 103.2 %dense_all.1 = (f32[1,1536]{1,0:T(1,128)}, bf16[6,4,1024,256]{3,2,1,0:T(8,128)(2,1)}, bf16[640,1536]{1,0:T(8,128)(2,1)}, bf16[4,4,256,256]{3,2,1,0:T(8,128)(2,1)}) custom-call(s32[19]{0:T(128)} %concatenate.9.ids_ref, bf16[640,1536]{1,0:T(8,128)(2,1)} %bitcast.37, f32[1536,128]{1,0:T(8,128)} %feats_ref.3, f32[8,16,128]{2,1,0:T(8,128)} %get-tuple-element.42.every_ref, ...), custom_call_target="tpu_custom_call" | custom-call | flops 38999998464 | bytes 62914560 | tf_op jit(solution)/shard_map/dense_all/pallas_call | solution.py:1196
  212.5 203.2 %reduce_all.1 = (bf16[9,2,1024,256]{3,2,1,0:T(8,128)(2,1)}, bf16[3,512,256]{2,1,0:T(8,128)(2,1)}, bf16[8,160,768]{2,1,0:T(8,128)(2,1)}) custom-call(bf16[6,4,1024,256]{3,2,1,0:T(8,128)(2,1)} %get-tuple-element.49.own_ref, bf16[4,1024,256]{2,1,0:T(8,128)(2,1)} %bitcast.25, s32[10,6144]{1,0:T(8,128)} %bitcast.29, bf16[4,160,1536]{2,1,0:T(8,128)(2,1)} %bitcast.26), custom_call_target="tpu_custom_call" | custom-call | bytes 62914560 | tf_op jit(solution)/shard_map/reduce_all/pallas_call | solution.py:807
  415.8 0.6 concatenate.11.ids_ref
  416.4 0.0 copy-start.1
  416.4 15.7 %finish.1 = (f32[1,8,160,768]{3,2,1,0:T(8,128)}, f32[14,512,256]{2,1,0:T(8,128)}, f32[14,256,512]{2,1,0:T(8,128)}, f32[160,512]{1,0:T(8,128)}, f32[128,512]{1,0:...) custom-call(s32[18]{0:T(128)} %concatenate.11.ids_ref, ...), custom_call_target="tpu_custom_call" | custom-call | bytes 33554432 | tf_op jit(solution)/shard_map/finish/pallas_call | solution.py:1324
  432.1 1.2 slice_bitcast_fusion
  433.3 0.0 copy-done.1
  433.3 0.6 reduce
  (3 shorter events, 0.1 us)
Async XLA Ops:
  4.4 103.1 %copy-start = (s32[1536]{0:T(1024)S(1)}, s32[1536]{0:T(1024)}, u32[]{:S(2)}) copy-start(s32[1536]{0:T(1024)} %param.22) | copy-start | bytes 18436
  4.4 103.7 %copy-start.2 = (bf16[6,128]{1,0:T(8,128)(2,1)S(1)}, bf16[6,128]{1,0:T(8,128)(2,1)}, u32[]{:S(2)}) copy-start(bf16[6,128]{1,0:T(8,128)(2,1)} %param.34) | copy-start | bytes 4612
  4.4 103.7 %copy-start.3 = (bf16[6,128]{1,0:T(8,128)(2,1)S(1)}, bf16[6,128]{1,0:T(8,128)(2,1)}, u32[]{:S(2)}) copy-start(bf16[6,128]{1,0:T(8,128)(2,1)} %param.33) | copy-start | bytes 4612
  4.4 103.7 %copy-start.5 = (bf16[6]{0:T(256)(128)(2,1)S(1)}, bf16[6]{0:T(256)(128)(2,1)}, u32[]{:S(2)}) copy-start(bf16[6]{0:T(256)(128)(2,1)} %param.35) | copy-start | bytes 40
  4.4 104.3 %copy-start.4 = (bf16[512]{0:T(512)(128)(2,1)S(1)}, bf16[512]{0:T(512)(128)(2,1)}, u32[]{:S(2)}) copy-start(bf16[512]{0:T(512)(128)(2,1)} %param.26) | copy-start | bytes 3076
  416.4 16.9 %copy-start.1 = (f32[1,1536]{1,0:T(1,128)S(1)}, f32[1,1536]{1,0:T(1,128)}, u32[]{:S(2)}) copy-start(f32[1,1536]{1,0:T(1,128)} %get-tuple-element.48) | copy-start | bytes 18436

commit v5 on v4

--- a/solution.py
+++ b/solution.py
@@ -22,6 +22,7 @@
 MESH = pl.DeviceIdType.MESH
 UNITS = 9
 TURNED = 0
+TOGETHER = 2
 ROW_AT = 5
 ROW_STEP = 1
 ROWS_U = 1024
@@ -164,18 +165,18 @@
     emb_ref, far_up, far_down, their_up, their_down, proj_out, every_ref,
     asked, found, received, ordered, both,
     req_send, req_recv, row_send, row_recv, near_send, near_recv, keep_sem,
-    far_send, far_recv, side_send, own_send, own_recv, their_send, their_recv, proj_send, proj_recv,
+    far_send, far_recv, side_send, above_send, own_send, own_recv, their_send, their_recv, proj_send, proj_recv,
     stat_send, stat_recv,
 ):
     wide, me = lax.axis_index("wide"), lax.axis_index("narrow")
     chip, core = me // 2, me % 2
     owners, fields, cap = req_ref.shape
     share = fields // groups
-    parity = wide % 2
+    parity, upper = wide % 2, (wide // 2) % 2
     near = [{"narrow": me + 1 - 2 * core}, {"narrow": me + 2 - 4 * chip}, {"narrow": 3 - me}]
     near_at = [me + 1 - 2 * core, me + 2 - 4 * chip, 3 - me]
     peers = [None] + [{"wide": (wide + d) % owners} for d in range(1, owners)]
-    side = {"wide": wide + 1 - 2 * parity}
+    side, above = {"wide": wide + 1 - 2 * parity}, {"wide": wide + 2 - 4 * upper}
     barrier = pltpu.get_barrier_semaphore()
     for mate in near + peers[1:]:
         pl.semaphore_signal(barrier, inc=1, device_id=mate, device_id_type=MESH)
@@ -196,14 +197,23 @@
 
     weights = ((up_ref, far_up, their_up), (down_ref, far_down, their_down))
 
+    def far_at(j, side_of):
+        return jnp.where(j == 0, 4 + side_of + 2 * upper, 2 * (j - 1) + side_of)
+
     def far_copy(j, a):
-        p = 2 * j + parity
-        expert = jnp.where(j == 0, parity, 6 * (1 - chip) + p)
+        p = far_at(j, parity)
+        expert = jnp.where(p < 2, p, 6 * (1 - chip) + p)
         return remote(weights[a][0].at[expert], weights[a][1].at[p], far_send.at[a, j], far_recv.at[a, p], near[1])
 
-    def side_copy(p, a):
+    def side_copy(j, a, side_of):
+        p = far_at(j, side_of)
         view = weights[a][1].at[p]
-        return remote(view, view, side_send.at[a, p // 2], far_recv.at[a, p], side)
+        return remote(view, view, side_send.at[a, j], far_recv.at[a, p], side)
+
+    def above_copy(i, a, half):
+        p = 4 + i + 2 * half
+        view = weights[a][1].at[p]
+        return remote(view, view, above_send.at[a, i], far_recv.at[a, p], above)
 
     def own_copy(i, a):
         expert = jnp.where(i < 2, i, 6 * chip + jnp.where(i < 4, i + 4 * (1 - core), i))
@@ -226,7 +236,7 @@
         lax.fori_loop(0, n, body, 0)
 
 
-    for_all(4, lambda j, a: far_copy(j, a).start())
+    for_all(3, lambda j, a: far_copy(j, a).start())
 
     def stat_core():
         return remote(both.at[pl.ds(0, 8)], both.at[pl.ds(8, 8)], stat_send.at[0], stat_recv.at[0], near[0])
@@ -241,9 +251,17 @@
     def proj_copy(i):
         return remote(proj_ref, proj_out.at[me], proj_send.at[i], proj_recv.at[i], near[i])
 
+    def proj_pass():
+        view = proj_out.at[near_at[1]]
+        return remote(view, view, proj_send.at[2], proj_recv.at[2], near[0])
+
+    def other_proj():
+        proj_copy(1).wait_recv()
+        proj_pass().start()
+
     keep_proj = pltpu.make_async_copy(proj_ref, proj_out.at[me], keep_sem.at[1])
     keep_proj.start()
-    for i in range(3):
+    for i in range(2):
         proj_copy(i).start()
     for_all(6, lambda i, a: own_copy(i, a).start())
     stat_core().wait_recv()
@@ -252,24 +270,35 @@
     keep_stat = pltpu.make_async_copy(both, every_ref.at[wide], keep_sem.at[2])
     keep_stat.start()
 
+    def pass_on(p):
+        @pl.when(wanted(p))
+        def _():
+            for a in range(2):
+                their_copy(p, a).start()
+
+    def lift(j, side_of):
+        @pl.when(j == 0)
+        def _():
+            for a in range(2):
+                above_copy(side_of, a, upper).start()
+
     def far_step(j):
-        p = 2 * j + parity
         for a in range(2):
             far_copy(j, a).wait_recv()
-            side_copy(p, a).start()
-        pass_on(p)
-
-    def pass_on(p):
-        @pl.when(wanted(p))
-        def _():
-            for a in range(2):
-                their_copy(p, a).start()
+            side_copy(j, a, parity).start()
+        lift(j, parity)
+        pass_on(far_at(j, parity))
 
     def side_step(j):
-        p = 2 * j + 1 - parity
         for a in range(2):
-            side_copy(p, a).wait_recv()
-        pass_on(p)
+            side_copy(j, a, 1 - parity).wait_recv()
+        lift(j, 1 - parity)
+        pass_on(far_at(j, 1 - parity))
+
+    def above_step(i):
+        for a in range(2):
+            above_copy(i, a, 1 - upper).wait_recv()
+        pass_on(4 + i + 2 * (1 - upper))
 
     hi_n = 512
     lo_n = table_ref.shape[1] // hi_n
@@ -297,31 +326,26 @@
         )
 
     def look(g):
-        def one(d, _):
-            sender = (wide + d) % owners
-
-            @pl.when(jnp.logical_and(g == 0, d > 0))
-            def _():
-                remote(req_ref.at[0], asked.at[sender], req_send.at[d], req_recv.at[owners - d], peers[1]).wait_recv()
-
-            for k in range(share):
-                cols, block = find(g * share + k, sender)
-
-                @pl.when(d == 0)
-                def _():
-                    received[wide, cols, :] = block
-
+        @pl.when(g == 0)
+        def _():
+            for d in range(1, owners):
+                req_copy(d).wait_recv()
+
+        def some(i, _):
+            ahead = [i * TOGETHER + e for e in range(TOGETHER)]
+            for d in ahead:
+                for k in range(share):
+                    cols, block = find(g * share + k, (wide + d) % owners)
+                    found[(wide + d) % owners, cols, :] = block
+            for d in ahead:
                 @pl.when(d > 0)
                 def _():
-                    found[sender, cols, :] = block
-
-            @pl.when(d > 0)
-            def _():
-                row_copy(g, d, {"wide": sender}).start()
+                    row_copy(g, d, {"wide": (wide + d) % owners}).start()
 
             return 0
 
-        lax.fori_loop(0, owners, one, 0)
+        lax.fori_loop(0, owners // TOGETHER, some, 0)
+        received[wide, group_rows(g), :] = found[wide, group_rows(g), :]
 
     hi_e = 256
     outer = owners * cap // hi_e
@@ -375,7 +399,7 @@
         def _():
             look(t)
 
-        @pl.when(jnp.logical_and(t >= 1, t < 5))
+        @pl.when(jnp.logical_and(t >= 1, t < 4))
         def _():
             far_step(t - 1)
 
@@ -383,9 +407,17 @@
         def _():
             order(t - 2)
 
-        @pl.when(t >= 3)
+        @pl.when(t == 3)
+        def _():
+            other_proj()
+
+        @pl.when(jnp.logical_and(t >= 3, t < 6))
         def _():
             side_step(t - 3)
+
+        @pl.when(t >= 5)
+        def _():
+            above_step(jnp.where(t == 5, parity, 1 - parity))
 
         return 0
 
@@ -397,8 +429,9 @@
     stat_core().wait_send()
     keep_stat.wait()
     keep_proj.wait()
-    for i in range(3):
-        proj_copy(i).wait()
+    proj_copy(0).wait()
+    proj_copy(1).wait_send()
+    proj_pass().wait()
 
     def rows_left(g, _):
         def one(d, _):
@@ -415,9 +448,10 @@
 
     def weights_left(j, a):
         far_copy(j, a).wait_send()
-        side_copy(2 * j + parity, a).wait_send()
-
-    for_all(4, weights_left)
+        side_copy(j, a, parity).wait_send()
+
+    for_all(3, weights_left)
+    for_all(2, lambda i, a: above_copy(i, a, upper).wait_send())
     for_all(6, lambda i, a: own_copy(i, a).wait())
 
     def passed(p, a):
@@ -462,9 +496,10 @@
             dma((groups, 3)),
             dma((groups, 3)),
             dma((3 + groups,)),
-            dma((2, 4)),
+            dma((2, 3)),
             dma((2, 8)),
-            dma((2, 4)),
+            dma((2, 3)),
+            dma((2, 2)),
             dma((2, 6)),
             dma((2, 6)),
             dma((2, 6)),
@@ -952,17 +987,17 @@
     def _():
         lanes = pl.ds(pl.multiple_of(chunk * HALF, HALF), HALF)
 
-        def piece(s):
+        for s in range(4):
             pre = dot(ups[s][...], xt[:, lanes], 0, 0)
             a, g = gelu_both(pre)
             a = a.astype(BF)
             act[slot, s, :, lanes] = a
             slope[slot, s, :, lanes] = g.astype(BF)
-            return dot(downs[s][...], a, 0, 0)
-
-        outs[slot] = piece(0)
+
+        total = dot(downs[0][...], act[slot, 0, :, lanes], 0, 0)
         for s in range(1, 4):
-            outs[slot] += piece(s)
+            total += dot(downs[s][...], act[slot, s, :, lanes], 0, 0)
+        outs[slot] = total
 
     def middle():
         lanes = pl.ds(pl.multiple_of(chunk * HALF, HALF), HALF)
@@ -990,8 +1025,8 @@
                 stat[k : k + 1, cols] = mean
                 stat[4 + k : 5 + k, cols] = lax.rsqrt(var + 1e-05)
             scale = [stat[4 + k : 5 + k, cols] * stat[8 + k : 9 + k, cols] for k in range(4)]
-            for r in range(4):
-                band = slice(r * 128, (r + 1) * 128)
+            for r in range(8):
+                band = slice(r * 64, (r + 1) * 64)
                 acc = hg[band, cols]
                 for k in range(4):
                     n = (outs[k, band, cols] - stat[k : k + 1, cols]) * scale[k]
@@ -1026,8 +1061,8 @@
                 mean, rstd = stat[k : k + 1, cols], stat[4 + k : 5 + k, cols]
                 c = stat[8 + k : 9 + k, cols]
                 m2 = 0.0
-                for r in range(4):
-                    band = slice(r * 128, (r + 1) * 128)
+                for r in range(8):
+                    band = slice(r * 64, (r + 1) * 64)
                     w = (outs[k, band, cols] - mean) * rstd * hg[band, cols]
                     m2 = m2 + jnp.sum(w * gains[expert[k], band, :].astype(F32), axis=0, keepdims=True)
                     gain_acc[expert[k], band, :] += w * c
@@ -1036,8 +1071,8 @@
                 cr = c * rstd
                 slant = cr * rstd * m2 * (1.0 / D)
                 level = mean * slant - cr * m1 * (1.0 / D)
-                for r in range(4):
-                    band = slice(r * 128, (r + 1) * 128)
+                for r in range(8):
+                    band = slice(r * 64, (r + 1) * 64)
                     scaled = hg[band, cols] * gains[expert[k], band, :].astype(F32)
                     og[k, band, place] = (scaled * cr - outs[k, band, cols] * slant + level).astype(BF)
             return 0
@@ -1064,25 +1099,19 @@
             p = dot(downs[s][...], og[k, :, lanes], 1, 0) * slope[k, s, :, lanes].astype(F32)
             slope[k, s, :, lanes] = p.astype(BF)
 
-        def piece(s, _):
+        for s in range(4):
             grad, p = og[k, :, lanes], slope[k, s, :, lanes]
             own_ref[0, s, 0:D, :] = dot(xt[:, lanes], p, 1, 1).astype(BF)
             d = dot(act[k, s, :, lanes], grad, 1, 1).astype(BF)
             own_ref[0, s, D : D + 256, :] = d[:, 0:256]
             own_ref[0, s, D + 256 : D + 512, :] = d[:, 256:512]
-            return 0
-
-        lax.fori_loop(0, 4, piece, 0)
-
-        def grow(t, _):
-            cols = pl.ds(pl.multiple_of(at + t * HALF, HALF), HALF)
+
+        for t in range(n // HALF):
+            cols = slice(at + t * HALF, at + (t + 1) * HALF)
             total = dot(ups[0][...], slope[k, 0, :, cols], 1, 0)
             for s in range(1, 4):
                 total += dot(ups[s][...], slope[k, s, :, cols], 1, 0)
             ing[:, cols] += total
-            return 0
-
-        lax.fori_loop(0, n // HALF, grow, 0)
 
     expert = step - 12
 

time: 435 us -> 411 us (0.945)
  Pallas kernels: 425 us -> 401 us
    pallas_call x1, Pallas kernels: 103 us -> 86.7 us  [dense(): pl.pallas_call(dense_kernel, grid_spec=pltpu.PrefetchScalarGridSpec(num_s...]
    pallas_call x1, Pallas kernels: 103 us -> 94.3 us  [front(): pl.pallas_call(functools.partial(front_kernel, groups), in_specs=[vmem] *...]
where the time goes in v5:
time: 411 us; the launch traced here: 410 us
  Pallas kernels  401 us (98%)
  local copies, waits for them, and re-layouts  6.65 us (2%)
    pallas_call x1, Pallas kernels, reduce_all(): pl.pallas_call(functools.partial(reduce_kernel, bits, rows is not None),...  205 us
    pallas_call x1, Pallas kernels, front(): pl.pallas_call(functools.partial(front_kernel, groups), in_specs=[vmem] *...  94.3 us
    pallas_call x1, Pallas kernels, dense(): pl.pallas_call(dense_kernel, grid_spec=pltpu.PrefetchScalarGridSpec(num_s...  86.7 us
    pallas_call x1, Pallas kernels, finish(): pl.pallas_call(functools.partial(finish_kernel, 0 if back is None else ba...  15.7 us

profile of v5, /device:TPU:0, one launch (start us, length us, event | category | flops | bytes accessed | tf_op | source)
XLA Modules:
  0.0 410.1 jit_solution(8226614301779869245)
XLA Ops:
  0.7 0.6 concatenate.9.ids_ref
  1.3 1.3 broadcast_in_dim.24.mask_ref
  2.6 1.8 copy.34
  4.4 0.0 copy-start
  4.4 0.0 copy-start.2
  4.4 0.0 copy-start.3
  4.4 0.0 copy-start.5
  4.4 0.0 copy-start.4
  4.4 94.3 %front.1 = (bf16[4,160,1536]{2,1,0:T(8,128)(2,1)}, bf16[8,512,256]{2,1,0:T(8,128)(2,1)}, bf16[8,256,512]{2,1,0:T(8,128)(2,1)}, bf16[2,6,512,256]{3,2,1,0:T(8,128...) custom-call(s32[8,10,768]{2,1,0:T(8,128)} %bitcast.27, ...), custom_call_target="tpu_custom_call" | custom-call | flops 44999999488 | bytes 41943040 | tf_op jit(solution)/shard_map/front/pallas_call | solution.py:473
  98.7 0.0 copy-done
  98.7 0.6 broadcast_in_dim.25.label_ref
  99.3 0.0 copy-done.2
  99.3 0.0 copy-done.3
  99.3 0.0 copy-done.5
  99.3 0.6 fusion.1.tower_ref
  99.9 0.0 copy-done.4
  99.9 0.6 broadcast_in_dim.26.bias_ref
  100.5 86.7 %dense_all.1 = (f32[1,1536]{1,0:T(1,128)}, bf16[6,4,1024,256]{3,2,1,0:T(8,128)(2,1)}, bf16[640,1536]{1,0:T(8,128)(2,1)}, bf16[4,4,256,256]{3,2,1,0:T(8,128)(2,1)}) custom-call(s32[19]{0:T(128)} %concatenate.9.ids_ref, bf16[640,1536]{1,0:T(8,128)(2,1)} %bitcast.37, f32[1536,128]{1,0:T(8,128)} %feats_ref.3, f32[8,16,128]{2,1,0:T(8,128)} %get-tuple-element.42.every_ref, ...), custom_call_target="tpu_custom_call" | custom-call | flops 38999998464 | bytes 62914560 | tf_op jit(solution)/shard_map/dense_all/pallas_call | solution.py:1225
  187.3 204.7 %reduce_all.1 = (bf16[9,2,1024,256]{3,2,1,0:T(8,128)(2,1)}, bf16[3,512,256]{2,1,0:T(8,128)(2,1)}, bf16[8,160,768]{2,1,0:T(8,128)(2,1)}) custom-call(bf16[6,4,1024,256]{3,2,1,0:T(8,128)(2,1)} %get-tuple-element.49.own_ref, bf16[4,1024,256]{2,1,0:T(8,128)(2,1)} %bitcast.25, s32[10,6144]{1,0:T(8,128)} %bitcast.29, bf16[4,160,1536]{2,1,0:T(8,128)(2,1)} %bitcast.26), custom_call_target="tpu_custom_call" | custom-call | bytes 62914560 | tf_op jit(solution)/shard_map/reduce_all/pallas_call | solution.py:842
  392.0 0.6 concatenate.11.ids_ref
  392.6 0.0 copy-start.1
  392.6 15.7 %finish.1 = (f32[1,8,160,768]{3,2,1,0:T(8,128)}, f32[14,512,256]{2,1,0:T(8,128)}, f32[14,256,512]{2,1,0:T(8,128)}, f32[160,512]{1,0:T(8,128)}, f32[128,512]{1,0:...) custom-call(s32[18]{0:T(128)} %concatenate.11.ids_ref, ...), custom_call_target="tpu_custom_call" | custom-call | bytes 33554432 | tf_op jit(solution)/shard_map/finish/pallas_call | solution.py:1353
  408.3 1.2 slice_bitcast_fusion
  409.5 0.0 copy-done.1
  409.5 0.6 reduce
  (3 shorter events, 0.1 us)
Async XLA Ops:
  4.4 94.3 %copy-start = (s32[1536]{0:T(1024)S(1)}, s32[1536]{0:T(1024)}, u32[]{:S(2)}) copy-start(s32[1536]{0:T(1024)} %param.22) | copy-start | bytes 18436
  4.4 94.9 %copy-start.2 = (bf16[6,128]{1,0:T(8,128)(2,1)S(1)}, bf16[6,128]{1,0:T(8,128)(2,1)}, u32[]{:S(2)}) copy-start(bf16[6,128]{1,0:T(8,128)(2,1)} %param.34) | copy-start | bytes 4612
  4.4 94.9 %copy-start.3 = (bf16[6,128]{1,0:T(8,128)(2,1)S(1)}, bf16[6,128]{1,0:T(8,128)(2,1)}, u32[]{:S(2)}) copy-start(bf16[6,128]{1,0:T(8,128)(2,1)} %param.33) | copy-start | bytes 4612
  4.4 94.9 %copy-start.5 = (bf16[6]{0:T(256)(128)(2,1)S(1)}, bf16[6]{0:T(256)(128)(2,1)}, u32[]{:S(2)}) copy-start(bf16[6]{0:T(256)(128)(2,1)} %param.35) | copy-start | bytes 40
  4.4 95.5 %copy-start.4 = (bf16[512]{0:T(512)(128)(2,1)S(1)}, bf16[512]{0:T(512)(128)(2,1)}, u32[]{:S(2)}) copy-start(bf16[512]{0:T(512)(128)(2,1)} %param.26) | copy-start | bytes 3076
  392.6 16.9 %copy-start.1 = (f32[1,1536]{1,0:T(1,128)S(1)}, f32[1,1536]{1,0:T(1,128)}, u32[]{:S(2)}) copy-start(f32[1,1536]{1,0:T(1,128)} %get-tuple-element.48) | copy-start | bytes 18436

commit v6 on v5

--- a/solution.py
+++ b/solution.py
@@ -21,7 +21,7 @@
 F32 = jnp.float32
 MESH = pl.DeviceIdType.MESH
 UNITS = 9
-TURNED = 0
+TURNED = 4
 TOGETHER = 2
 ROW_AT = 5
 ROW_STEP = 1
@@ -754,17 +754,18 @@
     todo += [functools.partial(halving, k) for k in range(1, bits + 1)] + [cross]
     todo += [functools.partial(lambda j, u: grow(u, j), j) for j in reversed(range(bits))]
     plain_gaps = [0, 1, 2] + [1] * (len(todo) - 4) + [2]
-    turned_gaps = [0, 1, 3, 4] + [1] * (len(todo) - 6) + [3, 3]
+    turned_gaps = [0, 1, 3, 4] + [1] * (len(todo) - 6) + [4, 3]
     plain_lag = [sum(plain_gaps[: i + 1]) for i in range(len(todo))]
     turned_lag = [sum(turned_gaps[: i + 1]) for i in range(len(todo))]
 
     def tick(t,_):
         for s in reversed(range(len(todo))):
             def stage(c, _):
-                plain = t - plain_lag[s]
+                at = t - plain_lag[s]
+                plain = jnp.where(at < 2, at + 4, jnp.where(at < 6, at - 2, at))
                 u = jnp.where(c == 0, plain, TURNED)
-                fits = jnp.logical_and(jnp.logical_and(plain >= 0, plain < UNITS), plain != TURNED)
-                due = jnp.where(c == 0, fits, t == TURNED + turned_lag[s])
+                fits = jnp.logical_and(jnp.logical_and(at >= 0, at < UNITS), plain != TURNED)
+                due = jnp.where(c == 0, fits, t == turned_lag[s])
 
                 @pl.when(due)
                 def _():
@@ -779,7 +780,7 @@
     if with_rows:
         keep_copy().start()
         for i in range(3): near_row_copy(i).start()
-    lax.fori_loop(0, max(UNITS + plain_lag[-1], TURNED + turned_lag[-1] + 1), tick, 0)
+    lax.fori_loop(0, max(UNITS + plain_lag[-1], turned_lag[-1] + 1), tick, 0)
     if with_rows:
         keep_back().wait()
         for i in range(3): near_row_copy(i).wait_send()
@@ -1279,20 +1280,21 @@
     )(ids, emb, feats, every, mask, label, projw, featw, bias, *ups, *downs, gains, shifts, gate, gate, tin, tin, tower)
 
 
-def finish_kernel(with_rows, ids_ref, sums_ref, unit_ref, others_ref, *refs):
+def finish_kernel(with_rows, ids_ref, even_ref, odd_ref, unit_ref, others_ref, *refs):
     if with_rows:
         back_ref, row_ref = refs[0], refs[1]
         refs = refs[2:]
     (up_ref, down_ref, proj_ref, feat_ref, bias_ref, gain_ref, shift_ref, gate_ref, tin_ref, tbias_ref,
      tout_ref, tob_ref, quarters) = refs
     step = pl.program_id(0)
-    up_ref[0] = sums_ref[0, 0, 0:D, :].astype(F32)
-    down_ref[0, :, 0:256] = sums_ref[0, 0, D : D + 256, :].astype(F32)
-    down_ref[0, :, 256:512] = sums_ref[0, 0, D + 256 : D + 512, :].astype(F32)
+    for i, sums_ref in enumerate((even_ref, odd_ref)):
+        up_ref[i] = sums_ref[0, 0, 0:D, :].astype(F32)
+        down_ref[i, :, 0:256] = sums_ref[0, 0, D : D + 256, :].astype(F32)
+        down_ref[i, :, 256:512] = sums_ref[0, 0, D + 256 : D + 512, :].astype(F32)
     if with_rows:
         @pl.when(step < with_rows)
         def _():
-            row_ref[0, 0] = back_ref[0].astype(F32)
+            row_ref[0] = back_ref[...].astype(F32)
 
     @pl.when(step == 0)
     def _():
@@ -1326,35 +1328,37 @@
     def whole(s):
         return pl.BlockSpec(s, lambda i, ids: (0,) * len(s))
 
-    def unit(i, ids):
-        return (ids[i] % 16, ids[i] // 16, 0, 0)
+    def unit(odd):
+        return lambda i, ids: (ids[2 * i + odd] % 16, ids[2 * i + odd] // 16, 0, 0)
 
     in_specs = [
-        pl.BlockSpec((1, 1, ROWS_U, LANES), unit),
+        pl.BlockSpec((1, 1, ROWS_U, LANES), unit(0)),
+        pl.BlockSpec((1, 1, ROWS_U, LANES), unit(1)),
         pl.BlockSpec((1, 1, ROWS_U, LANES), lambda i, ids: (6, 0, 0, 0)),
         whole(others.shape),
     ]
-    args = [sums, sums, others]
+    args = [sums, sums, sums, others]
     shapes = [
         (14, D, 256), (14, 256, D), (proj_cols, D), (DENSE, D), (1, D), (14, D), (14, D), (DOMAINS, 6, D),
         (DOMAINS, D, 128), (DOMAINS, 128), (DOMAINS, 128), (1, 128),
     ]
     out_specs = [
-        pl.BlockSpec((1, D, 256), lambda i, ids: (i, 0, 0)),
-        pl.BlockSpec((1, 256, D), lambda i, ids: (i, 0, 0)),
+        pl.BlockSpec((2, D, 256), lambda i, ids: (i, 0, 0)),
+        pl.BlockSpec((2, 256, D), lambda i, ids: (i, 0, 0)),
     ] + [whole(s) for s in shapes[2:]]
     if back is not None:
         blocks, cols, cap = back.shape
-        last = lambda i: jnp.minimum(i, blocks - 1)
+        each = -(-blocks // 7)
+        last = lambda i: jnp.minimum(i, blocks // each - 1)
         args.append(back)
-        in_specs.append(pl.BlockSpec((1, cols, cap), lambda i, ids: (last(i), 0, 0)))
+        in_specs.append(pl.BlockSpec((each, cols, cap), lambda i, ids: (last(i), 0, 0)))
         shapes.insert(0, (1, blocks, cols, cap))
-        out_specs.insert(0, pl.BlockSpec((1, 1, cols, cap), lambda i, ids: (0, last(i), 0, 0)))
+        out_specs.insert(0, pl.BlockSpec((1, each, cols, cap), lambda i, ids: (0, last(i), 0, 0)))
     return pl.pallas_call(
-        functools.partial(finish_kernel, 0 if back is None else back.shape[0]),
+        functools.partial(finish_kernel, 0 if back is None else blocks // each),
         grid_spec=pltpu.PrefetchScalarGridSpec(
             num_scalar_prefetch=1,
-            grid=(14,),
+            grid=(7,),
             in_specs=in_specs,
             out_specs=out_specs,
             scratch_shapes=[pltpu.VMEM((4, REP_ROWS, LANES), F32)],

time: 411 us -> 404 us (0.983)
  Pallas kernels: 401 us -> 394 us
    pallas_call x1, Pallas kernels: 205 us -> 200 us  [reduce_all(): pl.pallas_call(functools.partial(reduce_kernel, bits, rows is not None),...]
where the time goes in v6:
time: 404 us; the launch traced here: 403 us
  Pallas kernels  394 us (98%)
  local copies, waits for them, and re-layouts  6.65 us (2%)
    pallas_call x1, Pallas kernels, reduce_all(): pl.pallas_call(functools.partial(reduce_kernel, bits, rows is not None),...  200 us
    pallas_call x1, Pallas kernels, front(): pl.pallas_call(functools.partial(front_kernel, groups), in_specs=[vmem] *...  94.4 us
    pallas_call x1, Pallas kernels, dense(): pl.pallas_call(dense_kernel, grid_spec=pltpu.PrefetchScalarGridSpec(num_s...  86.7 us
    pallas_call x1, Pallas kernels, finish(): pl.pallas_call(functools.partial(finish_kernel, 0 if back is None else bl...  13.4 us

profile of v6, /device:TPU:0, one launch (start us, length us, event | category | flops | bytes accessed | tf_op | source)
XLA Modules:
  0.0 402.8 jit_solution(2610612536944721620)
XLA Ops:
  0.7 0.6 concatenate.9.ids_ref
  1.3 1.3 broadcast_in_dim.24.mask_ref
  2.6 1.8 copy.34
  4.4 0.0 copy-start
  4.4 0.0 copy-start.2
  4.4 0.0 copy-start.3
  4.4 0.0 copy-start.5
  4.4 0.0 copy-start.4
  4.4 94.4 %front.1 = (bf16[4,160,1536]{2,1,0:T(8,128)(2,1)}, bf16[8,512,256]{2,1,0:T(8,128)(2,1)}, bf16[8,256,512]{2,1,0:T(8,128)(2,1)}, bf16[2,6,512,256]{3,2,1,0:T(8,128...) custom-call(s32[8,10,768]{2,1,0:T(8,128)} %bitcast.27, ...), custom_call_target="tpu_custom_call" | custom-call | flops 44999999488 | bytes 41943040 | tf_op jit(solution)/shard_map/front/pallas_call | solution.py:473
  98.8 0.0 copy-done
  98.8 0.6 broadcast_in_dim.25.label_ref
  99.4 0.0 copy-done.2
  99.4 0.0 copy-done.3
  99.4 0.0 copy-done.5
  99.4 0.6 fusion.1.tower_ref
  100.0 0.0 copy-done.4
  100.0 0.6 broadcast_in_dim.26.bias_ref
  100.6 86.7 %dense_all.1 = (f32[1,1536]{1,0:T(1,128)}, bf16[6,4,1024,256]{3,2,1,0:T(8,128)(2,1)}, bf16[640,1536]{1,0:T(8,128)(2,1)}, bf16[4,4,256,256]{3,2,1,0:T(8,128)(2,1)}) custom-call(s32[19]{0:T(128)} %concatenate.9.ids_ref, bf16[640,1536]{1,0:T(8,128)(2,1)} %bitcast.37, f32[1536,128]{1,0:T(8,128)} %feats_ref.3, f32[8,16,128]{2,1,0:T(8,128)} %get-tuple-element.42.every_ref, ...), custom_call_target="tpu_custom_call" | custom-call | flops 38999998464 | bytes 62914560 | tf_op jit(solution)/shard_map/dense_all/pallas_call | solution.py:1226
  187.3 199.6 %reduce_all.1 = (bf16[9,2,1024,256]{3,2,1,0:T(8,128)(2,1)}, bf16[3,512,256]{2,1,0:T(8,128)(2,1)}, bf16[8,160,768]{2,1,0:T(8,128)(2,1)}) custom-call(bf16[6,4,1024,256]{3,2,1,0:T(8,128)(2,1)} %get-tuple-element.49.own_ref, bf16[4,1024,256]{2,1,0:T(8,128)(2,1)} %bitcast.25, s32[10,6144]{1,0:T(8,128)} %bitcast.29, bf16[4,160,1536]{2,1,0:T(8,128)(2,1)} %bitcast.26), custom_call_target="tpu_custom_call" | custom-call | bytes 62914560 | tf_op jit(solution)/shard_map/reduce_all/pallas_call | solution.py:843
  387.0 0.6 concatenate.11.ids_ref
  387.6 0.0 copy-start.1
  387.6 13.4 %finish.1 = (f32[1,8,160,768]{3,2,1,0:T(8,128)}, f32[14,512,256]{2,1,0:T(8,128)}, f32[14,256,512]{2,1,0:T(8,128)}, f32[160,512]{1,0:T(8,128)}, f32[128,512]{1,0:...) custom-call(s32[18]{0:T(128)} %concatenate.11.ids_ref, ...), custom_call_target="tpu_custom_call" | custom-call | bytes 33554432 | tf_op jit(solution)/shard_map/finish/pallas_call | solution.py:1357
  401.0 1.2 slice_bitcast_fusion
  402.2 0.0 copy-done.1
  402.2 0.6 reduce
  (3 shorter events, 0.1 us)
Async XLA Ops:
  4.4 94.4 %copy-start = (s32[1536]{0:T(1024)S(1)}, s32[1536]{0:T(1024)}, u32[]{:S(2)}) copy-start(s32[1536]{0:T(1024)} %param.22) | copy-start | bytes 18436
  4.4 95.0 %copy-start.2 = (bf16[6,128]{1,0:T(8,128)(2,1)S(1)}, bf16[6,128]{1,0:T(8,128)(2,1)}, u32[]{:S(2)}) copy-start(bf16[6,128]{1,0:T(8,128)(2,1)} %param.34) | copy-start | bytes 4612
  4.4 95.0 %copy-start.3 = (bf16[6,128]{1,0:T(8,128)(2,1)S(1)}, bf16[6,128]{1,0:T(8,128)(2,1)}, u32[]{:S(2)}) copy-start(bf16[6,128]{1,0:T(8,128)(2,1)} %param.33) | copy-start | bytes 4612
  4.4 95.0 %copy-start.5 = (bf16[6]{0:T(256)(128)(2,1)S(1)}, bf16[6]{0:T(256)(128)(2,1)}, u32[]{:S(2)}) copy-start(bf16[6]{0:T(256)(128)(2,1)} %param.35) | copy-start | bytes 40
  4.4 95.6 %copy-start.4 = (bf16[512]{0:T(512)(128)(2,1)S(1)}, bf16[512]{0:T(512)(128)(2,1)}, u32[]{:S(2)}) copy-start(bf16[512]{0:T(512)(128)(2,1)} %param.26) | copy-start | bytes 3076
  387.6 14.6 %copy-start.1 = (f32[1,1536]{1,0:T(1,128)S(1)}, f32[1,1536]{1,0:T(1,128)}, u32[]{:S(2)}) copy-start(f32[1,1536]{1,0:T(1,128)} %get-tuple-element.48) | copy-start | bytes 18436

commit v7 on v6

--- a/solution.py
+++ b/solution.py
@@ -23,7 +23,7 @@
 UNITS = 9
 TURNED = 4
 TOGETHER = 2
-ROW_AT = 5
+ROW_AT = 6
 ROW_STEP = 1
 ROWS_U = 1024
 LANES = 256
@@ -395,29 +395,29 @@
     mine.wait()
 
     def tick(t, _):
+        @pl.when(t >= 2)
+        def _():
+            order(t - 2)
+
         @pl.when(t < groups)
         def _():
             look(t)
 
-        @pl.when(jnp.logical_and(t >= 1, t < 4))
-        def _():
-            far_step(t - 1)
-
-        @pl.when(t >= 2)
-        def _():
-            order(t - 2)
+        @pl.when(t < 3)
+        def _():
+            far_step(t)
 
         @pl.when(t == 3)
         def _():
             other_proj()
 
-        @pl.when(jnp.logical_and(t >= 3, t < 6))
-        def _():
-            side_step(t - 3)
-
-        @pl.when(t >= 5)
-        def _():
-            above_step(jnp.where(t == 5, parity, 1 - parity))
+        @pl.when(jnp.logical_and(t >= 2, t < 5))
+        def _():
+            side_step(t - 2)
+
+        @pl.when(jnp.logical_and(t >= 4, t < 6))
+        def _():
+            above_step(jnp.where(t == 4, parity, 1 - parity))
 
         return 0
 

time: 404 us -> 402 us (level)
  no operation moved by 1% of the time
where the time goes in v7:
time: 402 us; the launch traced here: 401 us
  Pallas kernels  392 us (98%)
  local copies, waits for them, and re-layouts  6.65 us (2%)
    pallas_call x1, Pallas kernels, reduce_all(): pl.pallas_call(functools.partial(reduce_kernel, bits, rows is not None),...  199 us
    pallas_call x1, Pallas kernels, front(): pl.pallas_call(functools.partial(front_kernel, groups), in_specs=[vmem] *...  93.3 us
    pallas_call x1, Pallas kernels, dense(): pl.pallas_call(dense_kernel, grid_spec=pltpu.PrefetchScalarGridSpec(num_s...  86.7 us
    pallas_call x1, Pallas kernels, finish(): pl.pallas_call(functools.partial(finish_kernel, 0 if back is None else bl...  13.4 us

profile of v7, /device:TPU:0, one launch (start us, length us, event | category | flops | bytes accessed | tf_op | source)
XLA Modules:
  0.0 401.2 jit_solution(5799891195835762928)
XLA Ops:
  0.7 0.6 concatenate.9.ids_ref
  1.3 1.3 broadcast_in_dim.24.mask_ref
  2.6 1.8 copy.34
  4.4 0.0 copy-start
  4.4 0.0 copy-start.2
  4.4 0.0 copy-start.3
  4.4 0.0 copy-start.5
  4.4 0.0 copy-start.4
  4.4 93.3 %front.1 = (bf16[4,160,1536]{2,1,0:T(8,128)(2,1)}, bf16[8,512,256]{2,1,0:T(8,128)(2,1)}, bf16[8,256,512]{2,1,0:T(8,128)(2,1)}, bf16[2,6,512,256]{3,2,1,0:T(8,128...) custom-call(s32[8,10,768]{2,1,0:T(8,128)} %bitcast.27, ...), custom_call_target="tpu_custom_call" | custom-call | flops 44999999488 | bytes 41943040 | tf_op jit(solution)/shard_map/front/pallas_call | solution.py:473
  97.7 0.0 copy-done
  97.7 0.6 broadcast_in_dim.25.label_ref
  98.3 0.0 copy-done.2
  98.3 0.0 copy-done.3
  98.3 0.0 copy-done.5
  98.3 0.6 fusion.1.tower_ref
  98.9 0.0 copy-done.4
  98.9 0.6 broadcast_in_dim.26.bias_ref
  99.5 86.7 %dense_all.1 = (f32[1,1536]{1,0:T(1,128)}, bf16[6,4,1024,256]{3,2,1,0:T(8,128)(2,1)}, bf16[640,1536]{1,0:T(8,128)(2,1)}, bf16[4,4,256,256]{3,2,1,0:T(8,128)(2,1)}) custom-call(s32[19]{0:T(128)} %concatenate.9.ids_ref, bf16[640,1536]{1,0:T(8,128)(2,1)} %bitcast.37, f32[1536,128]{1,0:T(8,128)} %feats_ref.3, f32[8,16,128]{2,1,0:T(8,128)} %get-tuple-element.42.every_ref, ...), custom_call_target="tpu_custom_call" | custom-call | flops 38999998464 | bytes 62914560 | tf_op jit(solution)/shard_map/dense_all/pallas_call | solution.py:1226
  186.3 199.1 %reduce_all.1 = (bf16[9,2,1024,256]{3,2,1,0:T(8,128)(2,1)}, bf16[3,512,256]{2,1,0:T(8,128)(2,1)}, bf16[8,160,768]{2,1,0:T(8,128)(2,1)}) custom-call(bf16[6,4,1024,256]{3,2,1,0:T(8,128)(2,1)} %get-tuple-element.49.own_ref, bf16[4,1024,256]{2,1,0:T(8,128)(2,1)} %bitcast.25, s32[10,6144]{1,0:T(8,128)} %bitcast.29, bf16[4,160,1536]{2,1,0:T(8,128)(2,1)} %bitcast.26), custom_call_target="tpu_custom_call" | custom-call | bytes 62914560 | tf_op jit(solution)/shard_map/reduce_all/pallas_call | solution.py:843
  385.4 0.6 concatenate.11.ids_ref
  386.0 0.0 copy-start.1
  386.0 13.4 %finish.1 = (f32[1,8,160,768]{3,2,1,0:T(8,128)}, f32[14,512,256]{2,1,0:T(8,128)}, f32[14,256,512]{2,1,0:T(8,128)}, f32[160,512]{1,0:T(8,128)}, f32[128,512]{1,0:...) custom-call(s32[18]{0:T(128)} %concatenate.11.ids_ref, ...), custom_call_target="tpu_custom_call" | custom-call | bytes 33554432 | tf_op jit(solution)/shard_map/finish/pallas_call | solution.py:1357
  399.4 1.2 slice_bitcast_fusion
  400.5 0.0 copy-done.1
  400.5 0.6 reduce
  (3 shorter events, 0.1 us)
Async XLA Ops:
  4.4 93.3 %copy-start = (s32[1536]{0:T(1024)S(1)}, s32[1536]{0:T(1024)}, u32[]{:S(2)}) copy-start(s32[1536]{0:T(1024)} %param.22) | copy-start | bytes 18436
  4.4 93.9 %copy-start.2 = (bf16[6,128]{1,0:T(8,128)(2,1)S(1)}, bf16[6,128]{1,0:T(8,128)(2,1)}, u32[]{:S(2)}) copy-start(bf16[6,128]{1,0:T(8,128)(2,1)} %param.34) | copy-start | bytes 4612
  4.4 93.9 %copy-start.3 = (bf16[6,128]{1,0:T(8,128)(2,1)S(1)}, bf16[6,128]{1,0:T(8,128)(2,1)}, u32[]{:S(2)}) copy-start(bf16[6,128]{1,0:T(8,128)(2,1)} %param.33) | copy-start | bytes 4612
  4.4 93.9 %copy-start.5 = (bf16[6]{0:T(256)(128)(2,1)S(1)}, bf16[6]{0:T(256)(128)(2,1)}, u32[]{:S(2)}) copy-start(bf16[6]{0:T(256)(128)(2,1)} %param.35) | copy-start | bytes 40
  4.4 94.5 %copy-start.4 = (bf16[512]{0:T(512)(128)(2,1)S(1)}, bf16[512]{0:T(512)(128)(2,1)}, u32[]{:S(2)}) copy-start(bf16[512]{0:T(512)(128)(2,1)} %param.26) | copy-start | bytes 3076
  386.0 14.6 %copy-start.1 = (f32[1,1536]{1,0:T(1,128)S(1)}, f32[1,1536]{1,0:T(1,128)}, u32[]{:S(2)}) copy-start(f32[1,1536]{1,0:T(1,128)} %get-tuple-element.48) | copy-start | bytes 18436
